TPU v7x, 128 devices: a whole 4x4x4 slice. The times are simulated.
128 devices in a mesh: dp: 8 (over y, core), store: 16 (over x, z).
Axes of the slice: x: 4, y: 4, z: 4, core: 2. Of those that a mesh axis runs over, the one named last changes fastest.
Arguments:
- node_table: bfloat16 [32768, 1024], P('store'), may hold values from -160 to 160
- touched: int32 [128, 16, 40], P(('dp', 'store')), may hold values from -1 to 2047, as said below
- member_slot: int32 [256, 256], P(('dp', 'store')), may hold values from 0 to 639, as said below
- distances: int32 [256, 256, 256], P(('dp', 'store')), may hold values from 0 to 31, as said below
- cotangent: bfloat16 [256, 256, 1024], P(('dp', 'store')), may hold values from -6 to 6
- w_qkv: bfloat16 [1024, 3072], replicated, may hold values from -0.1875 to 0.1875
- w_out: bfloat16 [1024, 1024], replicated, may hold values from -0.1875 to 0.1875
- w_up: bfloat16 [1024, 1024], replicated, may hold values from -0.1875 to 0.1875
- w_down: bfloat16 [1024, 1024], replicated, may hold values from -0.1875 to 0.1875
- gains: float32 [2, 1024], replicated, may hold values from 0.25 to 1.75
- bias_table: float32 [32, 32], replicated, may hold values from -3 to 300
Outputs:
- layer_out: bfloat16 [256, 256, 1024], P(('dp', 'store'))
- grad_table: bfloat16 [32768, 1024], P('store', 'dp')
- grad_qkv: bfloat16 [1024, 3072], P(('dp', 'store'))
- grad_out: bfloat16 [1024, 1024], P(('dp', 'store'))
- grad_up: bfloat16 [1024, 1024], P(('dp', 'store'))
- grad_down: bfloat16 [1024, 1024], P(('dp', 'store'))
- grad_gains: float32 [2, 1024], replicated
- grad_bias: float32 [32, 32], replicated
Inputs may be any that keep to these rules, and one draw needn't show every extreme that they name: touched[r, o, c] is a row within store shard o (shard o holds rows o * 2048 to o * 2048 + 2047), or -1 for an unused slot. In each [r, o] the used slots come first, name distinct rows, and number at least 16; every reader uses all 40 slots of one shard, the same shard for all readers of one index of dp. member_slot[e, n] = o * 40 + c names a used slot [o, c] of touched for the reader that holds ego-net e; the 256 slots of one ego-net are distinct. `distances`: symmetric in the two node dimensions, zero exactly on the diagonal.
All inputs are finite; a program needn't handle non-finite values.
Results may differ from a plain program's by a relative error of at most 0.017.
Values may be sent and summed in bfloat16 or wider, within the bound.
A program may use at most 192 MiB of HBM per device.

v0:
```python
import math

import jax
import jax.numpy as jnp
from jax import lax
from jax.sharding import PartitionSpec as P

EPS = 1e-05
ROOT_HALF = 1.0 / math.sqrt(2.0)
ROOT_TWO_PI = 1.0 / math.sqrt(2.0 * math.pi)


def layer_normalize(value, gain):
    mean = jnp.mean(value, -1, keepdims=True)
    centred = value - mean
    rstd = lax.rsqrt(jnp.mean(centred * centred, -1, keepdims=True) + EPS)
    vhat = centred * rstd
    return (vhat * gain, vhat, rstd)


def layer_normalize_backward(grad, gain, vhat, rstd):
    scaled = grad * gain
    first = jnp.mean(scaled, -1, keepdims=True)
    second = jnp.mean(scaled * vhat, -1, keepdims=True)
    return (rstd * (scaled - first - vhat * second), jnp.sum(grad * vhat, 0))


def gelu_parts(upper):
    normal_cdf = 0.5 * (1.0 + jax.scipy.special.erf(upper * ROOT_HALF))
    activation_slope = normal_cdf + upper * jnp.exp(-0.5 * upper * upper) * ROOT_TWO_PI
    return (upper * normal_cdf, activation_slope)


def one_hot_buckets(spd, buckets):
    return (spd[None] == jnp.arange(buckets)[:, None, None]).astype(jnp.float32)


def attend(query_rows, key_matrix_rows, value_matrix_rows, spd, table):
    scale = query_rows.shape[2] ** (-0.5)
    onehot = one_hot_buckets(spd, table.shape[0])
    bias = jnp.einsum("bnm,bh->hnm", onehot, table, precision=lax.Precision.HIGHEST)
    scores = (
        jnp.einsum("nhc,mhc->hnm", query_rows, key_matrix_rows, preferred_element_type=jnp.float32)
        * scale
        + bias
    )
    attention_probabilities = jax.nn.softmax(scores, axis=-1)
    probs_b = attention_probabilities.astype(jnp.bfloat16)
    attention_mixed = jnp.einsum(
        "hnm,mhc->nhc", probs_b, value_matrix_rows, preferred_element_type=jnp.float32
    )
    return (attention_mixed.astype(jnp.bfloat16), attention_probabilities)


def attend_back(
    dattn, query_rows, key_matrix_rows, value_matrix_rows, attention_probabilities, spd, table
):
    scale = query_rows.shape[2] ** (-0.5)
    probs_b = attention_probabilities.astype(jnp.bfloat16)
    dprobs = jnp.einsum(
        "nhc,mhc->hnm", dattn, value_matrix_rows, preferred_element_type=jnp.float32
    )
    dscores = attention_probabilities * (
        dprobs - jnp.sum(dprobs * attention_probabilities, -1, keepdims=True)
    )
    onehot = one_hot_buckets(spd, table.shape[0])
    table_grad = jnp.einsum("bnm,hnm->bh", onehot, dscores, precision=lax.Precision.HIGHEST)
    dscores_b = (dscores * scale).astype(jnp.bfloat16)
    grad_q = jnp.einsum(
        "hnm,mhc->nhc", dscores_b, key_matrix_rows, preferred_element_type=jnp.float32
    )
    grad_k = jnp.einsum("hnm,nhc->mhc", dscores_b, query_rows, preferred_element_type=jnp.float32)
    grad_v = jnp.einsum("hnm,nhc->mhc", probs_b, dattn, preferred_element_type=jnp.float32)
    count = query_rows.shape[0]
    joined = jnp.concatenate(
        [grad_q.reshape(count, -1), grad_k.reshape(count, -1), grad_v.reshape(count, -1)], axis=1
    )
    return (joined.astype(jnp.bfloat16), table_grad)


def layer_forward(x_rows, spd, w_qkv, w_out, w_up, w_down, gains, table):
    egos, count, width = x_rows.shape
    heads = table.shape[1]
    flattened_rows = x_rows.reshape(egos * count, width).astype(jnp.float32)
    first_hidden_float, normalized_input, first_inverse_deviation = layer_normalize(
        flattened_rows, gains[0]
    )
    first_hidden = first_hidden_float.astype(jnp.bfloat16)
    qkv = jnp.dot(first_hidden, w_qkv, preferred_element_type=jnp.float32).astype(jnp.bfloat16)
    qkv = qkv.reshape(egos, count, 3, heads, width // heads)
    query_rows, key_matrix_rows, value_matrix_rows = (qkv[:, :, 0], qkv[:, :, 1], qkv[:, :, 2])
    attention_mixed, attention_probabilities = jax.vmap(attend, in_axes=(0, 0, 0, 0, None))(
        query_rows, key_matrix_rows, value_matrix_rows, spd, table
    )
    attention_mixed = attention_mixed.reshape(egos * count, width)
    y_rows = flattened_rows + jnp.dot(attention_mixed, w_out, preferred_element_type=jnp.float32)
    h2f, normalized_output, second_inverse_deviation = layer_normalize(y_rows, gains[1])
    second_hidden = h2f.astype(jnp.bfloat16)
    upper = jnp.dot(second_hidden, w_up, preferred_element_type=jnp.float32)
    act_f, activation_slope = gelu_parts(upper)
    activation_values = act_f.astype(jnp.bfloat16)
    result = (
        y_rows + jnp.dot(activation_values, w_down, preferred_element_type=jnp.float32)
    ).astype(jnp.bfloat16)
    saved_residuals = (
        first_hidden,
        normalized_input,
        first_inverse_deviation,
        query_rows,
        key_matrix_rows,
        value_matrix_rows,
        attention_probabilities,
        attention_mixed,
        normalized_output,
        second_inverse_deviation,
        second_hidden,
        activation_slope,
        activation_values,
    )
    return (result.reshape(egos, count, width), saved_residuals)


def ffn_back(dout, saved_residuals, w_up, w_down, gains):
    (
        first_hidden,
        normalized_input,
        first_inverse_deviation,
        query_rows,
        key_matrix_rows,
        value_matrix_rows,
        attention_probabilities,
        attention_mixed,
        normalized_output,
        second_inverse_deviation,
        second_hidden,
        activation_slope,
        activation_values,
    ) = saved_residuals
    grad_down = jnp.dot(activation_values.T, dout, preferred_element_type=jnp.float32)
    dgate = jnp.dot(dout, w_down.T, preferred_element_type=jnp.float32)
    grad_u = (dgate * activation_slope).astype(jnp.bfloat16)
    grad_up = jnp.dot(second_hidden.T, grad_u, preferred_element_type=jnp.float32)
    dh2 = jnp.dot(grad_u, w_up.T, preferred_element_type=jnp.float32)
    norm_input_gradient, gain_two = layer_normalize_backward(
        dh2, gains[1], normalized_output, second_inverse_deviation
    )
    return (grad_down, grad_up, dout.astype(jnp.float32) + norm_input_gradient, gain_two)


def attn_back(grad_y, saved_residuals, spd, w_qkv, w_out, gains, table):
    (
        first_hidden,
        normalized_input,
        first_inverse_deviation,
        query_rows,
        key_matrix_rows,
        value_matrix_rows,
        attention_probabilities,
        attention_mixed,
        normalized_output,
        second_inverse_deviation,
        second_hidden,
        activation_slope,
        activation_values,
    ) = saved_residuals
    egos, count = (query_rows.shape[0], query_rows.shape[1])
    grad_yb = grad_y.astype(jnp.bfloat16)
    grad_out = jnp.dot(attention_mixed.T, grad_yb, preferred_element_type=jnp.float32)
    dattn = jnp.dot(grad_yb, w_out.T, preferred_element_type=jnp.float32).astype(jnp.bfloat16)
    dattn = dattn.reshape(query_rows.shape)
    grad_qkv_rows, table_grads = jax.vmap(attend_back, in_axes=(0, 0, 0, 0, 0, 0, None))(
        dattn, query_rows, key_matrix_rows, value_matrix_rows, attention_probabilities, spd, table
    )
    grad_qkv_rows = grad_qkv_rows.reshape(egos * count, -1)
    grad_qkv = jnp.dot(first_hidden.T, grad_qkv_rows, preferred_element_type=jnp.float32)
    first_hidden_gradient = jnp.dot(grad_qkv_rows, w_qkv.T, preferred_element_type=jnp.float32)
    norm_input_gradient, first_norm_gain = layer_normalize_backward(
        first_hidden_gradient, gains[0], normalized_input, first_inverse_deviation
    )
    return (
        grad_qkv,
        grad_out,
        jnp.sum(table_grads, 0),
        grad_y + norm_input_gradient,
        first_norm_gain,
    )


def body(
    node_table,
    touched,
    member_slot,
    distances,
    cotangent,
    w_qkv,
    w_out,
    w_up,
    w_down,
    gains,
    bias_table,
):
    shard_rows = node_table.shape[0]
    width = node_table.shape[1]
    requests = lax.all_to_all(touched, "store", split_axis=1, concat_axis=1, tiled=True)
    valid = requests >= 0
    picked = jnp.take(node_table, jnp.maximum(requests, 0), axis=0)
    picked = jnp.where(valid[..., None], picked, jnp.zeros((), picked.dtype))
    returned = lax.all_to_all(picked, "store", split_axis=1, concat_axis=1, tiled=True)
    fetched = returned
    lists = lax.all_gather(requests[0], "dp", axis=1, tiled=True)
    owners, cap = (fetched.shape[1], fetched.shape[2])
    slots = fetched.reshape(owners * cap, width)
    x_rows = jnp.take(slots, member_slot, axis=0)
    egos, count = member_slot.shape
    result, saved_residuals = layer_forward(
        x_rows, distances, w_qkv, w_out, w_up, w_down, gains, bias_table
    )
    dout = cotangent.reshape(egos * count, width)
    grad_down, grad_up, grad_y, gain_two = ffn_back(dout, saved_residuals, w_up, w_down, gains)
    grad_qkv, grad_out, table_grad, grad_x, first_norm_gain = attn_back(
        grad_y, saved_residuals, distances, w_qkv, w_out, gains, bias_table
    )
    slot_grads = jax.ops.segment_sum(grad_x, member_slot.reshape(-1), num_segments=owners * cap)
    slot_grads = slot_grads.reshape(owners, cap, width)
    returned = lax.all_to_all(
        lax.all_to_all(
            slot_grads.astype(jnp.bfloat16), "dp", split_axis=2, concat_axis=1, tiled=True
        ),
        "store",
        split_axis=0,
        concat_axis=0,
        tiled=True,
    ).astype(slot_grads.dtype)
    target = jnp.where(lists >= 0, lists, shard_rows).reshape(-1)
    summed = jax.ops.segment_sum(
        returned.reshape(-1, returned.shape[2]), target, num_segments=shard_rows + 1
    )
    grad_table = summed[:shard_rows].astype(jnp.bfloat16)
    sum_qkv, sum_out, sum_up, sum_down = (
        lax.psum_scatter(grad_qkv, ("dp", "store"), scatter_dimension=0, tiled=True),
        lax.psum_scatter(grad_out, ("dp", "store"), scatter_dimension=0, tiled=True),
        lax.psum_scatter(grad_up, ("dp", "store"), scatter_dimension=0, tiled=True),
        lax.psum_scatter(grad_down, ("dp", "store"), scatter_dimension=0, tiled=True),
    )
    grad_gains, grad_bias = lax.psum(
        (jnp.stack([first_norm_gain, gain_two]), table_grad), ("dp", "store")
    )
    return (
        result,
        grad_table,
        sum_qkv.astype(jnp.bfloat16),
        sum_out.astype(jnp.bfloat16),
        sum_up.astype(jnp.bfloat16),
        sum_down.astype(jnp.bfloat16),
        grad_gains,
        grad_bias,
    )


def solution(mesh):
    in_specs = (
        P("store", None),
        P(("dp", "store"), None, None),
        P(("dp", "store"), None),
        P(("dp", "store"), None, None),
        P(("dp", "store"), None, None),
        P(),
        P(),
        P(),
        P(),
        P(),
        P(),
    )
    out_specs = (
        P(("dp", "store"), None, None),
        P("store", "dp"),
        P(("dp", "store"), None),
        P(("dp", "store"), None),
        P(("dp", "store"), None),
        P(("dp", "store"), None),
        P(),
        P(),
    )
    return jax.shard_map(body, mesh=mesh, in_specs=in_specs, out_specs=out_specs, check_vma=False)
```

profile of v0, /device:TPU:1, one launch (start us, length us, event | category | flops | bytes accessed | tf_op | source)
XLA Modules:
  0.0 2305.9 jit_solution(761297293275735256)
XLA Ops:
  7.2 8.6 all-to-all-start
  34.5 11.1 fusion.3
  58.3 8.0 convolution_convert_fusion
  82.5 20.4 bitcast_add_fusion
  102.9 18.6 fusion.80
  121.5 15.4 fusion.47
  172.3 15.4 fusion.44
  190.5 10.6 multiply_reduce_fusion
  201.1 12.2 subtract_multiply_fusion
  220.3 8.4 fusion.50
  231.9 7.2 fusion.73
  239.8 9.1 fusion.25
  249.0 8.1 scatter_custom_fusion
  263.9 9.0 reshape.219
  272.9 8.3 all-to-all-start.2
  281.3 24.5 %all-gather = s32[1,16,320]{1,0,2:T(1,128)S(1)} all-gather(s32[1,16,40]{1,0,2:T(1,128)S(1)} %copy.113), channel_id=2, replica_groups=mesh['dp'=8,'store'=16] {'dp'}, dimensions={2}, use_global_device_ids=true | all-gather | bytes 23040 | tf_op jit(solution)/shard_map/all_gather | solution.py:210
  306.0 7.4 reshape.220
  322.6 24.8 %fusion.53 = f32[32,32]{1,0:T(8,128)S(1)} fusion(f32[2,32,256,256]{2,3,1,0:T(8,128)} %copy-done.2, s32[2,256,256]{1,0,2:T(2,128)S(1)} %copy-done.6), kind=kOutput, calls=%fused_computation.74 | convolution fusion | flops 1614807040 | bytes 17305600 | tf_op jit(solution)/shard_map/vmap(bnm,hnm->bh)/dot_general | solution.py:67
  347.4 67.0 %all-reduce = (f32[2,1024]{1,0:T(2,128)}, f32[32,32]{1,0:T(8,128)}) all-reduce(f32[2,1024]{1,0:T(2,128)S(1)} %pad_maximum_fusion, f32[32,32]{1,0:T(8,128)S(1)} %fusion.53), channel_id=1, replica_groups=mesh['dp'=8,'store'=16] {'dp','store'}, use_global_device_ids=true, to_apply=%region_19.20 | all-reduce | flops 3072 | bytes 24576 | tf_op jit(solution)/shard_map/psum | solution.py:245
  419.3 30.1 %scatter_custom_fusion.1 = f32[2049,128]{1,0:T(8,128)} fusion(s32[5120]{0:T(1024)S(1)} %reshape.198, bf16[5120,128]{1,0:T(8,128)(2,1)S(1)} %bitcast.125, f32[]{:T(128)} %constant.34.clone.1), kind=kCustom, calls=%fused_computation.28 | custom fusion | flops 1310720 | bytes 2359812 | tf_op jit(solution)/shard_map/scatter-add | solution.py:235
  451.5 314.4 %reduce-scatter.9.cloned.1.call-done = f32[8,1024]{1,0:T(8,128)} async-done(((f32[1024,1024]{1,0:T(8,128)}), f32[8,1024]{1,0:T(8,128)}) %reduce-scatter.9.cloned.1.call-update) | async-done | bytes 32784 | tf_op jit(solution)/shard_map/reduce_scatter | solution.py:242
  767.3 639.2 %reduce-scatter.7.cloned.1.call-done = f32[8,1024]{1,0:T(8,128)} async-done(((f32[1024,1024]{1,0:T(8,128)}), f32[8,1024]{1,0:T(8,128)}) %reduce-scatter.7.cloned.1.call-update) | async-done | bytes 32784 | tf_op jit(solution)/shard_map/reduce_scatter | solution.py:241
  1407.8 638.4 %reduce-scatter.11.cloned.1.call-done = f32[8,1024]{1,0:T(8,128)} async-done(((f32[1024,1024]{1,0:T(8,128)}), f32[8,1024]{1,0:T(8,128)}) %reduce-scatter.11.cloned.1.call-update) | async-done | bytes 32784 | tf_op jit(solution)/shard_map/reduce_scatter | solution.py:243
  2047.6 250.0 %reduce-scatter.5.cloned.1.call-done = f32[8,3072]{1,0:T(8,128)} async-done(((f32[1024,3072]{1,0:T(8,128)}), f32[8,3072]{1,0:T(8,128)}) %reduce-scatter.5.cloned.1.call-update) | async-done | bytes 98320 | tf_op jit(solution)/shard_map/reduce_scatter | solution.py:240
  (133 shorter events, 125.3 us)
Async XLA Ops:
  7.2 134.1 %copy-start = (bf16[1024,1024]{1,0:T(8,128)(2,1)S(1)}, bf16[1024,1024]{1,0:T(8,128)(2,1)}, u32[]{:S(2)}) copy-start(bf16[1024,1024]{1,0:T(8,128)(2,1)} %param.18) | copy-start | bytes 6291460
  7.2 14.9 all-to-all-start
  29.3 5.2 copy-start.24
  29.3 5.2 copy-start.23
  30.7 21.4 all-to-all-start.1
  34.4 731.5 %reduce-scatter.9.cloned.1.call-start = ((), (), s32[]{:S(2)}) async-start(), calls=%async_computation.10 | async-start | bytes 4227072 | tf_op jit(solution)/shard_map/reduce_scatter | solution.py:242
  54.9 3.5 copy-start.5
  136.8 2.7 copy-start.15
  140.9 5.1 copy-start.3
  141.3 2.7 copy-start.13
  141.3 2.7 copy-start.25
  150.6 1255.9 %reduce-scatter.7.cloned.1.call-start = ((), (), s32[]{:S(2)}) async-start(), calls=%async_computation.9 | async-start | bytes 4227072 | tf_op jit(solution)/shard_map/reduce_scatter | solution.py:241
  150.8 3.8 copy-start.4
  150.8 3.8 copy-start.14
  159.1 1887.2 %reduce-scatter.11.cloned.1.call-start = ((), (), s32[]{:S(2)}) async-start(), calls=%async_computation.11 | async-start | bytes 4227072 | tf_op jit(solution)/shard_map/reduce_scatter | solution.py:243
  163.9 2133.7 %reduce-scatter.5.cloned.1.call-start = ((), (), s32[]{:S(2)}) async-start(), calls=%async_computation.8 | async-start | bytes 12681216 | tf_op jit(solution)/shard_map/reduce_scatter | solution.py:240
  187.7 2.7 copy-start.18
  201.1 12.2 copy-start.12
  213.3 5.7 copy-start.2
  272.9 8.3 copy-start.21
  272.9 33.1 %all-to-all-start.2 = ((bf16[8,2,40960]{2,1,0:T(2,128)(2,1)}), bf16[8,2,40960]{2,1,0:T(2,128)(2,1)S(1)}, u32[]{:S(2)}, u32[]{:S(2)}) async-start(bf16[8,2,40960]{2,1,0:T(2,128)(2,1)} %reshape.219), calls=%async_computation.2 | async-start | bytes 2621440 | tf_op jit(solution)/shard_map/all_to_all | solution.py:226
  318.7 3.8 copy-start.6
  318.7 100.6 %all-to-all-start.3 = ((bf16[16,320,128]{2,1,0:T(8,128)(2,1)}), bf16[16,320,128]{2,1,0:T(8,128)(2,1)S(1)}, u32[]{:S(2)}, u32[]{:S(2)}) async-start(bf16[16,320,128]{2,1,0:T(8,128)(2,1)} %bitcast.27), calls=%async_computation.3 | async-start | bytes 2621440 | tf_op jit(solution)/shard_map/all_to_all | solution.py:225
  414.4 1884.8 %copy-start.1 = (bf16[1024,1024]{1,0:T(8,128)(2,1)S(1)}, bf16[1024,1024]{1,0:T(8,128)(2,1)}, u32[]{:S(2)}) copy-start(bf16[1024,1024]{1,0:T(8,128)(2,1)} %param.18) | copy-start | bytes 6291460
  (10 other events, 12.9 us)
Sparse Core Ops, SparseCore 0:
  150.7 615.1 reduce-scatter.8
  768.4 638.0 reduce-scatter.6
  1408.8 637.4 reduce-scatter.10
  2051.9 245.7 reduce-scatter.4
where the time goes:
time: 2320 us; the launch traced here: 2310 us
  waiting for transfers between devices  1850 us (80%)
  matrix products  162 us (7%)
  blocking collectives  91.5 us (4%)
  other arithmetic  83.8 us (4%)
  local copies, waits for them, and re-layouts  77.5 us (3%)
  starting transfers between devices  24.9 us (1%)
    reduce_scatter x1, waiting for transfers between devices, body(): lax.psum_scatter(grad_out, ('dp', 'store'), scatter_dimension=0, tiled=True)  639 us
    reduce_scatter x1, waiting for transfers between devices, body(): lax.psum_scatter(grad_down, ('dp', 'store'), scatter_dimension=0, tiled=T...  638 us
    reduce_scatter x1, waiting for transfers between devices, body(): lax.psum_scatter(grad_up, ('dp', 'store'), scatter_dimension=0, tiled=True)  314 us
    reduce_scatter x1, waiting for transfers between devices, body(): lax.psum_scatter(grad_qkv, ('dp', 'store'), scatter_dimension=0, tiled=True)  250 us
    psum x1, blocking collectives, body(): lax.psum((jnp.stack([first_norm_gain, gain_two]), table_grad), ('dp', 'st...  67 us
  transfers between devices with their start and end apart: 8, of which 6 were waited for; matrix products, arithmetic and copies ran while one was open for 9% of the time, Pallas kernels for 0%

commit v1 on v0

--- a/solution.py
+++ b/solution.py
@@ -3,6 +3,8 @@
 import jax
 import jax.numpy as jnp
 from jax import lax
+from jax.experimental import pallas as pl
+from jax.experimental.pallas import tpu as pltpu
 from jax.sharding import PartitionSpec as P
 
 EPS = 1e-05
@@ -184,6 +186,232 @@
         grad_y + norm_input_gradient,
         first_norm_gain,
     )
+
+
+MESH = pl.DeviceIdType.MESH
+ORDERS = ((0, 1, 2), (1, 2, 0), (2, 0, 1))
+PIECES = 6
+
+
+def coordinates():
+    dp, store = lax.axis_index("dp"), lax.axis_index("store")
+    return lax.div(dp, 2), lax.rem(dp, 2), lax.div(store, 4), lax.rem(store, 4)
+
+
+def peer(y, core, x, z):
+    return (y * 2 + core, x * 4 + z)
+
+
+def along(axis, offset):
+    y, core, x, z = coordinates()
+    place = [y, x, z]
+    place[axis] = lax.rem(place[axis] + offset, 4)
+    return peer(place[0], core, place[1], place[2]), place[axis]
+
+
+def reduce_kernel(
+    g_qkv, g_out, g_up, g_down, small,
+    o_qkv, o_out, o_up, o_down, o_small,
+    own, got, part0, recv0, part1, recv1, part2, recv2, small_core, small_all,
+    own_sem, core_send, core_recv, send, recv, sc_send, sc_recv, s_send, s_recv,
+):
+    y, core, x, z = coordinates()
+    here = (y, x, z)
+    other = peer(y, 1 - core, x, z)
+    everyone = [other] + [along(a, k)[0] for a in range(3) for k in (1, 2, 3)]
+
+    barrier = pltpu.get_barrier_semaphore()
+    for device in everyone:
+        pl.semaphore_signal(barrier, inc=1, device_id=device, device_id_type=MESH)
+    pl.semaphore_wait(barrier, len(everyone))
+
+    sources = [g_down, g_up, g_out] + [g_qkv] * 3
+    outs = [o_down, o_up, o_out] + [o_qkv] * 3
+    columns = [0, 0, 0, 0, 1024, 2048]
+    sends = []
+
+    local, cross = [], []
+    tiny = pltpu.make_async_remote_copy(
+        src_ref=small, dst_ref=small_core, send_sem=sc_send, recv_sem=sc_recv,
+        device_id=other, device_id_type=MESH)
+    tiny.start()
+    for j in range(PIECES):
+        cols = pl.ds(columns[j], 1024)
+        remote = pltpu.make_async_remote_copy(
+            src_ref=sources[j].at[:, 1 - core, :, cols], dst_ref=got.at[j],
+            send_sem=core_send.at[j], recv_sem=core_recv.at[j],
+            device_id=other, device_id_type=MESH)
+        remote.start()
+        cross.append(remote)
+        keep = pltpu.make_async_copy(sources[j].at[:, core, :, cols], own.at[j], own_sem.at[j])
+        keep.start()
+        local.append(keep)
+
+    tiny.wait()
+
+    def spread_small(axis):
+        copies = []
+        for k in (1, 2, 3):
+            device, _ = along(axis, k)
+            copy = pltpu.make_async_remote_copy(
+                src_ref=small_all.at[axis, here[axis]], dst_ref=small_all.at[axis, here[axis]],
+                send_sem=s_send.at[axis, k - 1], recv_sem=s_recv.at[axis, k - 1],
+                device_id=device, device_id_type=MESH)
+            copy.start()
+            copies.append(copy)
+        return copies
+
+    def total_small(axis):
+        return (small_all[axis, 0] + small_all[axis, 1]) + (small_all[axis, 2] + small_all[axis, 3])
+
+    small_all[0, here[0]] = small[...] + small_core[...]
+    tiny_copies = spread_small(0)
+
+    def scatter(j, stage, part):
+        order = ORDERS[j % 3]
+        axis = order[stage]
+        left = [a for a in (0, 1, 2) if a not in order[:stage]]
+        where = left.index(axis)
+        landing = (recv0, recv1, recv2)[stage]
+        copies = []
+        for k in (1, 2, 3):
+            device, place = along(axis, k)
+            block = (j,) + (slice(None),) * where + (place,)
+            copy = pltpu.make_async_remote_copy(
+                src_ref=part.at[block], dst_ref=landing.at[j, k - 1],
+                send_sem=send.at[stage, j, k - 1], recv_sem=recv.at[stage, j, k - 1],
+                device_id=device, device_id_type=MESH)
+            copy.start()
+            copies.append(copy)
+        return copies
+
+    flight = [None] * PIECES
+    for j in range(PIECES):
+        local[j].wait()
+        cross[j].wait_recv()
+
+        def add_cores(i, carry, j=j):
+            yy, xx = lax.div(i, 4), lax.rem(i, 4)
+            rows = pl.ds(pl.multiple_of(xx * 32, 32), 32)
+            total = own[j, yy, rows, :].astype(jnp.float32) + got[j, yy, rows, :].astype(jnp.float32)
+            for zz in range(4):
+                mine = total[8 * zz : 8 * zz + 8]
+                part0[j, yy, xx, zz] = jnp.concatenate([mine[:, :512], mine[:, 512:]], 0).astype(jnp.bfloat16)
+            return carry
+
+        lax.fori_loop(0, 16, add_cores, 0)
+        flight[j] = scatter(j, 0, part0)
+
+    for copy in tiny_copies:
+        copy.wait()
+    small_all[1, here[1]] = total_small(0)
+    tiny_copies = spread_small(1)
+
+    for j in range(PIECES):
+        for copy in flight[j]:
+            copy.wait_recv()
+        sends += flight[j]
+        axis = ORDERS[j % 3][0]
+
+        def add_first(i, carry, j=j, axis=axis):
+            a, b = lax.div(i, 4), lax.rem(i, 4)
+            block = [a, b]
+            block.insert(axis, here[axis])
+            total = part0[(j,) + tuple(block)].astype(jnp.float32)
+            for k in range(3):
+                total = total + recv0[j, k, a, b].astype(jnp.float32)
+            part1[j, a, b] = total.astype(jnp.bfloat16)
+            return carry
+
+        lax.fori_loop(0, 16, add_first, 0)
+        flight[j] = scatter(j, 1, part1)
+
+    for copy in tiny_copies:
+        copy.wait()
+    small_all[2, here[2]] = total_small(1)
+    tiny_copies = spread_small(2)
+
+    for j in range(PIECES):
+        for copy in flight[j]:
+            copy.wait_recv()
+        sends += flight[j]
+        order = ORDERS[j % 3]
+        where = [a for a in (0, 1, 2) if a != order[0]].index(order[1])
+
+        def add_second(i, carry, j=j, axis=order[1], where=where):
+            block = [i]
+            block.insert(where, here[axis])
+            total = part1[(j,) + tuple(block)].astype(jnp.float32)
+            for k in range(3):
+                total = total + recv1[j, k, i].astype(jnp.float32)
+            part2[j, i] = total.astype(jnp.bfloat16)
+            return carry
+
+        lax.fori_loop(0, 4, add_second, 0)
+        flight[j] = scatter(j, 2, part2)
+
+    for copy in tiny_copies:
+        copy.wait()
+    o_small[...] = total_small(2)
+
+    for j in range(PIECES):
+        for copy in flight[j]:
+            copy.wait_recv()
+        sends += flight[j]
+        axis = ORDERS[j % 3][2]
+        total = part2[j, here[axis]].astype(jnp.float32)
+        for k in range(3):
+            total = total + recv2[j, k].astype(jnp.float32)
+        joined = jnp.concatenate([total[:8], total[8:]], 1).astype(jnp.bfloat16)
+        outs[j][:, columns[j] : columns[j] + 1024] = joined
+
+    for copy in cross + sends:
+        copy.wait_send()
+
+
+def reduce_gradients(g_qkv, g_out, g_up, g_down, small):
+    bf16, f32 = jnp.bfloat16, jnp.float32
+    hbm = pl.BlockSpec(memory_space=pl.ANY)
+    vmem = pl.BlockSpec(memory_space=pltpu.VMEM)
+    dma = pltpu.SemaphoreType.DMA
+    split = lambda g: g.reshape(4, 2, 128, g.shape[1])
+    return pl.pallas_call(
+        reduce_kernel,
+        name="reduce_gradients",
+        out_shape=(
+            jax.ShapeDtypeStruct((8, 3072), bf16),
+            jax.ShapeDtypeStruct((8, 1024), bf16),
+            jax.ShapeDtypeStruct((8, 1024), bf16),
+            jax.ShapeDtypeStruct((8, 1024), bf16),
+            jax.ShapeDtypeStruct(small.shape, f32),
+        ),
+        in_specs=[hbm] * 4 + [vmem],
+        out_specs=[vmem] * 5,
+        scratch_shapes=[
+            pltpu.VMEM((PIECES, 4, 128, 1024), bf16),
+            pltpu.VMEM((PIECES, 4, 128, 1024), bf16),
+            pltpu.VMEM((PIECES, 4, 4, 4, 16, 512), bf16),
+            pltpu.VMEM((PIECES, 3, 4, 4, 16, 512), bf16),
+            pltpu.VMEM((PIECES, 4, 4, 16, 512), bf16),
+            pltpu.VMEM((PIECES, 3, 4, 16, 512), bf16),
+            pltpu.VMEM((PIECES, 4, 16, 512), bf16),
+            pltpu.VMEM((PIECES, 3, 16, 512), bf16),
+            pltpu.VMEM(small.shape, f32),
+            pltpu.VMEM((3, 4) + small.shape, f32),
+            dma((PIECES,)),
+            dma((PIECES,)),
+            dma((PIECES,)),
+            dma((3, PIECES, 3)),
+            dma((3, PIECES, 3)),
+            dma,
+            dma,
+            dma((3, 3)),
+            dma((3, 3)),
+        ],
+        compiler_params=pltpu.CompilerParams(
+            collective_id=0, has_side_effects=True, vmem_limit_bytes=40 * 1024 * 1024
+        ),
+    )(split(g_qkv), split(g_out), split(g_up), split(g_down), small)
 
 
 def body(
@@ -236,22 +464,23 @@
         returned.reshape(-1, returned.shape[2]), target, num_segments=shard_rows + 1
     )
     grad_table = summed[:shard_rows].astype(jnp.bfloat16)
-    sum_qkv, sum_out, sum_up, sum_down = (
-        lax.psum_scatter(grad_qkv, ("dp", "store"), scatter_dimension=0, tiled=True),
-        lax.psum_scatter(grad_out, ("dp", "store"), scatter_dimension=0, tiled=True),
-        lax.psum_scatter(grad_up, ("dp", "store"), scatter_dimension=0, tiled=True),
-        lax.psum_scatter(grad_down, ("dp", "store"), scatter_dimension=0, tiled=True),
-    )
-    grad_gains, grad_bias = lax.psum(
-        (jnp.stack([first_norm_gain, gain_two]), table_grad), ("dp", "store")
-    )
+    grad_qkv, grad_out, grad_up, grad_down = (
+        g.astype(jnp.bfloat16) for g in (grad_qkv, grad_out, grad_up, grad_down)
+    )
+    small = jnp.concatenate(
+        [first_norm_gain.reshape(8, 128), gain_two.reshape(8, 128), table_grad.reshape(8, 128)]
+    )
+    sum_qkv, sum_out, sum_up, sum_down, small = reduce_gradients(
+        grad_qkv, grad_out, grad_up, grad_down, small
+    )
+    grad_gains, grad_bias = small[:16].reshape(2, 1024), small[16:].reshape(32, 32)
     return (
         result,
         grad_table,
-        sum_qkv.astype(jnp.bfloat16),
-        sum_out.astype(jnp.bfloat16),
-        sum_up.astype(jnp.bfloat16),
-        sum_down.astype(jnp.bfloat16),
+        sum_qkv,
+        sum_out,
+        sum_up,
+        sum_down,
         grad_gains,
         grad_bias,
     )

time: 2320 us -> 414 us (0.18)
  waiting for transfers between devices: 1850 us -> 0.87 us
  blocking collectives: 91.5 us -> 14.6 us
  Pallas kernels: 0 us -> 48.5 us
    reduce_scatter x4 -> x0, waiting for transfers between devices: 1840 us -> none  [the longest x1 639 us: body(): lax.psum_scatter(grad_out, ('dp', 'store'), scatter_dimension=0, tiled=True)]
    psum x1 -> x0, blocking collectives: 67 us -> none  [body(): lax.psum((jnp.stack([first_norm_gain, gain_two]), table_grad), ('dp', 'st...]
    pallas_call x0 -> x1, Pallas kernels: none -> 48.5 us  [reduce_gradients(): pl.pallas_call(reduce_kernel, name='reduce_gradients', out_shape=(jax.Sha...]
  transfers between devices with their start and end apart: 8 -> 4, of which waited for: 6 -> 1; matrix products, arithmetic and copies ran while one was open for 9% -> 16% of each run, Pallas kernels for 0% -> 12%
where the time goes in v1:
time: 414 us; the launch traced here: 408 us
  matrix products  156 us (38%)
  other arithmetic  84.5 us (20%)
  local copies, waits for them, and re-layouts  75.9 us (18%)
  Pallas kernels  48.5 us (12%)
  starting transfers between devices  26.3 us (6%)
  blocking collectives  14.6 us (4%)
    pallas_call x1, Pallas kernels, reduce_gradients(): pl.pallas_call(reduce_kernel, name='reduce_gradients', out_shape=(jax.Sha...  48.5 us
    scatter-add x1, other arithmetic, body(): jax.ops.segment_sum(returned.reshape(-1, returned.shape[2]), target, num_...  29.5 us
    unnamed x75, local copies, waits for them, and re-layouts  27 us
    dot_general x1, matrix products, attend_back(): jnp.einsum('bnm,hnm->bh', onehot, dscores, precision=lax.Precision.HIGHEST)  24.8 us
    dot_general x1, matrix products, attend(): jnp.einsum('nhc,mhc->hnm', query_rows, key_matrix_rows, preferred_element...  19.9 us
    sub x1, other arithmetic, attend(): attention_probabilities = jax.nn.softmax(scores, axis=-1)  18.9 us
    mul x1, other arithmetic, attend_back(): attention_probabilities * (dprobs - jnp.sum(dprobs * attention_probabilit...  18 us
    dot_general x1, matrix products, attend(): jnp.einsum('hnm,mhc->nhc', probs_b, value_matrix_rows, preferred_element_...  15.4 us
  transfers between devices with their start and end apart: 4, of which 1 were waited for; matrix products, arithmetic and copies ran while one was open for 16% of the time, Pallas kernels for 12%

profile of v1, /device:TPU:1, one launch (start us, length us, event | category | flops | bytes accessed | tf_op | source)
XLA Modules:
  0.0 407.7 jit_solution(9795556370249064799)
XLA Ops:
  0.6 8.6 %all-to-all-start = ((s32[1,16,40]{2,0,1:T(1,128)}), s32[1,16,40]{2,0,1:T(1,128)S(1)}, u32[]{:S(2)}, u32[]{:S(2)}) async-start(s32[1,16,40]{2,0,1:T(1,128)} %bitcast.165), calls=%async_computation | async-start | bytes 16384 | tf_op jit(solution)/shard_map/all_to_all | solution.py:432
  15.7 6.6 %gather_fusion = bf16[640,1024]{1,0:T(8,128)(2,1)S(1)} fusion(bf16[2048,1024]{1,0:T(8,128)(2,1)} %param.11, s32[1024]{0:T(1024)S(1)} %pad_clamp_fusion.1), kind=kCustom, calls=%fused_computation | custom fusion | bytes 2624000 | tf_op jit(solution)/shard_map/jit(_take)/gather | solution.py:434
  23.6 5.8 %all-to-all-start.1 = ((bf16[1,16,40,1024]{3,2,0,1:T(8,128)(2,1)}), bf16[1,16,40,1024]{3,2,0,1:T(8,128)(2,1)S(1)}, u32[]{:S(2)}, u32[]{:S(2)}) async-start(bf16[1,16,40,1024]{3,2,0,1:T(8,128)(2,1)} %select_select_fusion), calls=%async_computation.1 | async-start | bytes 2621440 | tf_op jit(solution)/shard_map/all_to_all | solution.py:436
  29.5 11.1 %fusion.3 = f32[2,256,256,32]{1,3,2,0:T(8,128)} fusion(f32[32,32]{1,0:T(8,128)S(1)} %copy-done.22, s32[2,256,256]{1,0,2:T(2,128)} %copy.107), kind=kOutput, calls=%fused_computation.13 | convolution fusion | flops 1614807040 | bytes 17305600 | tf_op jit(solution)/shard_map/vmap(bnm,bh->hnm)/dot_general | solution.py:43
  40.6 14.6 %all-gather = s32[1,16,320]{1,0,2:T(1,128)S(1)} all-gather(s32[1,16,40]{1,0,2:T(1,128)S(1)} %copy.113), channel_id=2, replica_groups=mesh['dp'=8,'store'=16] {'dp'}, dimensions={2}, use_global_device_ids=true | all-gather | bytes 23040 | tf_op jit(solution)/shard_map/all_gather | solution.py:438
  64.1 8.0 %convolution_convert_fusion.1 = bf16[512,3072]{1,0:T(8,128)(2,1)} fusion(bf16[1024,3072]{1,0:T(8,128)(2,1)} %param.16, f32[1024]{0:T(1024)S(1)} %bitcast.148, f32[512]{0:T(512)S(1)} %bitcast.156, f32[512]{0:T(512)S(1)} %bitcast.160, bf16[512,1024]{1,0:T(8,128)(2,1)S(1)} %copy-done.4, pred[512]{0:T(512)(128)(4,1)S(1)} %broadcast_in_dim.70), kind=kOutput, calls=%fused_computation.17 | convolution fusion | flops 3225944064 | bytes 10494464 | tf_op jit(solution)/shard_map/dot_general | solution.py:91
  76.8 5.5 %reshape.190 = bf16[2,256,3,32,32]{1,0,4,3,2:T(2,128)(2,1)} reshape(bf16[512,3072]{0,1:T(8,128)(2,1)} %copy.103) | data formatting | bytes 6291456 | tf_op jit(solution)/shard_map/reshape | solution.py:92
  88.3 19.9 %bitcast_add_fusion = f32[2,32,256,256]{2,3,1,0:T(8,128)} fusion(f32[2,256,256,32]{1,3,2,0:T(8,128)} %fusion.3, bf16[2,256,1,32,32]{1,0,4,3,2:T(2,128)(2,1)S(1)} %get-tuple-element.25, bf16[2,256,1,32,32]{1,0,4,3,2:T(2,128)(2,1)S(1)} %get-tuple-element.24), kind=kOutput, calls=%fused_computation.5 | convolution fusion | flops 276824064 | bytes 35651584 | tf_op jit(solution)/shard_map/vmap(nhc,mhc->hnm)/dot_general | solution.py:45
  108.3 18.9 %fusion.77 = (f32[2,32,256]{2,1,0:T(8,128)S(1)}, f32[2,32,256,256]{2,3,1,0:T(8,128)}) fusion(f32[2,32,256,256]{2,3,1,0:T(8,128)} %bitcast_add_fusion), kind=kOutput, calls=%fused_computation.124 | output fusion | flops 8388863 | bytes 33619968 | tf_op jit(solution)/shard_map/vmap()/sub | solution.py:49
  127.2 15.4 %fusion.47 = bf16[2,256,32,32]{1,3,2,0:T(8,128)(2,1)} fusion(bf16[2,256,1,32,32]{1,0,4,3,2:T(2,128)(2,1)} %get-tuple-element.26, f32[2,32,256]{2,1,0:T(8,128)S(1)} %get-tuple-element.33, f32[2,32,256,256]{2,3,1,0:T(8,128)} %bitcast_add_fusion), kind=kOutput, calls=%fused_computation.73 | convolution fusion | flops 281559296 | bytes 18939904 | tf_op jit(solution)/shard_map/vmap(hnm,mhc->nhc)/dot_general | solution.py:51
  160.5 14.6 %fusion.44 = bf16[2,256,32,32]{1,3,2,0:T(8,128)(2,1)} fusion(bf16[2,256,32,32]{1,0,3,2:T(2,128)(2,1)S(1)} %reshape.194, f32[2,32,256]{2,1,0:T(8,128)S(1)} %get-tuple-element.33, f32[2,32,256,256]{2,3,1,0:T(8,128)} %bitcast_add_fusion), kind=kOutput, calls=%fused_computation.72 | convolution fusion | flops 281559296 | bytes 18939904 | tf_op jit(solution)/shard_map/vmap(hnm,nhc->mhc)/dot_general | solution.py:75
  175.1 10.5 %multiply_reduce_fusion = (f32[2,32,256]{2,1,0:T(8,128)S(1)}, f32[2,32,256,256]{2,3,1,0:T(8,128)}) fusion(f32[2,32,256,256]{2,3,1,0:T(8,128)} %get-tuple-element.34, f32[2,32,256]{2,1,0:T(8,128)S(1)} %get-tuple-element.33, bf16[2,256,1,32,32]{1,0,4,3,2:T(2,128)(2,1)S(1)} %copy-done.20, bf16[2,256,32,32]{1,0,3,2:T(2,128)(2,1)S(1)} %reshape.194), kind=kOutput, calls=%fused_computation.10 | convolution fusion | flops 281001984 | bytes 35782656 | tf_op jit(solution)/shard_map/vmap(nhc,mhc->hnm)/dot_general | solution.py:62
  185.6 18.0 %subtract_multiply_fusion = f32[2,32,256,256]{2,3,1,0:T(8,128)} fusion(f32[2,32,256,256]{2,3,1,0:T(8,128)} %get-tuple-element.41, f32[2,32,256]{2,1,0:T(8,128)S(1)} %get-tuple-element.40, f32[2,32,256,256]{2,3,1,0:T(8,128)} %get-tuple-element.34, f32[2,32,256]{2,1,0:T(8,128)S(1)} %get-tuple-element.33), kind=kLoop, calls=%fused_computation.9 | loop fusion | flops 12582912 | bytes 50462720 | tf_op jit(solution)/shard_map/vmap()/mul | solution.py:65
  203.7 8.4 %fusion.50 = bf16[2,256,32,32]{1,3,2,0:T(8,128)(2,1)S(1)} fusion(f32[2,32,256,256]{2,3,1,0:T(8,128)} %subtract_multiply_fusion, bf16[2,256,1,32,32]{1,0,4,3,2:T(2,128)(2,1)S(1)} %copy-done.11), kind=kOutput, calls=%fused_computation.74 | convolution fusion | flops 277348352 | bytes 18874368 | tf_op jit(solution)/shard_map/vmap(hnm,nhc->mhc)/dot_general | solution.py:74
  212.1 7.6 %fusion.51 = bf16[2,256,32,32]{1,3,2,0:T(8,128)(2,1)S(1)} fusion(f32[2,32,256,256]{2,3,1,0:T(8,128)} %subtract_multiply_fusion, bf16[2,256,1,32,32]{1,0,4,3,2:T(2,128)(2,1)S(1)} %copy-done.9), kind=kOutput, calls=%fused_computation.75 | convolution fusion | flops 277348352 | bytes 18874368 | tf_op jit(solution)/shard_map/vmap(hnm,mhc->nhc)/dot_general | solution.py:71
  224.6 5.6 %fusion.25 = (f32[1024]{0:T(1024)S(1)}, f32[512]{0:T(512)S(1)}, f32[512]{0:T(512)S(1)}, f32[512,1024]{1,0:T(8,128)}) fusion(f32[512]{0:T(512)S(1)} %bitcast.157, f32[512]{0:T(512)S(1)} %bitcast.161, bf16[512,1024]{1,0:T(8,128)(2,1)S(1)} %copy-done.4, pred[512]{0:T(512)(128)(4,1)S(1)} %broadcast_in_dim.70, f32[1024]{0:T(1024)S(1)} %bitcast.149, ...), kind=kOutput, calls=%fused_computation.42 | convolution fusion | flops 3226466304 | bytes 12599808 | tf_op jit(solution)/shard_map/dot_general | solution.py:178
  230.2 8.1 %scatter_custom_fusion = f32[640,1024]{1,0:T(8,128)} fusion(s32[512]{0:T(512)} %bitcast.168, f32[512,1024]{1,0:T(8,128)S(1)} %copy-done.13, f32[512,1024]{1,0:T(8,128)} %get-tuple-element.42, f32[]{:T(128)} %constant.34.clone.1, f32[512]{0:T(512)S(1)} %broadcast_multiply_fusion, f32[512]{0:T(512)S(1)} %broadcast_multiply_fusion.1, f32[1024]{0:T(1024)S(1)} %bitcast.150, ...), kind=kCustom, calls=%fused_computation.41 | custom fusion | flops 5767168 | bytes 7877632 | tf_op jit(solution)/shard_map/scatter-add | solution.py:451
  245.1 9.0 %reshape.255 = bf16[8,2,40960]{2,1,0:T(2,128)(2,1)} reshape(bf16[1024,16,40]{2,1,0:T(8,128)(2,1)} %bitcast.128) | data formatting | bytes 2621440
  258.7 24.8 %fusion.53 = f32[32,32]{1,0:T(8,128)S(1)} fusion(f32[2,32,256,256]{2,3,1,0:T(8,128)} %subtract_multiply_fusion, s32[2,256,256]{1,0,2:T(2,128)S(1)} %copy-done.7), kind=kOutput, calls=%fused_computation.78 | convolution fusion | flops 1614807040 | bytes 17305600 | tf_op jit(solution)/shard_map/vmap(bnm,hnm->bh)/dot_general | solution.py:69
  292.1 9.1 %reshape.256 = bf16[1024,16,40]{2,1,0:T(8,128)(2,1)} reshape(bf16[8,2,40960]{2,1,0:T(2,128)(2,1)} %all-to-all-done.2) | data formatting | bytes 2621440
  306.6 7.2 %all-to-all-start.3 = ((bf16[16,320,128]{2,1,0:T(8,128)(2,1)}), bf16[16,320,128]{2,1,0:T(8,128)(2,1)}, u32[]{:S(2)}, u32[]{:S(2)}) async-start(bf16[16,320,128]{2,1,0:T(8,128)(2,1)} %bitcast.131), calls=%async_computation.3 | async-start | bytes 2621440 | tf_op jit(solution)/shard_map/all_to_all | solution.py:453
  313.9 6.3 %convolution_convert_fusion = bf16[1024,3072]{1,0:T(8,128)(2,1)S(1)} fusion(bf16[512,3072]{0,1:T(8,128)(2,1)} %copy-done.21, f32[1024]{0:T(1024)S(1)} %bitcast.151, f32[512]{0:T(512)S(1)} %bitcast.159, f32[512]{0:T(512)S(1)} %bitcast.163, bf16[512,1024]{1,0:T(8,128)(2,1)S(1)} %copy-done.4, pred[512]{0:T(512)(128)(4,1)S(1)} %broadcast_in_dim.70), kind=kOutput, calls=%fused_computation.16 | convolution fusion | flops 3227516928 | bytes 10494464 | tf_op jit(solution)/shard_map/dot_general | solution.py:177
  320.2 48.5 %reduce_gradients.1 = (bf16[8,3072]{1,0:T(8,128)(2,1)S(1)}, bf16[8,1024]{1,0:T(8,128)(2,1)S(1)}, bf16[8,1024]{1,0:T(8,128)(2,1)S(1)}, bf16[8,1024]{1,0:T(8,128)(2,1)S(1)}, f32[24,128]{1,0:T(8,128)S(1)}) custom-call(bf16[4,2,128,3072]{3,2,1,0:T(8,128)(2,1)S(1)} %bitcast.121, bf16[4,2,128,1024]{3,2,1,0:T(8,128)(2,1)S(1)} %bitcast.123, ...), custom_call_target="tpu_custom_call" | custom-call | tf_op jit(solution)/shard_map/reduce_gradients/pallas_call | solution.py:378
  374.7 29.5 %scatter_custom_fusion.1 = f32[2049,128]{1,0:T(8,128)S(1)} fusion(s32[5120]{0:T(1024)} %reshape.234, bf16[5120,128]{1,0:T(8,128)(2,1)} %bitcast.39, f32[]{:T(128)} %constant.34.clone.1), kind=kCustom, calls=%fused_computation.29 | custom fusion | flops 1310720 | bytes 2360320 | tf_op jit(solution)/shard_map/scatter-add | solution.py:463
  (133 shorter events, 84.5 us)
Async XLA Ops:
  0.6 146.4 %copy-start = (bf16[1024,1024]{1,0:T(8,128)(2,1)S(1)}, bf16[1024,1024]{1,0:T(8,128)(2,1)}, u32[]{:S(2)}) copy-start(bf16[1024,1024]{1,0:T(8,128)(2,1)} %param.18) | copy-start | bytes 6291460
  0.6 14.9 %all-to-all-start = ((s32[1,16,40]{2,0,1:T(1,128)}), s32[1,16,40]{2,0,1:T(1,128)S(1)}, u32[]{:S(2)}, u32[]{:S(2)}) async-start(s32[1,16,40]{2,0,1:T(1,128)} %bitcast.165), calls=%async_computation | async-start | bytes 16384 | tf_op jit(solution)/shard_map/all_to_all | solution.py:432
  22.3 7.2 %copy-start.22 = (f32[32,32]{1,0:T(8,128)S(1)}, f32[32,32]{1,0:T(8,128)}, u32[]{:S(2)}) copy-start(f32[32,32]{1,0:T(8,128)} %param.21) | copy-start | bytes 12292
  23.6 34.0 %all-to-all-start.1 = ((bf16[1,16,40,1024]{3,2,0,1:T(8,128)(2,1)}), bf16[1,16,40,1024]{3,2,0,1:T(8,128)(2,1)S(1)}, u32[]{:S(2)}, u32[]{:S(2)}) async-start(bf16[1,16,40,1024]{3,2,0,1:T(8,128)(2,1)} %select_select_fusion), calls=%async_computation.1 | async-start | bytes 2621440 | tf_op jit(solution)/shard_map/all_to_all | solution.py:436
  60.7 3.5 copy-start.4
  142.6 2.7 copy-start.17
  146.7 7.0 %copy-start.5 = (f32[512,1024]{1,0:T(8,128)}, f32[512,1024]{1,0:T(8,128)S(1)}, u32[]{:S(2)}) copy-start(f32[512,1024]{1,0:T(8,128)S(1)} %get-tuple-element.36) | copy-start | bytes 6291460
  147.1 2.7 copy-start.19
  160.5 14.6 %copy-start.20 = (bf16[2,256,1,32,32]{1,0,4,3,2:T(2,128)(2,1)S(1)}, bf16[2,256,1,32,32]{1,0,4,3,2:T(2,128)(2,1)}, u32[]{:S(2)}) copy-start(bf16[2,256,1,32,32]{1,0,4,3,2:T(2,128)(2,1)} %get-tuple-element.26) | copy-start | bytes 3145732
  185.6 18.0 %copy-start.11 = (bf16[2,256,1,32,32]{1,0,4,3,2:T(2,128)(2,1)S(1)}, bf16[2,256,1,32,32]{1,0,4,3,2:T(2,128)(2,1)}, u32[]{:S(2)}) copy-start(bf16[2,256,1,32,32]{1,0,4,3,2:T(2,128)(2,1)} %copy-done.10) | copy-start | bytes 3145732
  203.7 8.4 %copy-start.9 = (bf16[2,256,1,32,32]{1,0,4,3,2:T(2,128)(2,1)S(1)}, bf16[2,256,1,32,32]{1,0,4,3,2:T(2,128)(2,1)}, u32[]{:S(2)}) copy-start(bf16[2,256,1,32,32]{1,0,4,3,2:T(2,128)(2,1)} %copy-done.8) | copy-start | bytes 3145732
  212.1 7.6 %copy-start.18 = (bf16[2,256,32,32]{1,3,2,0:T(8,128)(2,1)S(1)}, bf16[2,256,32,32]{1,3,2,0:T(8,128)(2,1)}, u32[]{:S(2)}) copy-start(bf16[2,256,32,32]{1,3,2,0:T(8,128)(2,1)} %fusion.44) | copy-start | bytes 3145732
  219.8 4.3 %slice-start = ((s8[6291456]{0:T(1024)(128)(4,1)}), s8[2097152]{0:T(1024)(128)(4,1)S(1)}, s32[]{:S(2)}) async-start(s8[6291456]{0:T(1024)(128)(4,1)} %bitcast.169), calls=%async_computation.4 | async-start | bytes 4194304
  224.6 5.6 %copy-start.21 = (bf16[512,3072]{0,1:T(8,128)(2,1)}, bf16[512,3072]{0,1:T(8,128)(2,1)S(1)}, u32[]{:S(2)}) copy-start(bf16[512,3072]{0,1:T(8,128)(2,1)S(1)} %constant_dynamic-update-slice_fusion) | copy-start | bytes 9437188
  224.6 5.6 %copy-start.13 = (f32[512,1024]{1,0:T(8,128)S(1)}, f32[512,1024]{1,0:T(8,128)}, u32[]{:S(2)}) copy-start(f32[512,1024]{1,0:T(8,128)} %copy-done.12) | copy-start | bytes 6291460
  254.0 4.7 %copy-start.7 = (s32[2,256,256]{1,0,2:T(2,128)S(1)}, s32[2,256,256]{1,0,2:T(2,128)}, u32[]{:S(2)}) copy-start(s32[2,256,256]{1,0,2:T(2,128)} %copy.107) | copy-start | bytes 1572868
  254.0 38.1 %all-to-all-start.2 = ((bf16[8,2,40960]{2,1,0:T(2,128)(2,1)}), bf16[8,2,40960]{2,1,0:T(2,128)(2,1)}, u32[]{:S(2)}, u32[]{:S(2)}) async-start(bf16[8,2,40960]{2,1,0:T(2,128)(2,1)} %reshape.255), calls=%async_computation.2 | async-start | bytes 2621440 | tf_op jit(solution)/shard_map/all_to_all | solution.py:454
  283.6 3.0 copy-start.14
  283.6 3.0 copy-start.16
  306.6 68.1 %all-to-all-start.3 = ((bf16[16,320,128]{2,1,0:T(8,128)(2,1)}), bf16[16,320,128]{2,1,0:T(8,128)(2,1)}, u32[]{:S(2)}, u32[]{:S(2)}) async-start(bf16[16,320,128]{2,1,0:T(8,128)(2,1)} %bitcast.131), calls=%async_computation.3 | async-start | bytes 2621440 | tf_op jit(solution)/shard_map/all_to_all | solution.py:453
  313.9 6.4 %copy-start.2 = (bf16[1024,1024]{1,0:T(8,128)(2,1)S(1)}, bf16[1024,1024]{1,0:T(8,128)(2,1)}, u32[]{:S(2)}) copy-start(bf16[1024,1024]{1,0:T(8,128)(2,1)} %convolution_convert_fusion.4) | copy-start | bytes 6291460
  313.9 6.4 %copy-start.3 = (bf16[1024,1024]{1,0:T(8,128)(2,1)S(1)}, bf16[1024,1024]{1,0:T(8,128)(2,1)}, u32[]{:S(2)}) copy-start(bf16[1024,1024]{1,0:T(8,128)(2,1)} %convolution_convert_fusion.3) | copy-start | bytes 6291460
  320.2 49.8 %copy-start.26 = (bf16[512,1024]{1,0:T(8,128)(2,1)S(1)}, bf16[512,1024]{1,0:T(8,128)(2,1)}, u32[]{:S(2)}) copy-start(bf16[512,1024]{1,0:T(8,128)(2,1)} %get-tuple-element.37) | copy-start | bytes 3145732
  370.1 37.4 %copy-start.1 = (bf16[1024,1024]{1,0:T(8,128)(2,1)S(1)}, bf16[1024,1024]{1,0:T(8,128)(2,1)}, u32[]{:S(2)}) copy-start(bf16[1024,1024]{1,0:T(8,128)(2,1)} %param.18) | copy-start | bytes 6291460
  (9 other events, 18.0 us)

commit v2 on v1

v2 whole, which is shorter than its diff:
```python
import math

import jax
import jax.numpy as jnp
from jax import lax
from jax.experimental import pallas as pl
from jax.experimental.pallas import tpu as pltpu
from jax.sharding import PartitionSpec as P

EPS = 1e-05
ROOT_HALF = 1.0 / math.sqrt(2.0)
ROOT_TWO_PI = 1.0 / math.sqrt(2.0 * math.pi)


def layer_normalize(value, gain):
    mean = jnp.mean(value, -1, keepdims=True)
    centred = value - mean
    rstd = lax.rsqrt(jnp.mean(centred * centred, -1, keepdims=True) + EPS)
    vhat = centred * rstd
    return (vhat * gain, vhat, rstd)


def layer_normalize_backward(grad, gain, vhat, rstd):
    scaled = grad * gain
    first = jnp.mean(scaled, -1, keepdims=True)
    second = jnp.mean(scaled * vhat, -1, keepdims=True)
    return (rstd * (scaled - first - vhat * second), jnp.sum(grad * vhat, 0))


def gelu_parts(upper):
    normal_cdf = 0.5 * (1.0 + jax.scipy.special.erf(upper * ROOT_HALF))
    activation_slope = normal_cdf + upper * jnp.exp(-0.5 * upper * upper) * ROOT_TWO_PI
    return (upper * normal_cdf, activation_slope)


GROUP = 8
LOG2E = math.log2(math.e)


def head_mask(rows, width, head):
    lanes = lax.broadcasted_iota(jnp.int32, (rows, width), 1)
    return lax.div(lanes, width // GROUP) == head


def only_head(value, head):
    return jnp.where(head_mask(value.shape[0], value.shape[1], head), value, jnp.zeros((), value.dtype))


def attend_kernel(q_ref, k_ref, v_ref, spd_ref, table_ref, mixed_ref, probs_ref, scores):
    group = pl.program_id(1)
    count = q_ref.shape[0]
    head_width = q_ref.shape[1] // GROUP
    scale = LOG2E * head_width ** (-0.5)
    chunk = 32
    q, k, v = q_ref[...], k_ref[...], v_ref[...]
    lookups = [
        jnp.broadcast_to(table_ref[pl.ds(group * GROUP + j, 1), :], (8, 128)) for j in range(GROUP)
    ]

    def look_up(n, carry):
        rows = pl.ds(pl.multiple_of(n * 8, 8), 8)
        for a in range(0, count, 128):
            spd = spd_ref[0, rows, a : a + 128]
            for j in range(GROUP):
                scores[j, rows, a : a + 128] = jnp.take_along_axis(
                    lookups[j], spd, axis=1, mode="promise_in_bounds"
                )
        return carry

    lax.fori_loop(0, count // 8, look_up, 0, unroll=4)
    mixed = jnp.zeros(q.shape, jnp.float32)
    for j in range(GROUP):
        raw = lax.dot_general(
            q, only_head(k, j), (((1,), (1,)), ((), ())), preferred_element_type=jnp.float32
        )
        parts = []
        for c in range(count // chunk):
            rows = slice(c * chunk, c * chunk + chunk)
            logits = raw[rows] * scale + scores[j, rows, :]
            power = jnp.exp2(logits - jnp.max(logits, -1, keepdims=True))
            probs = power * (1.0 / jnp.sum(power, -1, keepdims=True))
            probs_ref[0, j, rows, :] = probs
            parts.append(probs.astype(jnp.bfloat16))
        mixed = mixed + jnp.dot(
            jnp.concatenate(parts, 0), only_head(v, j), preferred_element_type=jnp.float32
        )
    mixed_ref[...] = mixed.astype(mixed_ref.dtype)


def attend_back_kernel(
    q_ref, k_ref, v_ref, dattn_ref, probs_ref, spd_ref,
    dq_ref, dk_ref, dv_ref, bias_ref, slopes, onehot, corner,
):
    ego, group = pl.program_id(0), pl.program_id(1)
    count, width = q_ref.shape
    scale = (width // GROUP) ** (-0.5)
    buckets = 32
    chunk = 32
    q, k, v, dattn = q_ref[...], k_ref[...], v_ref[...], dattn_ref[...]

    @pl.when(group == 0)
    def _():
        def fill(n, carry):
            row = jnp.broadcast_to(spd_ref[0, pl.ds(n, 1), :], (buckets, count))
            hit = row == lax.broadcasted_iota(jnp.int32, (buckets, count), 0)
            onehot[pl.ds(pl.multiple_of(n * buckets, buckets), buckets), :] = jnp.where(hit, 1.0, 0.0).astype(jnp.bfloat16)
            return carry

        lax.fori_loop(0, count, fill, 0, unroll=8)

    dq = jnp.zeros((count, width), jnp.float32)
    dk = jnp.zeros((count, width), jnp.float32)
    dv = jnp.zeros((count, width), jnp.float32)
    over_rows = (((0,), (0,)), ((), ()))
    for j in range(GROUP):
        dprobs = lax.dot_general(
            dattn, only_head(v, j), (((1,), (1,)), ((), ())), preferred_element_type=jnp.float32
        )
        slope_parts, prob_parts = [], []
        for c in range(count // chunk):
            rows = slice(c * chunk, c * chunk + chunk)
            probs = probs_ref[0, j, rows, :]
            part = dprobs[rows]
            slope = probs * (part - jnp.sum(part * probs, -1, keepdims=True))
            for a in range(count // 128):
                slopes[group * (count // 128) + a, pl.ds(c * chunk * GROUP + j, chunk, stride=GROUP), :] = slope[:, a * 128 : a * 128 + 128]
            slope_parts.append((slope * scale).astype(jnp.bfloat16))
            prob_parts.append(probs.astype(jnp.bfloat16))
        slope_b = jnp.concatenate(slope_parts, 0)
        probs_b = jnp.concatenate(prob_parts, 0)
        dq = dq + jnp.dot(slope_b, only_head(k, j), preferred_element_type=jnp.float32)
        dk = dk + lax.dot_general(slope_b, only_head(q, j), over_rows, preferred_element_type=jnp.float32)
        dv = dv + lax.dot_general(probs_b, only_head(dattn, j), over_rows, preferred_element_type=jnp.float32)
    dq_ref[...] = dq.astype(dq_ref.dtype)
    dk_ref[...] = dk.astype(dk_ref.dtype)
    dv_ref[...] = dv.astype(dv_ref.dtype)

    @pl.when(group == pl.num_programs(1) - 1)
    def _():
        halves = count // 128
        groups = slopes.shape[0] // halves
        corner[...] = jnp.zeros_like(corner)

        def collect(i, carry):
            total = corner[...]
            for n in range(4):
                first = pl.multiple_of((i * 4 + n) * 8 * GROUP, 8 * GROUP)
                rows = pl.ds(first, 8 * GROUP)
                left = jnp.concatenate(
                    [
                        jnp.concatenate([slopes[g * halves + a, rows, :] for a in range(halves)], 1)
                        for g in range(groups)
                    ],
                    0,
                ).astype(jnp.bfloat16)
                first = pl.multiple_of((i * 4 + n) * 8 * buckets, 8 * buckets)
                right = onehot[pl.ds(first, 8 * buckets), :]
                total = total + lax.dot_general(
                    left, right, (((1,), (1,)), ((), ())), preferred_element_type=jnp.float32
                )
            corner[...] = total
            return carry

        lax.fori_loop(0, count // 32, collect, 0)
        shape = corner.shape
        node_row = lax.rem(lax.div(lax.broadcasted_iota(jnp.int32, shape, 0), GROUP), 8)
        node_col = lax.div(lax.broadcasted_iota(jnp.int32, shape, 1), buckets)
        kept = jnp.where(node_row == node_col, corner[...], 0.0)
        tall = []
        for g in range(groups):
            heads = kept[g * 8 * GROUP : g * 8 * GROUP + GROUP]
            for n in range(1, 8):
                heads = heads + kept[(g * 8 + n) * GROUP : (g * 8 + n) * GROUP + GROUP]
            tall.append(heads)
        bias_ref[0] = jnp.concatenate(tall, 0)


def attention_specs(count, width, heads):
    wide = width // heads * GROUP
    groups = heads // GROUP
    column = lambda part: pl.BlockSpec((count, wide), lambda e, g, part=part: (e, part * groups + g))
    probs = pl.BlockSpec((1, GROUP, count, count), lambda e, g: (e, g, 0, 0))
    spd = pl.BlockSpec((1, count, count), lambda e, g: (e, 0, 0))
    return column, probs, spd, groups


def attention_forward(qkv, spd, table):
    egos, count, _ = spd.shape
    heads, width = table.shape[1], qkv.shape[1] // 3
    column, probs, spd_spec, groups = attention_specs(count, width, heads)
    lookup = jnp.pad((table * LOG2E).T, ((0, 0), (0, 128 - table.shape[0])))
    return pl.pallas_call(
        attend_kernel,
        name="attend",
        grid=(egos, groups),
        out_shape=(
            jax.ShapeDtypeStruct((egos * count, width), jnp.bfloat16),
            jax.ShapeDtypeStruct((egos, heads, count, count), jnp.float32),
        ),
        in_specs=[column(0), column(1), column(2), spd_spec, pl.BlockSpec((heads, 128), lambda e, g: (0, 0))],
        out_specs=(column(0), probs),
        scratch_shapes=[pltpu.VMEM((GROUP, count, count), jnp.float32)],
        compiler_params=pltpu.CompilerParams(vmem_limit_bytes=40 * 1024 * 1024),
    )(qkv, qkv, qkv, spd, lookup)


def attention_backward(qkv, dattn, probs, spd, table):
    egos, count, _ = spd.shape
    heads, width = table.shape[1], qkv.shape[1] // 3
    column, probs_spec, spd_spec, groups = attention_specs(count, width, heads)
    flat = jax.ShapeDtypeStruct((egos * count, width), jnp.bfloat16)
    dq, dk, dv, bias = pl.pallas_call(
        attend_back_kernel,
        name="attend_back",
        grid=(egos, groups),
        out_shape=(flat, flat, flat, jax.ShapeDtypeStruct((egos, heads, 256), jnp.float32)),
        in_specs=[column(0), column(1), column(2), column(0), probs_spec, spd_spec],
        out_specs=(column(0), column(0), column(0), pl.BlockSpec((1, heads, 256), lambda e, g: (e, 0, 0))),
        scratch_shapes=[
            pltpu.VMEM((groups * (count // 128), count * GROUP, 128), jnp.float32),
            pltpu.VMEM((count * 32, count), jnp.bfloat16),
            pltpu.VMEM((groups * 8 * GROUP, 256), jnp.float32),
        ],
        compiler_params=pltpu.CompilerParams(vmem_limit_bytes=48 * 1024 * 1024),
    )(qkv, qkv, qkv, dattn, probs, spd)
    return dq, dk, dv, bias.reshape(egos, heads, 8, 32).sum((0, 2)).T


def pick_kernel(rows_ref, table_ref, out_ref, chosen):
    @pl.when(pl.program_id(0) == 0)
    def _():
        shape = chosen.shape
        hit = jnp.broadcast_to(rows_ref[...], shape) == lax.broadcasted_iota(jnp.int32, shape, 1)
        chosen[...] = jnp.where(hit, 1.0, 0.0).astype(jnp.bfloat16)

    out_ref[...] = jnp.dot(chosen[...], table_ref[...], preferred_element_type=jnp.float32).astype(out_ref.dtype)


def pick_rows(requests, node_table):
    rows, width = node_table.shape
    count = requests.size
    return pl.pallas_call(
        pick_kernel,
        name="pick_rows",
        grid=(width // 256,),
        out_shape=jax.ShapeDtypeStruct((count, width), node_table.dtype),
        in_specs=[pl.BlockSpec((count, 1), lambda i: (0, 0)), pl.BlockSpec((rows, 256), lambda i: (0, i))],
        out_specs=pl.BlockSpec((count, 256), lambda i: (0, i)),
        scratch_shapes=[pltpu.VMEM((count, rows), jnp.bfloat16)],
        compiler_params=pltpu.CompilerParams(vmem_limit_bytes=40 * 1024 * 1024),
    )(requests.reshape(count, 1), node_table)


def slot_kernel(member_ref, dx_ref, out_ref):
    slots, tokens = out_ref.shape[1], dx_ref.shape[0]
    shape = (slots, tokens)
    hit = jnp.broadcast_to(member_ref[...], shape) == lax.broadcasted_iota(jnp.int32, shape, 0)
    placed = jnp.where(hit, 1.0, 0.0).astype(jnp.bfloat16)
    dx = dx_ref[...]
    high = dx.astype(jnp.bfloat16)
    low = (dx - high.astype(jnp.float32)).astype(jnp.bfloat16)
    total = jnp.dot(placed, high, preferred_element_type=jnp.float32) + jnp.dot(
        placed, low, preferred_element_type=jnp.float32
    )
    for c in range(out_ref.shape[0]):
        out_ref[c] = total[:, c * 128 : c * 128 + 128].astype(out_ref.dtype)


def slot_gradients(member_slot, dx, slots):
    tokens, width = dx.shape
    return pl.pallas_call(
        slot_kernel,
        name="slot_gradients",
        grid=(width // 256,),
        out_shape=jax.ShapeDtypeStruct((width // 128, slots, 128), jnp.bfloat16),
        in_specs=[pl.BlockSpec((1, tokens), lambda i: (0, 0)), pl.BlockSpec((tokens, 256), lambda i: (0, i))],
        out_specs=pl.BlockSpec((2, slots, 128), lambda i: (i, 0, 0)),
        compiler_params=pltpu.CompilerParams(vmem_limit_bytes=40 * 1024 * 1024),
    )(member_slot.reshape(1, tokens), dx)


def place_kernel(lists_ref, grads_ref, out_ref):
    block, entries = out_ref.shape[0], lists_ref.shape[1]
    base = pl.program_id(0) * block
    total = jnp.zeros(out_ref.shape, jnp.float32)
    step = 1024
    for a in range(0, entries, step):
        shape = (block, step)
        hit = jnp.broadcast_to(lists_ref[:, a : a + step], shape) == lax.broadcasted_iota(jnp.int32, shape, 0) + base
        total = total + jnp.dot(
            jnp.where(hit, 1.0, 0.0).astype(jnp.bfloat16), grads_ref[a : a + step], preferred_element_type=jnp.float32
        )
    out_ref[...] = total.astype(out_ref.dtype)


def place_gradients(lists, grads, rows):
    entries, width = grads.shape
    return pl.pallas_call(
        place_kernel,
        name="place_gradients",
        grid=(rows // 256,),
        out_shape=jax.ShapeDtypeStruct((rows, width), jnp.bfloat16),
        in_specs=[pl.BlockSpec((1, entries), lambda i: (0, 0)), pl.BlockSpec((entries, width), lambda i: (0, 0))],
        out_specs=pl.BlockSpec((256, width), lambda i: (i, 0)),
        compiler_params=pltpu.CompilerParams(vmem_limit_bytes=40 * 1024 * 1024),
    )(lists.reshape(1, entries), grads)


MESH = pl.DeviceIdType.MESH
ORDERS = ((0, 1, 2), (1, 2, 0), (2, 0, 1))
PIECES = 6


def coordinates():
    dp, store = lax.axis_index("dp"), lax.axis_index("store")
    return lax.div(dp, 2), lax.rem(dp, 2), lax.div(store, 4), lax.rem(store, 4)


def peer(y, core, x, z):
    return (y * 2 + core, x * 4 + z)


def along(axis, offset):
    y, core, x, z = coordinates()
    place = [y, x, z]
    place[axis] = lax.rem(place[axis] + offset, 4)
    return peer(place[0], core, place[1], place[2]), place[axis]


def reduce_kernel(
    g_down, g_up, g_out, g_q, g_k, g_v, small,
    o_qkv, o_out, o_up, o_down, o_small,
    own, got, part0, recv0, part1, recv1, part2, recv2, small_core, small_all,
    own_sem, core_send, core_recv, send, recv, sc_send, sc_recv, s_send, s_recv,
):
    y, core, x, z = coordinates()
    here = (y, x, z)
    other = peer(y, 1 - core, x, z)
    everyone = [other] + [along(a, k)[0] for a in range(3) for k in (1, 2, 3)]

    barrier = pltpu.get_barrier_semaphore()
    for device in everyone:
        pl.semaphore_signal(barrier, inc=1, device_id=device, device_id_type=MESH)
    pl.semaphore_wait(barrier, len(everyone))

    sources = [g_down, g_up, g_out, g_q, g_k, g_v]
    outs = [o_down, o_up, o_out] + [o_qkv] * 3
    columns = [0, 0, 0, 0, 1024, 2048]
    sends = []

    local, cross = [], []
    tiny = pltpu.make_async_remote_copy(
        src_ref=small, dst_ref=small_core, send_sem=sc_send, recv_sem=sc_recv,
        device_id=other, device_id_type=MESH)
    tiny.start()
    for j in range(PIECES):
        remote = pltpu.make_async_remote_copy(
            src_ref=sources[j].at[:, 1 - core], dst_ref=got.at[j],
            send_sem=core_send.at[j], recv_sem=core_recv.at[j],
            device_id=other, device_id_type=MESH)
        remote.start()
        cross.append(remote)
        keep = pltpu.make_async_copy(sources[j].at[:, core], own.at[j], own_sem.at[j])
        keep.start()
        local.append(keep)

    tiny.wait()

    def spread_small(axis):
        copies = []
        for k in (1, 2, 3):
            device, _ = along(axis, k)
            copy = pltpu.make_async_remote_copy(
                src_ref=small_all.at[axis, here[axis]], dst_ref=small_all.at[axis, here[axis]],
                send_sem=s_send.at[axis, k - 1], recv_sem=s_recv.at[axis, k - 1],
                device_id=device, device_id_type=MESH)
            copy.start()
            copies.append(copy)
        return copies

    def total_small(axis):
        return (small_all[axis, 0] + small_all[axis, 1]) + (small_all[axis, 2] + small_all[axis, 3])

    small_all[0, here[0]] = small[...] + small_core[...]
    tiny_copies = spread_small(0)

    def scatter(j, stage, part):
        order = ORDERS[j % 3]
        axis = order[stage]
        left = [a for a in (0, 1, 2) if a not in order[:stage]]
        where = left.index(axis)
        landing = (recv0, recv1, recv2)[stage]
        copies = []
        for k in (1, 2, 3):
            device, place = along(axis, k)
            block = (j,) + (slice(None),) * where + (place,)
            copy = pltpu.make_async_remote_copy(
                src_ref=part.at[block], dst_ref=landing.at[j, k - 1],
                send_sem=send.at[stage, j, k - 1], recv_sem=recv.at[stage, j, k - 1],
                device_id=device, device_id_type=MESH)
            copy.start()
            copies.append(copy)
        return copies

    flight = [None] * PIECES
    for j in range(PIECES):
        local[j].wait()
        cross[j].wait_recv()

        def add_cores(i, carry, j=j):
            yy, xx = lax.div(i, 4), lax.rem(i, 4)
            rows = pl.ds(pl.multiple_of(xx * 32, 32), 32)
            total = own[j, yy, rows, :].astype(jnp.float32) + got[j, yy, rows, :].astype(jnp.float32)
            for zz in range(4):
                mine = total[8 * zz : 8 * zz + 8]
                part0[j, yy, xx, zz] = jnp.concatenate([mine[:, :512], mine[:, 512:]], 0).astype(jnp.bfloat16)
            return carry

        lax.fori_loop(0, 16, add_cores, 0)
        flight[j] = scatter(j, 0, part0)

    for copy in tiny_copies:
        copy.wait()
    small_all[1, here[1]] = total_small(0)
    tiny_copies = spread_small(1)

    for j in range(PIECES):
        for copy in flight[j]:
            copy.wait_recv()
        sends += flight[j]
        axis = ORDERS[j % 3][0]

        def add_first(i, carry, j=j, axis=axis):
            a, b = lax.div(i, 4), lax.rem(i, 4)
            block = [a, b]
            block.insert(axis, here[axis])
            total = part0[(j,) + tuple(block)].astype(jnp.float32)
            for k in range(3):
                total = total + recv0[j, k, a, b].astype(jnp.float32)
            part1[j, a, b] = total.astype(jnp.bfloat16)
            return carry

        lax.fori_loop(0, 16, add_first, 0)
        flight[j] = scatter(j, 1, part1)

    for copy in tiny_copies:
        copy.wait()
    small_all[2, here[2]] = total_small(1)
    tiny_copies = spread_small(2)

    for j in range(PIECES):
        for copy in flight[j]:
            copy.wait_recv()
        sends += flight[j]
        order = ORDERS[j % 3]
        where = [a for a in (0, 1, 2) if a != order[0]].index(order[1])

        def add_second(i, carry, j=j, axis=order[1], where=where):
            block = [i]
            block.insert(where, here[axis])
            total = part1[(j,) + tuple(block)].astype(jnp.float32)
            for k in range(3):
                total = total + recv1[j, k, i].astype(jnp.float32)
            part2[j, i] = total.astype(jnp.bfloat16)
            return carry

        lax.fori_loop(0, 4, add_second, 0)
        flight[j] = scatter(j, 2, part2)

    for copy in tiny_copies:
        copy.wait()
    o_small[...] = total_small(2)

    for j in range(PIECES):
        for copy in flight[j]:
            copy.wait_recv()
        sends += flight[j]
        axis = ORDERS[j % 3][2]
        total = part2[j, here[axis]].astype(jnp.float32)
        for k in range(3):
            total = total + recv2[j, k].astype(jnp.float32)
        joined = jnp.concatenate([total[:8], total[8:]], 1).astype(jnp.bfloat16)
        outs[j][:, columns[j] : columns[j] + 1024] = joined

    for copy in cross + sends:
        copy.wait_send()


def reduce_gradients(gradients, small):
    bf16, f32 = jnp.bfloat16, jnp.float32
    hbm = pl.BlockSpec(memory_space=pl.ANY)
    vmem = pl.BlockSpec(memory_space=pltpu.VMEM)
    dma = pltpu.SemaphoreType.DMA
    split = lambda g: g.reshape(4, 2, 128, g.shape[1])
    return pl.pallas_call(
        reduce_kernel,
        name="reduce_gradients",
        out_shape=(
            jax.ShapeDtypeStruct((8, 3072), bf16),
            jax.ShapeDtypeStruct((8, 1024), bf16),
            jax.ShapeDtypeStruct((8, 1024), bf16),
            jax.ShapeDtypeStruct((8, 1024), bf16),
            jax.ShapeDtypeStruct(small.shape, f32),
        ),
        in_specs=[hbm] * PIECES + [vmem],
        out_specs=[vmem] * 5,
        scratch_shapes=[
            pltpu.VMEM((PIECES, 4, 128, 1024), bf16),
            pltpu.VMEM((PIECES, 4, 128, 1024), bf16),
            pltpu.VMEM((PIECES, 4, 4, 4, 16, 512), bf16),
            pltpu.VMEM((PIECES, 3, 4, 4, 16, 512), bf16),
            pltpu.VMEM((PIECES, 4, 4, 16, 512), bf16),
            pltpu.VMEM((PIECES, 3, 4, 16, 512), bf16),
            pltpu.VMEM((PIECES, 4, 16, 512), bf16),
            pltpu.VMEM((PIECES, 3, 16, 512), bf16),
            pltpu.VMEM(small.shape, f32),
            pltpu.VMEM((3, 4) + small.shape, f32),
            dma((PIECES,)),
            dma((PIECES,)),
            dma((PIECES,)),
            dma((3, PIECES, 3)),
            dma((3, PIECES, 3)),
            dma,
            dma,
            dma((3, 3)),
            dma((3, 3)),
        ],
        compiler_params=pltpu.CompilerParams(
            collective_id=0, has_side_effects=True, vmem_limit_bytes=40 * 1024 * 1024
        ),
    )(*[split(g) for g in gradients], small)


def body(
    node_table,
    touched,
    member_slot,
    distances,
    cotangent,
    w_qkv,
    w_out,
    w_up,
    w_down,
    gains,
    bias_table,
):
    bf16, f32 = jnp.bfloat16, jnp.float32
    both = ("dp", "store")
    shard_rows, width = node_table.shape
    owners, cap = touched.shape[1:]
    egos, count = member_slot.shape
    tokens, slots_held = egos * count, owners * cap
    dot = lambda a, b: jnp.dot(a, b, preferred_element_type=f32)
    back = lambda a, b: lax.dot_general(a, b, (((1,), (1,)), ((), ())), preferred_element_type=f32)
    weight = lambda a, b: lax.dot_general(
        a, b, (((0,), (0,)), ((), ())), preferred_element_type=f32
    ).astype(bf16)

    asked = jnp.broadcast_to(touched, (lax.axis_size("dp"), owners, cap)).reshape(-1, cap)
    lists = lax.all_to_all(asked, both, split_axis=0, concat_axis=0, tiled=True)
    requests = lax.dynamic_slice_in_dim(lists, lax.axis_index("dp") * owners, owners, 0)
    picked = pick_rows(requests, node_table)
    slots = lax.all_to_all(
        picked.reshape(owners, cap, width), "store", split_axis=0, concat_axis=0, tiled=True
    ).reshape(slots_held, width)
    x = jnp.take(slots, member_slot.reshape(-1), axis=0, mode="clip").astype(f32)
    dout = cotangent.reshape(tokens, width)

    h1, x_hat, x_rstd = layer_normalize(x, gains[0])
    h1 = h1.astype(bf16)
    qkv = dot(h1, w_qkv).astype(bf16)
    attended, probs = attention_forward(qkv, distances, bias_table)
    y = x + dot(attended, w_out)
    h2, y_hat, y_rstd = layer_normalize(y, gains[1])
    h2 = h2.astype(bf16)
    act, slope = gelu_parts(dot(h2, w_up))
    act = act.astype(bf16)
    layer_out = (y + dot(act, w_down)).astype(bf16)

    du = (back(dout, w_down) * slope).astype(bf16)
    dy, gain_two = layer_normalize_backward(back(du, w_up), gains[1], y_hat, y_rstd)
    dy = dout.astype(f32) + dy
    dyb = dy.astype(bf16)
    dattn = back(dyb, w_out).astype(bf16)
    dq, dk, dv, grad_bias = attention_backward(qkv, dattn, probs, distances, bias_table)
    dh1 = (
        back(dq, w_qkv[:, :width])
        + back(dk, w_qkv[:, width : 2 * width])
        + back(dv, w_qkv[:, 2 * width :])
    )
    dx, gain_one = layer_normalize_backward(dh1, gains[0], x_hat, x_rstd)
    dx = dy + dx

    slot_grads = slot_gradients(member_slot, dx, slots_held)
    returned = lax.all_to_all(
        slot_grads.reshape(-1, cap, 128), both, split_axis=0, concat_axis=0, tiled=True
    )
    gradients = (
        weight(act, dout), weight(h2, du), weight(attended, dyb),
        weight(h1, dq), weight(h1, dk), weight(h1, dv),
    )
    small = jnp.concatenate(
        [gain_one.reshape(8, 128), gain_two.reshape(8, 128), grad_bias.reshape(8, 128)]
    )
    sum_qkv, sum_out, sum_up, sum_down, small = reduce_gradients(gradients, small)
    grad_table = place_gradients(lists, returned.reshape(-1, 128), shard_rows)
    return (
        layer_out.reshape(egos, count, width),
        grad_table,
        sum_qkv,
        sum_out,
        sum_up,
        sum_down,
        small[:16].reshape(2, width),
        small[16:].reshape(32, 32),
    )


def solution(mesh):
    in_specs = (
        P("store", None),
        P(("dp", "store"), None, None),
        P(("dp", "store"), None),
        P(("dp", "store"), None, None),
        P(("dp", "store"), None, None),
        P(),
        P(),
        P(),
        P(),
        P(),
        P(),
    )
    out_specs = (
        P(("dp", "store"), None, None),
        P("store", "dp"),
        P(("dp", "store"), None),
        P(("dp", "store"), None),
        P(("dp", "store"), None),
        P(("dp", "store"), None),
        P(),
        P(),
    )
    return jax.shard_map(body, mesh=mesh, in_specs=in_specs, out_specs=out_specs, check_vma=False)
```

time: 414 us -> 238 us (0.57); the launches traced: 408 us -> 237 us
  matrix products: 156 us -> 41.4 us
  Pallas kernels: 48.5 us -> 126 us
  other arithmetic: 84.5 us -> 7.45 us
  local copies, waits for them, and re-layouts: 75.9 us -> 14.3 us
  waiting for transfers between devices: 0.87 us -> 24.4 us
  blocking collectives: 14.6 us -> 0 us
    dot_general x20 -> x16, matrix products: 156 us -> 41.4 us  [the longest x6 16.1 us: body(): lax.dot_general(a, b, (((0,), (0,)), ((), ())), preferred_element_type=f32)]
    pallas_call x0 -> x5, Pallas kernels: none -> 78.3 us  [the longest x1 37.4 us: attention_backward(): pl.pallas_call(attend_back_kernel, name='attend_back', grid=(egos, groups...]
    scatter-add x2 -> x0, other arithmetic: 37.6 us -> none  [the longest x1 29.5 us: body(): jax.ops.segment_sum(returned.reshape(-1, returned.shape[2]), target, num_...]
    all_to_all x4 -> x3, waiting for transfers between devices: 0.87 us -> 24.4 us  [the longest x1 14.9 us: body(): lax.all_to_all(picked.reshape(owners, cap, width), 'store', split_axis=0,...]
    unnamed x75 -> x53, local copies, waits for them, and re-layouts: 27 us -> 6.18 us
    sub x1 -> x0, other arithmetic: 18.9 us -> none  [attend(): attention_probabilities = jax.nn.softmax(scores, axis=-1)]
    mul x1 -> x0, other arithmetic: 18 us -> none  [attend_back(): attention_probabilities * (dprobs - jnp.sum(dprobs * attention_probabilit...]
    all_gather x1 -> x0, blocking collectives: 14.6 us -> none  [body(): lists = lax.all_gather(requests[0], 'dp', axis=1, tiled=True)]
  transfers between devices with their start and end apart: 4 -> 3, of which waited for: 1 -> 2; matrix products, arithmetic and copies ran while one was open for 16% -> 8% of each run, Pallas kernels for 12% -> 20%
where the time goes in v2:
time: 238 us; the launch traced here: 237 us
  Pallas kernels  126 us (53%)
  matrix products  41.4 us (17%)
  waiting for transfers between devices  24.4 us (10%)
  starting transfers between devices  23 us (10%)
  local copies, waits for them, and re-layouts  14.3 us (6%)
  other arithmetic  7.45 us (3%)
    pallas_call x1, Pallas kernels, reduce_gradients(): pl.pallas_call(reduce_kernel, name='reduce_gradients', out_shape=(jax.Sha...  47.3 us
    pallas_call x1, Pallas kernels, attention_backward(): pl.pallas_call(attend_back_kernel, name='attend_back', grid=(egos, groups...  37.4 us
    pallas_call x1, Pallas kernels, attention_forward(): pl.pallas_call(attend_kernel, name='attend', grid=(egos, groups), out_sha...  25.2 us
    dot_general x6, matrix products, body(): lax.dot_general(a, b, (((0,), (0,)), ((), ())), preferred_element_type=f32)  16.1 us
    dot_general x4, matrix products, body(): dot = lambda a, b: jnp.dot(a, b, preferred_element_type=f32)  15.7 us
    all_to_all x1, waiting for transfers between devices, body(): lax.all_to_all(picked.reshape(owners, cap, width), 'store', split_axis=0,...  14.9 us
    all_to_all x1, starting transfers between devices, body(): lists = lax.all_to_all(asked, both, split_axis=0, concat_axis=0, tiled=True)  11.5 us
    dot_general x6, matrix products, body(): lax.dot_general(a, b, (((1,), (1,)), ((), ())), preferred_element_type=f32)  9.58 us
  transfers between devices with their start and end apart: 3, of which 2 were waited for; matrix products, arithmetic and copies ran while one was open for 8% of the time, Pallas kernels for 20%

profile of v2, /device:TPU:1, one launch (start us, length us, event | category | flops | bytes accessed | tf_op | source)
XLA Modules:
  0.0 237.2 jit_solution(14130984559965259147)
XLA Ops:
  2.1 11.5 %all-to-all-start = ((s32[128,1,40]{2,1,0:T(1,128)}), s32[128,1,40]{2,1,0:T(1,128)S(1)}, u32[]{:S(2)}, u32[]{:S(2)}) async-start(s32[128,1,40]{2,1,0:T(1,128)} %bitcast.1), calls=%async_computation | async-start | bytes 131072 | tf_op jit(solution)/shard_map/all_to_all | solution.py:560
  13.6 9.4 %all-to-all-done = s32[128,1,40]{2,1,0:T(1,128)S(1)} async-done(((s32[128,1,40]{2,1,0:T(1,128)}), s32[128,1,40]{2,1,0:T(1,128)S(1)}, u32[]{:S(2)}, u32[]{:S(2)}) %all-to-all-start) | async-done | bytes 20512 | tf_op jit(solution)/shard_map/all_to_all | solution.py:560
  23.3 2.2 copy-done.3
  25.5 5.2 %pick_rows.1 = bf16[640,1024]{1,0:T(8,128)(2,1)} custom-call(s32[640,1]{1,0:T(8,128)S(1)} %reshape.156.rows_ref, bf16[2048,1024]{1,0:T(8,128)(2,1)S(1)} %copy-done.3), custom_call_target="tpu_custom_call" | custom-call | tf_op jit(solution)/shard_map/pick_rows/pallas_call | solution.py:242
  30.7 4.0 %all-to-all-start.1 = ((bf16[16,40,1024]{2,1,0:T(8,128)(2,1)}), bf16[16,40,1024]{2,1,0:T(8,128)(2,1)S(1)}, u32[]{:S(2)}, u32[]{:S(2)}) async-start(bf16[16,40,1024]{2,1,0:T(8,128)(2,1)} %bitcast.2), calls=%async_computation.1 | async-start | bytes 2621440 | tf_op jit(solution)/shard_map/all_to_all | solution.py:563
  37.8 14.9 %all-to-all-done.1 = bf16[16,40,1024]{2,1,0:T(8,128)(2,1)S(1)} async-done(((bf16[16,40,1024]{2,1,0:T(8,128)(2,1)}), bf16[16,40,1024]{2,1,0:T(8,128)(2,1)S(1)}, u32[]{:S(2)}, u32[]{:S(2)}) %all-to-all-start.1) | async-done | bytes 1310752 | tf_op jit(solution)/shard_map/all_to_all | solution.py:563
  52.7 2.8 %gather_fusion = bf16[512,1024]{1,0:T(8,128)(2,1)} fusion(bf16[640,1024]{1,0:T(8,128)(2,1)S(1)} %bitcast.56, s32[1024]{0:T(1024)S(1)} %pad_clamp_fusion), kind=kCustom, calls=%fused_computation | custom fusion | bytes 2099200 | tf_op jit(solution)/shard_map/jit(_take)/gather | solution.py:566
  57.0 1.6 fusion.12
  58.7 6.7 %convolution_convert_fusion.q_ref.k_ref.v_ref = bf16[512,3072]{1,0:T(8,128)(2,1)S(1)} fusion(bf16[1024,3072]{1,0:T(8,128)(2,1)} %param.16, bf16[512,1024]{1,0:T(8,128)(2,1)S(1)} %copy-done.9, f32[1024]{0:T(1024)S(1)} %bitcast.64, f32[512]{0:T(512)S(1)} %add_rsqrt_fusion.1, f32[512]{0:T(512)S(1)} %broadcast_multiply_fusion.5), kind=kOutput, calls=%fused_computation.1 | convolution fusion | flops 3225419776 | bytes 10493952 | tf_op jit(solution)/shard_map/dot_general | solution.py:553
  65.5 25.2 %attend.1 = (bf16[512,1024]{1,0:T(8,128)(2,1)S(1)}, f32[2,32,256,256]{3,2,1,0:T(8,128)}) custom-call(bf16[512,3072]{1,0:T(8,128)(2,1)S(1)} %convolution_convert_fusion.q_ref.k_ref.v_ref, bf16[512,3072]{1,0:T(8,128)(2,1)S(1)} %convolution_convert_fusion.q_ref.k_ref.v_ref, bf16[512,3072]{1,0:T(8,128)(2,1)S(1)} %convolution_convert_fusion.q_ref.k_ref.v_ref, ...), custom_call_target="tpu_custom_call" | custom-call | tf_op jit(solution)/shard_map/attend/pallas_call | solution.py:192
  92.5 2.7 %multiply_convert_fusion = (bf16[512,1024]{1,0:T(8,128)(2,1)}, f32[512,1024]{1,0:T(8,128)S(1)}) fusion(bf16[1024,1024]{1,0:T(8,128)(2,1)S(1)} %copy-done, f32[512,1024]{1,0:T(8,128)S(1)} %get-tuple-element.39, f32[1024]{0:T(1024)S(1)} %bitcast.60, f32[512]{0:T(512)S(1)} %add_rsqrt_fusion, f32[512]{0:T(512)S(1)} %broadcast_multiply_fusion.4), kind=kOutput, calls=%fused_computation.36 | convolution fusion | flops 1078460416 | bytes 7348224 | tf_op jit(solution)/shard_map/dot_general | solution.py:553
  95.2 2.0 fusion.18
  97.2 1.8 multiply_reduce_fusion
  101.1 37.4 %attend_back.1 = (bf16[512,1024]{1,0:T(8,128)(2,1)S(1)}, bf16[512,1024]{1,0:T(8,128)(2,1)S(1)}, bf16[512,1024]{1,0:T(8,128)(2,1)S(1)}, f32[2,32,256]{2,1,0:T(8,128)S(1)}) custom-call(bf16[512,3072]{1,0:T(8,128)(2,1)} %copy-done.2, bf16[512,3072]{1,0:T(8,128)(2,1)} %copy-done.2, bf16[512,3072]{1,0:T(8,128)(2,1)} %copy-done.2, ...), custom_call_target="tpu_custom_call" | custom-call | tf_op jit(solution)/shard_map/attend_back/pallas_call | solution.py:212
  142.6 2.9 %convolution_convert_fusion.2 = bf16[1024,1024]{1,0:T(8,128)(2,1)} fusion(bf16[512,1024]{1,0:T(8,128)(2,1)S(1)} %get-tuple-element.22, bf16[512,1024]{1,0:T(8,128)(2,1)S(1)} %copy-done.9, f32[1024]{0:T(1024)S(1)} %bitcast.66, f32[512]{0:T(512)S(1)} %add_rsqrt_fusion.1, f32[512]{0:T(512)S(1)} %broadcast_multiply_fusion.5), kind=kOutput, calls=%fused_computation.42 | convolution fusion | flops 1077411840 | bytes 4202496 | tf_op jit(solution)/shard_map/dot_general | solution.py:555
  145.4 2.8 %convolution_convert_fusion.1 = bf16[1024,1024]{1,0:T(8,128)(2,1)} fusion(bf16[512,1024]{1,0:T(8,128)(2,1)S(1)} %get-tuple-element.23, bf16[512,1024]{1,0:T(8,128)(2,1)S(1)} %copy-done.9, f32[1024]{0:T(1024)S(1)} %bitcast.67, f32[512]{0:T(512)S(1)} %add_rsqrt_fusion.1, f32[512]{0:T(512)S(1)} %broadcast_multiply_fusion.5), kind=kOutput, calls=%fused_computation.41 | convolution fusion | flops 1077411840 | bytes 4202496 | tf_op jit(solution)/shard_map/dot_general | solution.py:555
  148.2 2.0 fusion.11
  151.0 3.2 %slot_gradients.1 = bf16[8,640,128]{2,1,0:T(8,128)(2,1)} custom-call(s32[1,512]{1,0:T(1,128)S(1)} %bitcast.55, f32[512,1024]{1,0:T(8,128)S(1)} %fusion.10.dx_ref), custom_call_target="tpu_custom_call" | custom-call | tf_op jit(solution)/shard_map/slot_gradients/pallas_call | solution.py:271
  154.1 7.5 %all-to-all-start.2 = ((bf16[128,40,128]{2,1,0:T(8,128)(2,1)}), bf16[128,40,128]{2,1,0:T(8,128)(2,1)S(1)}, u32[]{:S(2)}, u32[]{:S(2)}) async-start(bf16[128,40,128]{2,1,0:T(8,128)(2,1)} %bitcast.9), calls=%async_computation.2 | async-start | bytes 2621440 | tf_op jit(solution)/shard_map/all_to_all | solution.py:595
  161.6 4.2 %convolution_convert_fusion.6 = bf16[1024,1024]{1,0:T(8,128)(2,1)} fusion(bf16[512,1024]{1,0:T(8,128)(2,1)} %get-tuple-element.40, bf16[512,1024]{1,0:T(8,128)(2,1)} %bitcast.57), kind=kOutput, calls=%fused_computation.46 | convolution fusion | flops 1074790400 | bytes 4194304 | tf_op jit(solution)/shard_map/dot_general | solution.py:555
  167.6 3.3 %convolution_convert_fusion.4 = bf16[1024,1024]{1,0:T(8,128)(2,1)S(1)} fusion(bf16[512,1024]{1,0:T(8,128)(2,1)} %copy-done.8, f32[512,1024]{1,0:T(8,128)} %copy-done.12), kind=kOutput, calls=%fused_computation.44 | convolution fusion | flops 1075314688 | bytes 5242880 | tf_op jit(solution)/shard_map/dot_general | solution.py:555
  173.9 47.3 %reduce_gradients.1 = (bf16[8,3072]{1,0:T(8,128)(2,1)S(1)}, bf16[8,1024]{1,0:T(8,128)(2,1)S(1)}, bf16[8,1024]{1,0:T(8,128)(2,1)S(1)}, bf16[8,1024]{1,0:T(8,128)(2,1)S(1)}, f32[24,128]{1,0:T(8,128)S(1)}) custom-call(bf16[4,2,128,1024]{3,2,1,0:T(8,128)(2,1)S(1)} %bitcast.52, bf16[4,2,128,1024]{3,2,1,0:T(8,128)(2,1)S(1)} %bitcast.54, ...), custom_call_target="tpu_custom_call" | custom-call | tf_op jit(solution)/shard_map/reduce_gradients/pallas_call | solution.py:495
  222.5 4.9 %add_convert_fusion = bf16[512,1024]{1,0:T(8,128)(2,1)} fusion(f32[512,1024]{1,0:T(8,128)} %copy-done.10, bf16[512,1024]{1,0:T(8,128)(2,1)} %get-tuple-element.40, bf16[1024,1024]{1,0:T(8,128)(2,1)} %param.19), kind=kOutput, calls=%fused_computation.35 | convolution fusion | flops 1074790400 | bytes 6291456 | tf_op jit(solution)/shard_map/dot_general | solution.py:553
  227.4 7.4 %place_gradients.1 = bf16[2048,128]{1,0:T(8,128)(2,1)} custom-call(s32[1,5120]{1,0:T(1,128)S(1)} %reshape.131.lists_ref, bf16[5120,128]{1,0:T(8,128)(2,1)S(1)} %bitcast.48), custom_call_target="tpu_custom_call" | custom-call | tf_op jit(solution)/shard_map/place_gradients/pallas_call | solution.py:298
  (91 shorter events, 23.3 us)
Async XLA Ops:
  0.6 91.8 %copy-start = (bf16[1024,1024]{1,0:T(8,128)(2,1)S(1)}, bf16[1024,1024]{1,0:T(8,128)(2,1)}, u32[]{:S(2)}) copy-start(bf16[1024,1024]{1,0:T(8,128)(2,1)} %param.18) | copy-start | bytes 6291460
  2.1 21.0 %all-to-all-start = ((s32[128,1,40]{2,1,0:T(1,128)}), s32[128,1,40]{2,1,0:T(1,128)S(1)}, u32[]{:S(2)}, u32[]{:S(2)}) async-start(s32[128,1,40]{2,1,0:T(1,128)} %bitcast.1), calls=%async_computation | async-start | bytes 131072 | tf_op jit(solution)/shard_map/all_to_all | solution.py:560
  23.3 2.2 copy-start.3
  30.7 4.0 %copy-start.16 = (s32[2,256]{1,0:T(2,128)S(1)}, s32[2,256]{1,0:T(2,128)}, u32[]{:S(2)}) copy-start(s32[2,256]{1,0:T(2,128)} %param.13) | copy-start | bytes 6148
  30.7 4.0 %copy-start.14 = (f32[32,32]{1,0:T(8,128)S(1)}, f32[32,32]{1,0:T(8,128)}, u32[]{:S(2)}) copy-start(f32[32,32]{1,0:T(8,128)} %param.21) | copy-start | bytes 12292
  30.7 4.2 %copy-start.15 = (f32[2,1024]{1,0:T(2,128)S(1)}, f32[2,1024]{1,0:T(2,128)}, u32[]{:S(2)}) copy-start(f32[2,1024]{1,0:T(2,128)} %param.20) | copy-start | bytes 24580
  30.7 22.0 %all-to-all-start.1 = ((bf16[16,40,1024]{2,1,0:T(8,128)(2,1)}), bf16[16,40,1024]{2,1,0:T(8,128)(2,1)S(1)}, u32[]{:S(2)}, u32[]{:S(2)}) async-start(bf16[16,40,1024]{2,1,0:T(8,128)(2,1)} %bitcast.2), calls=%async_computation.1 | async-start | bytes 2621440 | tf_op jit(solution)/shard_map/all_to_all | solution.py:563
  55.5 3.2 %copy-start.9 = (bf16[512,1024]{1,0:T(8,128)(2,1)S(1)}, bf16[512,1024]{1,0:T(8,128)(2,1)}, u32[]{:S(2)}) copy-start(bf16[512,1024]{1,0:T(8,128)(2,1)} %gather_fusion) | copy-start | bytes 3145732
  58.7 6.8 %copy-start.7 = (s32[2,256,256]{2,1,0:T(8,128)S(1)}, s32[2,256,256]{2,1,0:T(8,128)}, u32[]{:S(2)}) copy-start(s32[2,256,256]{2,1,0:T(8,128)} %spd_ref.3) | copy-start | bytes 1572868
  65.5 25.2 %copy-start.2 = (bf16[512,3072]{1,0:T(8,128)(2,1)}, bf16[512,3072]{1,0:T(8,128)(2,1)S(1)}, u32[]{:S(2)}) copy-start(bf16[512,3072]{1,0:T(8,128)(2,1)S(1)} %convolution_convert_fusion.q_ref.k_ref.v_ref) | copy-start | bytes 9437188
  65.5 25.2 %copy-start.17 = (bf16[1024,1024]{1,0:T(8,128)(2,1)S(1)}, bf16[1024,1024]{1,0:T(8,128)(2,1)}, u32[]{:S(2)}) copy-start(bf16[1024,1024]{1,0:T(8,128)(2,1)} %param.17) | copy-start | bytes 6291460
  92.1 6.9 %copy-start.10 = (f32[512,1024]{1,0:T(8,128)}, f32[512,1024]{1,0:T(8,128)S(1)}, u32[]{:S(2)}) copy-start(f32[512,1024]{1,0:T(8,128)S(1)} %get-tuple-element.39) | copy-start | bytes 6291460
  92.4 2.7 %copy-start.13 = (bf16[2,256,1024]{2,1,0:T(8,128)(2,1)S(1)}, bf16[2,256,1024]{2,1,0:T(8,128)(2,1)}, u32[]{:S(2)}) copy-start(bf16[2,256,1024]{2,1,0:T(8,128)(2,1)} %param.15) | copy-start | bytes 3145732
  92.5 2.7 %copy-start.18 = (bf16[1024,1024]{1,0:T(8,128)(2,1)S(1)}, bf16[1024,1024]{1,0:T(8,128)(2,1)}, u32[]{:S(2)}) copy-start(bf16[1024,1024]{1,0:T(8,128)(2,1)} %param.19) | copy-start | bytes 6291460
  97.1 1.8 copy-start.19
  99.7 50.5 %copy-start.12 = (f32[512,1024]{1,0:T(8,128)}, f32[512,1024]{1,0:T(8,128)S(1)}, u32[]{:S(2)}) copy-start(f32[512,1024]{1,0:T(8,128)S(1)} %multiply_add_fusion) | copy-start | bytes 6291460
  99.7 38.7 %slice-start = ((s8[6291456]{0:T(1024)(128)(4,1)}), s8[4194304]{0:T(1024)(128)(4,1)S(1)}, s32[]{:S(2)}) async-start(s8[6291456]{0:T(1024)(128)(4,1)} %bitcast.76), calls=%async_computation.3 | async-start | bytes 8388608
  101.1 37.4 %slice-start.1 = ((s8[6291456]{0:T(1024)(128)(4,1)}), s8[2097152]{0:T(1024)(128)(4,1)S(1)}, s32[]{:S(2)}) async-start(s8[6291456]{0:T(1024)(128)(4,1)} %bitcast.76), calls=%async_computation.4 | async-start | bytes 4194304
  154.1 73.3 %all-to-all-start.2 = ((bf16[128,40,128]{2,1,0:T(8,128)(2,1)}), bf16[128,40,128]{2,1,0:T(8,128)(2,1)S(1)}, u32[]{:S(2)}, u32[]{:S(2)}) async-start(bf16[128,40,128]{2,1,0:T(8,128)(2,1)} %bitcast.9), calls=%async_computation.2 | async-start | bytes 2621440 | tf_op jit(solution)/shard_map/all_to_all | solution.py:595
  167.6 3.4 %copy-start.11 = (f32[512,1024]{1,0:T(8,128)S(1)}, f32[512,1024]{1,0:T(8,128)}, u32[]{:S(2)}) copy-start(f32[512,1024]{1,0:T(8,128)} %copy-done.10) | copy-start | bytes 6291460
  167.6 3.4 %copy-start.20 = (bf16[512,1024]{1,0:T(8,128)(2,1)S(1)}, bf16[512,1024]{1,0:T(8,128)(2,1)}, u32[]{:S(2)}) copy-start(bf16[512,1024]{1,0:T(8,128)(2,1)} %copy-done.19) | copy-start | bytes 3145732
  171.0 2.2 copy-start.5
  171.0 2.8 %copy-start.6 = (bf16[1024,1024]{1,0:T(8,128)(2,1)S(1)}, bf16[1024,1024]{1,0:T(8,128)(2,1)}, u32[]{:S(2)}) copy-start(bf16[1024,1024]{1,0:T(8,128)(2,1)} %convolution_convert_fusion.6) | copy-start | bytes 6291460
  222.5 14.7 %copy-start.1 = (bf16[1024,1024]{1,0:T(8,128)(2,1)S(1)}, bf16[1024,1024]{1,0:T(8,128)(2,1)}, u32[]{:S(2)}) copy-start(bf16[1024,1024]{1,0:T(8,128)(2,1)} %param.18) | copy-start | bytes 6291460
  (2 other events, 2.9 us)

commit v3 on v2

--- a/solution.py
+++ b/solution.py
@@ -7,6 +7,11 @@
 from jax.experimental.pallas import tpu as pltpu
 from jax.sharding import PartitionSpec as P
 
+MESH = pl.DeviceIdType.MESH
+ORDERS = ((0, 1, 2), (1, 2, 0), (2, 0, 1))
+PIECES = 6
+
+
 EPS = 1e-05
 ROOT_HALF = 1.0 / math.sqrt(2.0)
 ROOT_TWO_PI = 1.0 / math.sqrt(2.0 * math.pi)
@@ -33,6 +38,177 @@
     return (upper * normal_cdf, activation_slope)
 
 
+LISTED = 128
+
+
+def fetch_kernel(
+    touched, members, table_hbm, spd, lookup,
+    x_out, lists_out, bias_hbm,
+    table, asked, lists, chosen, outgoing, slots, bias,
+    table_sem, ask_send, ask_recv, list_send, list_recv, row_send, row_recv, bias_sem,
+):
+    dp, store = lax.axis_index("dp"), lax.axis_index("store")
+    shards, groups = asked.shape[0], lists.shape[0]
+    rows, width = table.shape
+    cap = slots.shape[1] // 2
+    half = width // 2
+    egos, heads, count, _ = bias.shape
+    turn = lambda here, k, size: lax.rem(here + k, size)
+    owners = [(dp, turn(store, k, shards)) for k in range(shards)]
+    copies_of_shard = [(turn(dp, k, groups), store) for k in range(groups)]
+
+    load = pltpu.make_async_copy(table_hbm, table, table_sem)
+    load.start()
+    barrier = pltpu.get_barrier_semaphore()
+    for device in owners[1:] + copies_of_shard[1:]:
+        pl.semaphore_signal(barrier, inc=1, device_id=device, device_id_type=MESH)
+    pl.semaphore_wait(barrier, shards + groups - 2)
+
+    requests = []
+    for k in range(1, shards):
+        copy = pltpu.make_async_remote_copy(
+            src_ref=touched.at[owners[k][1]], dst_ref=asked.at[store],
+            send_sem=ask_send.at[k], recv_sem=ask_recv.at[k],
+            device_id=owners[k], device_id_type=MESH)
+        copy.start()
+        requests.append(copy)
+    asked[store] = touched[store]
+
+    bias_copies = []
+
+    def look_up(ego, first, many):
+        def step(n, carry):
+            at = pl.ds(pl.multiple_of(n * 8, 8), 8)
+            for a in range(0, count, 128):
+                distance = spd[ego, at, a : a + 128]
+                for h in range(first, first + many):
+                    row = jnp.broadcast_to(lookup[h : h + 1, :], (8, 128))
+                    bias[ego, h, at, a : a + 128] = jnp.take_along_axis(
+                        row, distance, axis=1, mode="promise_in_bounds"
+                    )
+            return carry
+
+        lax.fori_loop(0, count // 8, step, 0, unroll=2)
+        part = pl.ds(first, many)
+        copy = pltpu.make_async_copy(
+            bias.at[ego, part], bias_hbm.at[ego, part], bias_sem.at[len(bias_copies)])
+        copy.start()
+        bias_copies.append(copy)
+
+    look_up(0, 0, 8)
+    for copy in requests:
+        copy.wait_recv()
+    shared = []
+    for k in range(1, groups):
+        copy = pltpu.make_async_remote_copy(
+            src_ref=asked, dst_ref=lists.at[dp],
+            send_sem=list_send.at[k], recv_sem=list_recv.at[k],
+            device_id=copies_of_shard[k], device_id_type=MESH)
+        copy.start()
+        shared.append(copy)
+    lists[dp] = asked[...]
+
+    order = list(range(1, shards)) + [0]
+    turned = jnp.concatenate(
+        [asked[owners[k][1]] for k in order] + [jnp.full((LISTED - shards, LISTED), -1, jnp.int32)], 0
+    ).T
+    for p in range(0, shards, 2):
+        pair = jnp.concatenate([turned[:cap, p : p + 1], turned[:cap, p + 1 : p + 2]], 0)
+        shape = (2 * cap, rows)
+        hit = jnp.broadcast_to(pair, shape) == lax.broadcasted_iota(jnp.int32, shape, 1)
+        chosen[p * cap : (p + 2) * cap, :] = jnp.where(hit, 1.0, 0.0).astype(jnp.bfloat16)
+    load.wait()
+    sent = []
+    for first in range(0, shards, 4):
+        picks = chosen[first * cap : (first + 4) * cap, :]
+        left = jnp.dot(picks, table[:, :half], preferred_element_type=jnp.float32)
+        right = jnp.dot(picks, table[:, half:], preferred_element_type=jnp.float32)
+        for i in range(4):
+            k = order[first + i]
+            mine = slice(i * cap, i * cap + cap)
+            block = jnp.concatenate([left[mine], right[mine]], 0).astype(jnp.bfloat16)
+            if k == 0:
+                slots[store] = block
+                continue
+            outgoing[k] = block
+            copy = pltpu.make_async_remote_copy(
+                src_ref=outgoing.at[k], dst_ref=slots.at[store],
+                send_sem=row_send.at[k], recv_sem=row_recv.at[k],
+                device_id=owners[k], device_id_type=MESH)
+            copy.start()
+            sent.append(copy)
+
+    look_up(0, 8, heads - 8)
+    look_up(1, 0, heads)
+    for copy in sent:
+        copy.wait_recv()
+    tokens = members.shape[0]
+    shape = (tokens, shards * 2 * cap)
+    held = slots[...].reshape(shards * 2 * cap, half)
+    places = lax.broadcasted_iota(jnp.int32, shape, 1)
+    for part in range(2):
+        hit = jnp.broadcast_to(members[...] + part * cap, shape) == places
+        x_out[:, part * half : part * half + half] = jnp.dot(
+            jnp.where(hit, 1.0, 0.0).astype(jnp.bfloat16), held, preferred_element_type=jnp.float32
+        ).astype(x_out.dtype)
+    for copy in shared:
+        copy.wait()
+    lists_out[...] = lists[...]
+    for copy in requests + sent:
+        copy.wait_send()
+    for copy in bias_copies:
+        copy.wait()
+
+
+def fetch(node_table, touched, member_slot, spd, table):
+    bf16, f32, i32 = jnp.bfloat16, jnp.float32, jnp.int32
+    _, shards, cap = touched.shape
+    groups = lax.axis_size("dp")
+    egos, count = member_slot.shape
+    heads = table.shape[1]
+    rows, width = node_table.shape
+    lookup = jnp.pad((table * LOG2E).T, ((0, 0), (0, 128 - table.shape[0])))
+    listed = jnp.pad(
+        touched.reshape(shards, 1, cap), ((0, 0), (0, 0), (0, LISTED - cap)), constant_values=-1
+    )
+    members = (member_slot + cap * lax.div(member_slot, cap)).reshape(egos * count, 1)
+    hbm = pl.BlockSpec(memory_space=pl.ANY)
+    vmem = pl.BlockSpec(memory_space=pltpu.VMEM)
+    dma = pltpu.SemaphoreType.DMA
+    x, lists, bias = pl.pallas_call(
+        fetch_kernel,
+        name="fetch",
+        out_shape=(
+            jax.ShapeDtypeStruct((egos * count, width), bf16),
+            jax.ShapeDtypeStruct((groups, shards, 1, LISTED), i32),
+            jax.ShapeDtypeStruct((egos, heads, count, count), f32),
+        ),
+        in_specs=[vmem, vmem, hbm, vmem, vmem],
+        out_specs=(vmem, vmem, hbm),
+        scratch_shapes=[
+            pltpu.VMEM((rows, width), bf16),
+            pltpu.VMEM((shards, 1, LISTED), i32),
+            pltpu.VMEM((groups, shards, 1, LISTED), i32),
+            pltpu.VMEM((shards * cap, rows), bf16),
+            pltpu.VMEM((shards, 2 * cap, width // 2), bf16),
+            pltpu.VMEM((shards, 2 * cap, width // 2), bf16),
+            pltpu.VMEM((egos, heads, count, count), f32),
+            dma,
+            dma((shards,)),
+            dma((shards,)),
+            dma((groups,)),
+            dma((groups,)),
+            dma((shards,)),
+            dma((shards,)),
+            dma((3,)),
+        ],
+        compiler_params=pltpu.CompilerParams(
+            collective_id=1, has_side_effects=True, vmem_limit_bytes=48 * 1024 * 1024
+        ),
+    )(listed, members, node_table, spd, lookup)
+    return x, lists[:, :, 0, :cap].reshape(-1), bias
+
+
 GROUP = 8
 LOG2E = math.log2(math.e)
 
@@ -46,28 +222,12 @@
     return jnp.where(head_mask(value.shape[0], value.shape[1], head), value, jnp.zeros((), value.dtype))
 
 
-def attend_kernel(q_ref, k_ref, v_ref, spd_ref, table_ref, mixed_ref, probs_ref, scores):
-    group = pl.program_id(1)
+def attend_kernel(q_ref, k_ref, v_ref, bias_ref, mixed_ref, probs_ref):
     count = q_ref.shape[0]
     head_width = q_ref.shape[1] // GROUP
     scale = LOG2E * head_width ** (-0.5)
     chunk = 32
     q, k, v = q_ref[...], k_ref[...], v_ref[...]
-    lookups = [
-        jnp.broadcast_to(table_ref[pl.ds(group * GROUP + j, 1), :], (8, 128)) for j in range(GROUP)
-    ]
-
-    def look_up(n, carry):
-        rows = pl.ds(pl.multiple_of(n * 8, 8), 8)
-        for a in range(0, count, 128):
-            spd = spd_ref[0, rows, a : a + 128]
-            for j in range(GROUP):
-                scores[j, rows, a : a + 128] = jnp.take_along_axis(
-                    lookups[j], spd, axis=1, mode="promise_in_bounds"
-                )
-        return carry
-
-    lax.fori_loop(0, count // 8, look_up, 0, unroll=4)
     mixed = jnp.zeros(q.shape, jnp.float32)
     for j in range(GROUP):
         raw = lax.dot_general(
@@ -76,7 +236,7 @@
         parts = []
         for c in range(count // chunk):
             rows = slice(c * chunk, c * chunk + chunk)
-            logits = raw[rows] * scale + scores[j, rows, :]
+            logits = raw[rows] * scale + bias_ref[0, j, rows, :]
             power = jnp.exp2(logits - jnp.max(logits, -1, keepdims=True))
             probs = power * (1.0 / jnp.sum(power, -1, keepdims=True))
             probs_ref[0, j, rows, :] = probs
@@ -184,11 +344,10 @@
     return column, probs, spd, groups
 
 
-def attention_forward(qkv, spd, table):
-    egos, count, _ = spd.shape
-    heads, width = table.shape[1], qkv.shape[1] // 3
-    column, probs, spd_spec, groups = attention_specs(count, width, heads)
-    lookup = jnp.pad((table * LOG2E).T, ((0, 0), (0, 128 - table.shape[0])))
+def attention_forward(qkv, bias):
+    egos, heads, count, _ = bias.shape
+    width = qkv.shape[1] // 3
+    column, probs, _, groups = attention_specs(count, width, heads)
     return pl.pallas_call(
         attend_kernel,
         name="attend",
@@ -197,16 +356,15 @@
             jax.ShapeDtypeStruct((egos * count, width), jnp.bfloat16),
             jax.ShapeDtypeStruct((egos, heads, count, count), jnp.float32),
         ),
-        in_specs=[column(0), column(1), column(2), spd_spec, pl.BlockSpec((heads, 128), lambda e, g: (0, 0))],
+        in_specs=[column(0), column(1), column(2), probs],
         out_specs=(column(0), probs),
-        scratch_shapes=[pltpu.VMEM((GROUP, count, count), jnp.float32)],
         compiler_params=pltpu.CompilerParams(vmem_limit_bytes=40 * 1024 * 1024),
-    )(qkv, qkv, qkv, spd, lookup)
-
-
-def attention_backward(qkv, dattn, probs, spd, table):
-    egos, count, _ = spd.shape
-    heads, width = table.shape[1], qkv.shape[1] // 3
+    )(qkv, qkv, qkv, bias)
+
+
+def attention_backward(qkv, dattn, probs, spd):
+    egos, heads, count, _ = probs.shape
+    width = qkv.shape[1] // 3
     column, probs_spec, spd_spec, groups = attention_specs(count, width, heads)
     flat = jax.ShapeDtypeStruct((egos * count, width), jnp.bfloat16)
     dq, dk, dv, bias = pl.pallas_call(
@@ -226,31 +384,6 @@
     return dq, dk, dv, bias.reshape(egos, heads, 8, 32).sum((0, 2)).T
 
 
-def pick_kernel(rows_ref, table_ref, out_ref, chosen):
-    @pl.when(pl.program_id(0) == 0)
-    def _():
-        shape = chosen.shape
-        hit = jnp.broadcast_to(rows_ref[...], shape) == lax.broadcasted_iota(jnp.int32, shape, 1)
-        chosen[...] = jnp.where(hit, 1.0, 0.0).astype(jnp.bfloat16)
-
-    out_ref[...] = jnp.dot(chosen[...], table_ref[...], preferred_element_type=jnp.float32).astype(out_ref.dtype)
-
-
-def pick_rows(requests, node_table):
-    rows, width = node_table.shape
-    count = requests.size
-    return pl.pallas_call(
-        pick_kernel,
-        name="pick_rows",
-        grid=(width // 256,),
-        out_shape=jax.ShapeDtypeStruct((count, width), node_table.dtype),
-        in_specs=[pl.BlockSpec((count, 1), lambda i: (0, 0)), pl.BlockSpec((rows, 256), lambda i: (0, i))],
-        out_specs=pl.BlockSpec((count, 256), lambda i: (0, i)),
-        scratch_shapes=[pltpu.VMEM((count, rows), jnp.bfloat16)],
-        compiler_params=pltpu.CompilerParams(vmem_limit_bytes=40 * 1024 * 1024),
-    )(requests.reshape(count, 1), node_table)
-
-
 def slot_kernel(member_ref, dx_ref, out_ref):
     slots, tokens = out_ref.shape[1], dx_ref.shape[0]
     shape = (slots, tokens)
@@ -304,11 +437,6 @@
         out_specs=pl.BlockSpec((256, width), lambda i: (i, 0)),
         compiler_params=pltpu.CompilerParams(vmem_limit_bytes=40 * 1024 * 1024),
     )(lists.reshape(1, entries), grads)
-
-
-MESH = pl.DeviceIdType.MESH
-ORDERS = ((0, 1, 2), (1, 2, 0), (2, 0, 1))
-PIECES = 6
 
 
 def coordinates():
@@ -556,20 +684,14 @@
         a, b, (((0,), (0,)), ((), ())), preferred_element_type=f32
     ).astype(bf16)
 
-    asked = jnp.broadcast_to(touched, (lax.axis_size("dp"), owners, cap)).reshape(-1, cap)
-    lists = lax.all_to_all(asked, both, split_axis=0, concat_axis=0, tiled=True)
-    requests = lax.dynamic_slice_in_dim(lists, lax.axis_index("dp") * owners, owners, 0)
-    picked = pick_rows(requests, node_table)
-    slots = lax.all_to_all(
-        picked.reshape(owners, cap, width), "store", split_axis=0, concat_axis=0, tiled=True
-    ).reshape(slots_held, width)
-    x = jnp.take(slots, member_slot.reshape(-1), axis=0, mode="clip").astype(f32)
+    x, lists, bias = fetch(node_table, touched, member_slot, distances, bias_table)
+    x = x.astype(f32)
     dout = cotangent.reshape(tokens, width)
 
     h1, x_hat, x_rstd = layer_normalize(x, gains[0])
     h1 = h1.astype(bf16)
     qkv = dot(h1, w_qkv).astype(bf16)
-    attended, probs = attention_forward(qkv, distances, bias_table)
+    attended, probs = attention_forward(qkv, bias)
     y = x + dot(attended, w_out)
     h2, y_hat, y_rstd = layer_normalize(y, gains[1])
     h2 = h2.astype(bf16)
@@ -582,7 +704,7 @@
     dy = dout.astype(f32) + dy
     dyb = dy.astype(bf16)
     dattn = back(dyb, w_out).astype(bf16)
-    dq, dk, dv, grad_bias = attention_backward(qkv, dattn, probs, distances, bias_table)
+    dq, dk, dv, grad_bias = attention_backward(qkv, dattn, probs, distances)
     dh1 = (
         back(dq, w_qkv[:, :width])
         + back(dk, w_qkv[:, width : 2 * width])

time: 238 us -> 214 us (0.90)
  waiting for transfers between devices: 24.4 us -> 0.01 us
  Pallas kernels: 126 us -> 148 us
  starting transfers between devices: 23 us -> 10.3 us
  other arithmetic: 7.45 us -> 3.4 us
  matrix products: 41.4 us -> 37.8 us
    pallas_call x1, Pallas kernels: 5.24 us -> 32.3 us  [fetch(): pl.pallas_call(fetch_kernel, name='fetch', out_shape=(jax.ShapeDtypeStruc...]
    all_to_all x2 -> x0, waiting for transfers between devices: 24.4 us -> none  [the longest x1 14.9 us: body(): lax.all_to_all(picked.reshape(owners, cap, width), 'store', split_axis=0,...]
    all_to_all x2 -> x0, starting transfers between devices: 15.5 us -> none  [the longest x1 11.5 us: body(): lists = lax.all_to_all(asked, both, split_axis=0, concat_axis=0, tiled=True)]
    pallas_call x1, Pallas kernels: 25.2 us -> 19.7 us  [attention_forward(): pl.pallas_call(attend_kernel, name='attend', grid=(egos, groups), out_sha...]
    dot_general x4, matrix products: 15.7 us -> 12.6 us  [body(): dot = lambda a, b: jnp.dot(a, b, preferred_element_type=f32)]
    all_to_all x1, starting transfers between devices: 7.46 us -> 10.3 us  [body(): lax.all_to_all(slot_grads.reshape(-1, cap, 128), both, split_axis=0, conc...]
    gather x1 -> x0, local copies, waits for them, and re-layouts: 2.77 us -> none  [body(): jnp.take(slots, member_slot.reshape(-1), axis=0, mode='clip').astype(f32)]
    unnamed x53 -> x68, local copies, waits for them, and re-layouts: 6.18 us -> 8.83 us
  transfers between devices with their start and end apart: 3 -> 1, of which waited for: 2 -> 0; matrix products, arithmetic and copies ran while one was open for 8% -> 10% of each run, Pallas kernels for 20% -> 22%
where the time goes in v3:
time: 214 us; the launch traced here: 213 us
  Pallas kernels  148 us (69%)
  matrix products  37.8 us (18%)
  local copies, waits for them, and re-layouts  12.1 us (6%)
  starting transfers between devices  10.3 us (5%)
  other arithmetic  3.4 us (2%)
    pallas_call x1, Pallas kernels, reduce_gradients(): pl.pallas_call(reduce_kernel, name='reduce_gradients', out_shape=(jax.Sha...  47.3 us
    pallas_call x1, Pallas kernels, attention_backward(): pl.pallas_call(attend_back_kernel, name='attend_back', grid=(egos, groups...  37.1 us
    pallas_call x1, Pallas kernels, fetch(): pl.pallas_call(fetch_kernel, name='fetch', out_shape=(jax.ShapeDtypeStruc...  32.3 us
    pallas_call x1, Pallas kernels, attention_forward(): pl.pallas_call(attend_kernel, name='attend', grid=(egos, groups), out_sha...  19.7 us
    dot_general x6, matrix products, body(): lax.dot_general(a, b, (((0,), (0,)), ((), ())), preferred_element_type=f32)  15.6 us
    dot_general x4, matrix products, body(): dot = lambda a, b: jnp.dot(a, b, preferred_element_type=f32)  12.6 us
    all_to_all x1, starting transfers between devices, body(): lax.all_to_all(slot_grads.reshape(-1, cap, 128), both, split_axis=0, conc...  10.3 us
    dot_general x6, matrix products, body(): lax.dot_general(a, b, (((1,), (1,)), ((), ())), preferred_element_type=f32)  9.64 us
  transfers between devices with their start and end apart: 1, of which 0 were waited for; matrix products, arithmetic and copies ran while one was open for 10% of the time, Pallas kernels for 22%

profile of v3, /device:TPU:1, one launch (start us, length us, event | category | flops | bytes accessed | tf_op | source)
XLA Modules:
  0.0 213.1 jit_solution(5152972277855568338)
XLA Ops:
  4.6 2.2 %copy-done.3 = bf16[2048,1024]{1,0:T(8,128)(2,1)S(1)} copy-done((bf16[2048,1024]{1,0:T(8,128)(2,1)S(1)}, bf16[2048,1024]{1,0:T(8,128)(2,1)}, u32[]{:S(2)}) %copy-start.3) | copy-done | bytes 4194328
  7.9 32.3 %fetch.1 = (bf16[512,1024]{1,0:T(8,128)(2,1)S(1)}, s32[8,16,1,128]{3,2,1,0:T(1,128)S(1)}, f32[2,32,256,256]{3,2,1,0:T(8,128)}) custom-call(s32[16,1,128]{2,1,0:T(1,128)S(1)} %pad.8.touched, s32[512,1]{1,0:T(8,128)S(1)} %bitcast.54, bf16[2048,1024]{1,0:T(8,128)(2,1)S(1)} %copy-done.3, s32[2,256,256]{2,1,0:T(8,128)S(1)} %copy-done.7, f32[32,128]{1,0:T(8,128)S(1)} %pad.9.lookup), custom_call_target="tpu_custom_call" | custom-call | tf_op jit(solution)/shard_map/fetch/pallas_call | solution.py:178
  40.9 4.0 %convolution_convert_fusion.q_ref.k_ref.v_ref = bf16[512,3072]{1,0:T(8,128)(2,1)S(1)} fusion(bf16[1024,3072]{1,0:T(8,128)(2,1)S(1)} %copy-done.21, bf16[512,1024]{1,0:T(8,128)(2,1)S(1)} %get-tuple-element.22, f32[1024]{0:T(1024)S(1)} %bitcast.63, f32[512]{0:T(512)S(1)} %add_rsqrt_fusion.1, f32[512]{0:T(512)S(1)} %broadcast_multiply_fusion.5), kind=kOutput, calls=%fused_computation | convolution fusion | flops 3225419776 | bytes 10493952 | tf_op jit(solution)/shard_map/dot_general | solution.py:681
  44.9 19.7 %attend.1 = (bf16[512,1024]{1,0:T(8,128)(2,1)S(1)}, f32[2,32,256,256]{3,2,1,0:T(8,128)}) custom-call(bf16[512,3072]{1,0:T(8,128)(2,1)S(1)} %convolution_convert_fusion.q_ref.k_ref.v_ref, bf16[512,3072]{1,0:T(8,128)(2,1)S(1)} %convolution_convert_fusion.q_ref.k_ref.v_ref, bf16[512,3072]{1,0:T(8,128)(2,1)S(1)} %convolution_convert_fusion.q_ref.k_ref.v_ref, ...), custom_call_target="tpu_custom_call" | custom-call | tf_op jit(solution)/shard_map/attend/pallas_call | solution.py:351
  64.6 1.3 fusion.35
  66.4 2.7 %multiply_convert_fusion = (bf16[512,1024]{1,0:T(8,128)(2,1)}, f32[512,1024]{1,0:T(8,128)S(1)}) fusion(bf16[1024,1024]{1,0:T(8,128)(2,1)S(1)} %copy-done, f32[512,1024]{1,0:T(8,128)S(1)} %get-tuple-element.45, f32[1024]{0:T(1024)S(1)} %bitcast.59, f32[512]{0:T(512)S(1)} %add_rsqrt_fusion, f32[512]{0:T(512)S(1)} %broadcast_multiply_fusion.4), kind=kOutput, calls=%fused_computation.35 | convolution fusion | flops 1078460416 | bytes 7348224 | tf_op jit(solution)/shard_map/dot_general | solution.py:681
  69.1 2.1 %fusion.18 = bf16[512,1024]{1,0:T(8,128)(2,1)S(1)} fusion(f32[512,1024]{1,0:T(8,128)S(1)} %get-tuple-element.47, bf16[512,1024]{1,0:T(8,128)(2,1)S(1)} %bitcast.56, bf16[1024,1024]{1,0:T(8,128)(2,1)S(1)} %copy-done.23), kind=kOutput, calls=%fused_computation.23 | convolution fusion | flops 1078984704 | bytes 6291456 | tf_op jit(solution)/shard_map/dot_general | solution.py:682
  71.2 1.7 multiply_reduce_fusion
  73.8 1.3 convolution_convert_fusion.7.dattn_ref
  75.2 37.1 %attend_back.1 = (bf16[512,1024]{1,0:T(8,128)(2,1)S(1)}, bf16[512,1024]{1,0:T(8,128)(2,1)S(1)}, bf16[512,1024]{1,0:T(8,128)(2,1)S(1)}, f32[2,32,256]{2,1,0:T(8,128)S(1)}) custom-call(bf16[512,3072]{1,0:T(8,128)(2,1)} %copy-done.2, bf16[512,3072]{1,0:T(8,128)(2,1)} %copy-done.2, bf16[512,3072]{1,0:T(8,128)(2,1)} %copy-done.2, ...), custom_call_target="tpu_custom_call" | custom-call | tf_op jit(solution)/shard_map/attend_back/pallas_call | solution.py:370
  112.3 1.3 fusion.23
  113.6 1.3 fusion.21
  114.9 1.9 fusion.11
  117.6 3.2 %slot_gradients.1 = bf16[8,640,128]{2,1,0:T(8,128)(2,1)} custom-call(s32[1,512]{1,0:T(1,128)S(1)} %bitcast.55, f32[512,1024]{1,0:T(8,128)S(1)} %fusion.10.dx_ref), custom_call_target="tpu_custom_call" | custom-call | tf_op jit(solution)/shard_map/slot_gradients/pallas_call | solution.py:404
  120.8 10.3 %all-to-all-start = ((bf16[128,40,128]{2,1,0:T(8,128)(2,1)}), bf16[128,40,128]{2,1,0:T(8,128)(2,1)}, u32[]{:S(2)}, u32[]{:S(2)}) async-start(bf16[128,40,128]{2,1,0:T(8,128)(2,1)} %bitcast.6), calls=%async_computation | async-start | bytes 2621440 | tf_op jit(solution)/shard_map/all_to_all | solution.py:717
  131.1 2.8 %convolution_convert_fusion.3 = bf16[1024,1024]{1,0:T(8,128)(2,1)S(1)} fusion(bf16[512,1024]{1,0:T(8,128)(2,1)} %copy-done.15, bf16[512,1024]{1,0:T(8,128)(2,1)S(1)} %get-tuple-element.22, f32[1024]{0:T(1024)S(1)} %bitcast.66, f32[512]{0:T(512)S(1)} %add_rsqrt_fusion.1, f32[512]{0:T(512)S(1)} %broadcast_multiply_fusion.5), kind=kOutput, calls=%fused_computation.42 | convolution fusion | flops 1077411840 | bytes 4202496 | tf_op jit(solution)/shard_map/dot_general | solution.py:683
  133.9 2.8 %convolution_convert_fusion.2 = bf16[1024,1024]{1,0:T(8,128)(2,1)} fusion(bf16[512,1024]{1,0:T(8,128)(2,1)S(1)} %copy-done.14, bf16[512,1024]{1,0:T(8,128)(2,1)S(1)} %get-tuple-element.22, f32[1024]{0:T(1024)S(1)} %bitcast.67, f32[512]{0:T(512)S(1)} %add_rsqrt_fusion.1, f32[512]{0:T(512)S(1)} %broadcast_multiply_fusion.5), kind=kOutput, calls=%fused_computation.41 | convolution fusion | flops 1077411840 | bytes 4202496 | tf_op jit(solution)/shard_map/dot_general | solution.py:683
  136.8 2.8 %convolution_convert_fusion.1 = bf16[1024,1024]{1,0:T(8,128)(2,1)} fusion(bf16[512,1024]{1,0:T(8,128)(2,1)S(1)} %copy-done.12, bf16[512,1024]{1,0:T(8,128)(2,1)S(1)} %get-tuple-element.22, f32[1024]{0:T(1024)S(1)} %bitcast.68, f32[512]{0:T(512)S(1)} %add_rsqrt_fusion.1, f32[512]{0:T(512)S(1)} %broadcast_multiply_fusion.5), kind=kOutput, calls=%fused_computation.40 | convolution fusion | flops 1077411840 | bytes 4202496 | tf_op jit(solution)/shard_map/dot_general | solution.py:683
  139.6 2.6 %convolution_convert_fusion.6 = bf16[1024,1024]{1,0:T(8,128)(2,1)} fusion(bf16[512,1024]{1,0:T(8,128)(2,1)S(1)} %copy-done.26, bf16[512,1024]{1,0:T(8,128)(2,1)S(1)} %bitcast.57), kind=kOutput, calls=%fused_computation.45 | convolution fusion | flops 1074790400 | bytes 4194304 | tf_op jit(solution)/shard_map/dot_general | solution.py:683
  142.6 3.0 %convolution_convert_fusion.4 = bf16[1024,1024]{1,0:T(8,128)(2,1)S(1)} fusion(bf16[512,1024]{1,0:T(8,128)(2,1)S(1)} %copy-done.10, f32[512,1024]{1,0:T(8,128)} %copy-done.18), kind=kOutput, calls=%fused_computation.43 | convolution fusion | flops 1075314688 | bytes 5242880 | tf_op jit(solution)/shard_map/dot_general | solution.py:683
  145.6 1.5 convolution_convert_fusion.5
  148.5 47.3 %reduce_gradients.1 = (bf16[8,3072]{1,0:T(8,128)(2,1)S(1)}, bf16[8,1024]{1,0:T(8,128)(2,1)S(1)}, bf16[8,1024]{1,0:T(8,128)(2,1)S(1)}, bf16[8,1024]{1,0:T(8,128)(2,1)S(1)}, f32[24,128]{1,0:T(8,128)S(1)}) custom-call(bf16[4,2,128,1024]{3,2,1,0:T(8,128)(2,1)S(1)} %bitcast.51, bf16[4,2,128,1024]{3,2,1,0:T(8,128)(2,1)S(1)} %bitcast.53, ...), custom_call_target="tpu_custom_call" | custom-call | tf_op jit(solution)/shard_map/reduce_gradients/pallas_call | solution.py:623
  197.4 4.6 %add_convert_fusion = bf16[512,1024]{1,0:T(8,128)(2,1)} fusion(f32[512,1024]{1,0:T(8,128)} %copy-done.16, bf16[512,1024]{1,0:T(8,128)(2,1)S(1)} %copy-done.27, bf16[1024,1024]{1,0:T(8,128)(2,1)} %param.19), kind=kOutput, calls=%fused_computation.34 | convolution fusion | flops 1074790400 | bytes 6291456 | tf_op jit(solution)/shard_map/dot_general | solution.py:681
  202.0 8.7 %place_gradients.1 = bf16[2048,128]{1,0:T(8,128)(2,1)} custom-call(s32[1,5120]{1,0:T(1,128)S(1)} %reshape_reshape_squeeze.3.lists_ref, bf16[5120,128]{1,0:T(8,128)(2,1)} %bitcast.7.grads_ref), custom_call_target="tpu_custom_call" | custom-call | tf_op jit(solution)/shard_map/place_gradients/pallas_call | solution.py:431
  (98 shorter events, 13.3 us)
Async XLA Ops:
  0.6 65.7 %copy-start = (bf16[1024,1024]{1,0:T(8,128)(2,1)S(1)}, bf16[1024,1024]{1,0:T(8,128)(2,1)}, u32[]{:S(2)}) copy-start(bf16[1024,1024]{1,0:T(8,128)(2,1)} %param.18) | copy-start | bytes 6291460
  4.6 2.2 %copy-start.3 = (bf16[2048,1024]{1,0:T(8,128)(2,1)S(1)}, bf16[2048,1024]{1,0:T(8,128)(2,1)}, u32[]{:S(2)}) copy-start(bf16[2048,1024]{1,0:T(8,128)(2,1)} %table_hbm.1) | copy-start | bytes 12582916
  7.9 33.0 %copy-start.21 = (bf16[1024,3072]{1,0:T(8,128)(2,1)S(1)}, bf16[1024,3072]{1,0:T(8,128)(2,1)}, u32[]{:S(2)}) copy-start(bf16[1024,3072]{1,0:T(8,128)(2,1)} %param.16) | copy-start | bytes 18874372
  44.8 19.8 %copy-start.2 = (bf16[512,3072]{1,0:T(8,128)(2,1)}, bf16[512,3072]{1,0:T(8,128)(2,1)S(1)}, u32[]{:S(2)}) copy-start(bf16[512,3072]{1,0:T(8,128)(2,1)S(1)} %convolution_convert_fusion.q_ref.k_ref.v_ref) | copy-start | bytes 9437188
  44.9 19.8 %copy-start.22 = (bf16[1024,1024]{1,0:T(8,128)(2,1)S(1)}, bf16[1024,1024]{1,0:T(8,128)(2,1)}, u32[]{:S(2)}) copy-start(bf16[1024,1024]{1,0:T(8,128)(2,1)} %param.17) | copy-start | bytes 6291460
  66.0 7.0 %copy-start.16 = (f32[512,1024]{1,0:T(8,128)}, f32[512,1024]{1,0:T(8,128)S(1)}, u32[]{:S(2)}) copy-start(f32[512,1024]{1,0:T(8,128)S(1)} %get-tuple-element.45) | copy-start | bytes 6291460
  66.3 2.7 %copy-start.19 = (bf16[2,256,1024]{2,1,0:T(8,128)(2,1)S(1)}, bf16[2,256,1024]{2,1,0:T(8,128)(2,1)}, u32[]{:S(2)}) copy-start(bf16[2,256,1024]{2,1,0:T(8,128)(2,1)} %param.15) | copy-start | bytes 3145732
  66.4 2.7 %copy-start.23 = (bf16[1024,1024]{1,0:T(8,128)(2,1)S(1)}, bf16[1024,1024]{1,0:T(8,128)(2,1)}, u32[]{:S(2)}) copy-start(bf16[1024,1024]{1,0:T(8,128)(2,1)} %param.19) | copy-start | bytes 6291460
  73.8 43.1 %copy-start.18 = (f32[512,1024]{1,0:T(8,128)}, f32[512,1024]{1,0:T(8,128)S(1)}, u32[]{:S(2)}) copy-start(f32[512,1024]{1,0:T(8,128)S(1)} %multiply_add_fusion) | copy-start | bytes 6291460
  73.8 38.5 %slice-start = ((s8[6291456]{0:T(1024)(128)(4,1)}), s8[4194304]{0:T(1024)(128)(4,1)S(1)}, s32[]{:S(2)}) async-start(s8[6291456]{0:T(1024)(128)(4,1)} %bitcast.74), calls=%async_computation.1 | async-start | bytes 8388608
  75.2 37.1 %slice-start.1 = ((s8[6291456]{0:T(1024)(128)(4,1)}), s8[2097152]{0:T(1024)(128)(4,1)S(1)}, s32[]{:S(2)}) async-start(s8[6291456]{0:T(1024)(128)(4,1)} %bitcast.74), calls=%async_computation.2 | async-start | bytes 4194304
  112.3 2.6 %copy-start.11 = (bf16[512,1024]{1,0:T(8,128)(2,1)}, bf16[512,1024]{1,0:T(8,128)(2,1)S(1)}, u32[]{:S(2)}) copy-start(bf16[512,1024]{1,0:T(8,128)(2,1)S(1)} %get-tuple-element.29) | copy-start | bytes 3145732
  120.8 81.2 %all-to-all-start = ((bf16[128,40,128]{2,1,0:T(8,128)(2,1)}), bf16[128,40,128]{2,1,0:T(8,128)(2,1)}, u32[]{:S(2)}, u32[]{:S(2)}) async-start(bf16[128,40,128]{2,1,0:T(8,128)(2,1)} %bitcast.6), calls=%async_computation | async-start | bytes 2621440 | tf_op jit(solution)/shard_map/all_to_all | solution.py:717
  131.1 2.8 %copy-start.14 = (bf16[512,1024]{1,0:T(8,128)(2,1)S(1)}, bf16[512,1024]{1,0:T(8,128)(2,1)}, u32[]{:S(2)}) copy-start(bf16[512,1024]{1,0:T(8,128)(2,1)} %copy-done.13) | copy-start | bytes 3145732
  133.9 2.9 %copy-start.12 = (bf16[512,1024]{1,0:T(8,128)(2,1)S(1)}, bf16[512,1024]{1,0:T(8,128)(2,1)}, u32[]{:S(2)}) copy-start(bf16[512,1024]{1,0:T(8,128)(2,1)} %copy-done.11) | copy-start | bytes 3145732
  136.8 2.8 %copy-start.20 = (bf16[2,256,1024]{2,1,0:T(8,128)(2,1)S(1)}, bf16[2,256,1024]{2,1,0:T(8,128)(2,1)}, u32[]{:S(2)}) copy-start(bf16[2,256,1024]{2,1,0:T(8,128)(2,1)} %param.15) | copy-start | bytes 3145732
  136.8 2.8 %copy-start.26 = (bf16[512,1024]{1,0:T(8,128)(2,1)S(1)}, bf16[512,1024]{1,0:T(8,128)(2,1)}, u32[]{:S(2)}) copy-start(bf16[512,1024]{1,0:T(8,128)(2,1)} %get-tuple-element.46) | copy-start | bytes 3145732
  139.6 2.9 %copy-start.10 = (bf16[512,1024]{1,0:T(8,128)(2,1)S(1)}, bf16[512,1024]{1,0:T(8,128)(2,1)}, u32[]{:S(2)}) copy-start(bf16[512,1024]{1,0:T(8,128)(2,1)} %copy-done.9) | copy-start | bytes 3145732
  142.5 3.1 %copy-start.17 = (f32[512,1024]{1,0:T(8,128)S(1)}, f32[512,1024]{1,0:T(8,128)}, u32[]{:S(2)}) copy-start(f32[512,1024]{1,0:T(8,128)} %copy-done.16) | copy-start | bytes 6291460
  142.5 3.1 %copy-start.25 = (bf16[512,1024]{1,0:T(8,128)(2,1)S(1)}, bf16[512,1024]{1,0:T(8,128)(2,1)}, u32[]{:S(2)}) copy-start(bf16[512,1024]{1,0:T(8,128)(2,1)} %copy-done.24) | copy-start | bytes 3145732
  145.6 2.2 %copy-start.5 = (bf16[1024,1024]{1,0:T(8,128)(2,1)S(1)}, bf16[1024,1024]{1,0:T(8,128)(2,1)}, u32[]{:S(2)}) copy-start(bf16[1024,1024]{1,0:T(8,128)(2,1)} %convolution_convert_fusion.1) | copy-start | bytes 6291460
  145.6 2.8 %copy-start.6 = (bf16[1024,1024]{1,0:T(8,128)(2,1)S(1)}, bf16[1024,1024]{1,0:T(8,128)(2,1)}, u32[]{:S(2)}) copy-start(bf16[1024,1024]{1,0:T(8,128)(2,1)} %convolution_convert_fusion.6) | copy-start | bytes 6291460
  148.5 48.9 %copy-start.27 = (bf16[512,1024]{1,0:T(8,128)(2,1)S(1)}, bf16[512,1024]{1,0:T(8,128)(2,1)}, u32[]{:S(2)}) copy-start(bf16[512,1024]{1,0:T(8,128)(2,1)} %get-tuple-element.46) | copy-start | bytes 3145732
  197.4 15.7 %copy-start.1 = (bf16[1024,1024]{1,0:T(8,128)(2,1)S(1)}, bf16[1024,1024]{1,0:T(8,128)(2,1)}, u32[]{:S(2)}) copy-start(bf16[1024,1024]{1,0:T(8,128)(2,1)} %param.18) | copy-start | bytes 6291460
  (7 other events, 9.9 us)

commit v4 on v3

--- a/solution.py
+++ b/solution.py
@@ -7,11 +7,6 @@
 from jax.experimental.pallas import tpu as pltpu
 from jax.sharding import PartitionSpec as P
 
-MESH = pl.DeviceIdType.MESH
-ORDERS = ((0, 1, 2), (1, 2, 0), (2, 0, 1))
-PIECES = 6
-
-
 EPS = 1e-05
 ROOT_HALF = 1.0 / math.sqrt(2.0)
 ROOT_TWO_PI = 1.0 / math.sqrt(2.0 * math.pi)
@@ -36,6 +31,147 @@
     normal_cdf = 0.5 * (1.0 + jax.scipy.special.erf(upper * ROOT_HALF))
     activation_slope = normal_cdf + upper * jnp.exp(-0.5 * upper * upper) * ROOT_TWO_PI
     return (upper * normal_cdf, activation_slope)
+
+
+MESH = pl.DeviceIdType.MESH
+ORDERS = ((0, 1, 2), (1, 2, 0), (2, 0, 1))
+PIECES = 3
+
+
+def coordinates():
+    dp, store = lax.axis_index("dp"), lax.axis_index("store")
+    return lax.div(dp, 2), lax.rem(dp, 2), lax.div(store, 4), lax.rem(store, 4)
+
+
+def peer(y, core, x, z):
+    return (y * 2 + core, x * 4 + z)
+
+
+def along(axis, offset):
+    y, core, x, z = coordinates()
+    place = [y, x, z]
+    place[axis] = lax.rem(place[axis] + offset, 4)
+    return peer(place[0], core, place[1], place[2]), place[axis]
+
+
+def other_core():
+    y, core, x, z = coordinates()
+    return peer(y, 1 - core, x, z)
+
+
+def meet(devices):
+    barrier = pltpu.get_barrier_semaphore()
+    for device in devices:
+        pl.semaphore_signal(barrier, inc=1, device_id=device, device_id_type=MESH)
+    pl.semaphore_wait(barrier, len(devices))
+
+
+class Reducer:
+    SCRATCH = (
+        (PIECES, 4, 128, 1024), (PIECES, 4, 4, 4, 16, 512), (PIECES, 3, 4, 4, 16, 512), (PIECES, 4, 4, 16, 512),
+        (PIECES, 3, 4, 16, 512), (PIECES, 4, 16, 512), (PIECES, 3, 16, 512),
+    )
+    SEMAPHORES = ((PIECES,), (PIECES,), (3, PIECES, 3), (3, PIECES, 3))
+
+    @classmethod
+    def scratch(cls):
+        return [pltpu.VMEM(s, jnp.bfloat16) for s in cls.SCRATCH] + [
+            pltpu.SemaphoreType.DMA(s) for s in cls.SEMAPHORES
+        ]
+
+    def __init__(self, refs, given, kept):
+        (self.got, part0, recv0, part1, recv1, part2, recv2,
+         self.core_send, self.core_recv, self.send, self.recv) = refs
+        self.parts, self.landing = (part0, part1, part2), (recv0, recv1, recv2)
+        self.given, self.kept = given, kept
+        y, self.core, x, z = coordinates()
+        self.here = (y, x, z)
+
+    def cross(self, j):
+        return pltpu.make_async_remote_copy(
+            src_ref=self.given(j), dst_ref=self.got.at[j],
+            send_sem=self.core_send.at[j], recv_sem=self.core_recv.at[j],
+            device_id=other_core(), device_id_type=MESH)
+
+    def spread(self, stage, j):
+        order = ORDERS[j]
+        axis = order[stage]
+        where = [a for a in (0, 1, 2) if a not in order[:stage]].index(axis)
+        copies = []
+        for k in (1, 2, 3):
+            device, place = along(axis, k)
+            block = (j,) + (slice(None),) * where + (place,)
+            copies.append(
+                pltpu.make_async_remote_copy(
+                    src_ref=self.parts[stage].at[block], dst_ref=self.landing[stage].at[j, k - 1],
+                    send_sem=self.send.at[stage, j, k - 1], recv_sem=self.recv.at[stage, j, k - 1],
+                    device_id=device, device_id_type=MESH)
+            )
+        return copies
+
+    def launch(self, stage, j):
+        for copy in self.spread(stage, j):
+            copy.start()
+
+    def add_cores(self, j):
+        self.cross(j).wait_recv()
+
+        def step(i, carry):
+            yy, xx = lax.div(i, 4), lax.rem(i, 4)
+            rows = pl.ds(pl.multiple_of(xx * 32, 32), 32)
+            total = self.kept(j, yy, rows).astype(jnp.float32) + self.got[j, yy, rows, :].astype(jnp.float32)
+            for zz in range(4):
+                mine = total[8 * zz : 8 * zz + 8]
+                self.parts[0][j, yy, xx, zz] = jnp.concatenate(
+                    [mine[:, :512], mine[:, 512:]], 0
+                ).astype(jnp.bfloat16)
+            return carry
+
+        lax.fori_loop(0, 16, step, 0)
+        self.launch(0, j)
+
+    def total(self, stage, j, block):
+        order = ORDERS[j]
+        where = [a for a in (0, 1, 2) if a not in order[:stage]].index(order[stage])
+        index = list(block)
+        index.insert(where, self.here[order[stage]])
+        total = self.parts[stage][(j,) + tuple(index)].astype(jnp.float32)
+        for k in range(3):
+            total = total + self.landing[stage][(j, k) + tuple(block)].astype(jnp.float32)
+        return total
+
+    def add(self, stage, j):
+        for copy in self.spread(stage, j):
+            copy.wait_recv()
+
+        def step(i, carry):
+            block = (lax.div(i, 4), lax.rem(i, 4)) if stage == 0 else (i,)
+            self.parts[stage + 1][(j,) + block] = self.total(stage, j, block).astype(jnp.bfloat16)
+            return carry
+
+        lax.fori_loop(0, 16 if stage == 0 else 4, step, 0)
+        self.launch(stage + 1, j)
+
+    def result(self, j):
+        for copy in self.spread(2, j):
+            copy.wait_recv()
+        total = self.total(2, j, ())
+        return jnp.concatenate([total[:8], total[8:]], 1).astype(jnp.bfloat16)
+
+    def close(self):
+        for j in range(PIECES):
+            self.cross(j).wait_send()
+            for stage in range(3):
+                for copy in self.spread(stage, j):
+                    copy.wait_send()
+
+
+def torus_peers():
+    return [other_core()] + [along(a, k)[0] for a in range(3) for k in (1, 2, 3)]
+
+
+def halves(g):
+    return g.reshape(4, 2, 128, g.shape[1])
 
 
 LISTED = 128
@@ -206,7 +342,7 @@
             collective_id=1, has_side_effects=True, vmem_limit_bytes=48 * 1024 * 1024
         ),
     )(listed, members, node_table, spd, lookup)
-    return x, lists[:, :, 0, :cap].reshape(-1), bias
+    return x, lists[:, :, 0, :], bias
 
 
 GROUP = 8
@@ -248,10 +384,48 @@
 
 
 def attend_back_kernel(
-    q_ref, k_ref, v_ref, dattn_ref, probs_ref, spd_ref,
-    dq_ref, dk_ref, dv_ref, bias_ref, slopes, onehot, corner,
+    q_ref, k_ref, v_ref, dattn_ref, probs_ref, spd_ref, g_down, g_up, g_out,
+    dq_ref, dk_ref, dv_ref, bias_ref, o_down, o_up, o_out, slopes, onehot, corner, own, own_sem, *rest,
 ):
     ego, group = pl.program_id(0), pl.program_id(1)
+    step = ego * pl.num_programs(1) + group
+    sources, sums = (g_down, g_up, g_out), (o_down, o_up, o_out)
+    core = lax.rem(lax.axis_index("dp"), 2)
+    reducer = Reducer(
+        rest, lambda j: sources[j].at[:, 1 - core], lambda j, yy, rows: own[j, yy, rows, :]
+    )
+    keep = lambda j: pltpu.make_async_copy(sources[j].at[:, core], own.at[j], own_sem.at[j])
+
+    @pl.when(step == 0)
+    def _():
+        for j in range(PIECES):
+            keep(j).start()
+        meet(torus_peers())
+        for j in range(PIECES):
+            reducer.cross(j).start()
+
+    @pl.when(step == 1)
+    def _():
+        for j in range(PIECES):
+            keep(j).wait()
+            reducer.add_cores(j)
+
+    @pl.when(step == 4)
+    def _():
+        for j in range(PIECES):
+            reducer.add(0, j)
+
+    @pl.when(step == 5)
+    def _():
+        for j in range(PIECES):
+            reducer.add(1, j)
+
+    @pl.when(step == 6)
+    def _():
+        for j in range(PIECES):
+            sums[j][...] = reducer.result(j)
+        reducer.close()
+
     count, width = q_ref.shape
     scale = (width // GROUP) ** (-0.5)
     buckets = 32
@@ -362,26 +536,35 @@
     )(qkv, qkv, qkv, bias)
 
 
-def attention_backward(qkv, dattn, probs, spd):
+def attention_backward(qkv, dattn, probs, spd, gradients):
     egos, heads, count, _ = probs.shape
     width = qkv.shape[1] // 3
     column, probs_spec, spd_spec, groups = attention_specs(count, width, heads)
     flat = jax.ShapeDtypeStruct((egos * count, width), jnp.bfloat16)
-    dq, dk, dv, bias = pl.pallas_call(
+    summed = jax.ShapeDtypeStruct((8, 1024), jnp.bfloat16)
+    whole = pl.BlockSpec((8, 1024), lambda e, g: (0, 0))
+    dq, dk, dv, bias, *sums = pl.pallas_call(
         attend_back_kernel,
         name="attend_back",
         grid=(egos, groups),
-        out_shape=(flat, flat, flat, jax.ShapeDtypeStruct((egos, heads, 256), jnp.float32)),
-        in_specs=[column(0), column(1), column(2), column(0), probs_spec, spd_spec],
-        out_specs=(column(0), column(0), column(0), pl.BlockSpec((1, heads, 256), lambda e, g: (e, 0, 0))),
+        out_shape=(flat, flat, flat, jax.ShapeDtypeStruct((egos, heads, 256), jnp.float32)) + (summed,) * 3,
+        in_specs=[column(0), column(1), column(2), column(0), probs_spec, spd_spec]
+        + [pl.BlockSpec(memory_space=pl.ANY)] * PIECES,
+        out_specs=(column(0), column(0), column(0), pl.BlockSpec((1, heads, 256), lambda e, g: (e, 0, 0)))
+        + (whole,) * 3,
         scratch_shapes=[
             pltpu.VMEM((groups * (count // 128), count * GROUP, 128), jnp.float32),
             pltpu.VMEM((count * 32, count), jnp.bfloat16),
             pltpu.VMEM((groups * 8 * GROUP, 256), jnp.float32),
-        ],
-        compiler_params=pltpu.CompilerParams(vmem_limit_bytes=48 * 1024 * 1024),
-    )(qkv, qkv, qkv, dattn, probs, spd)
-    return dq, dk, dv, bias.reshape(egos, heads, 8, 32).sum((0, 2)).T
+            pltpu.VMEM((PIECES, 4, 128, 1024), jnp.bfloat16),
+            pltpu.SemaphoreType.DMA((PIECES,)),
+        ]
+        + Reducer.scratch(),
+        compiler_params=pltpu.CompilerParams(
+            collective_id=2, has_side_effects=True, vmem_limit_bytes=48 * 1024 * 1024
+        ),
+    )(qkv, qkv, qkv, dattn, probs, spd, *[halves(g) for g in gradients])
+    return dq, dk, dv, bias.reshape(egos, heads, 8, 32).sum((0, 2)).T, sums
 
 
 def slot_kernel(member_ref, dx_ref, out_ref):
@@ -412,96 +595,44 @@
     )(member_slot.reshape(1, tokens), dx)
 
 
-def place_kernel(lists_ref, grads_ref, out_ref):
-    block, entries = out_ref.shape[0], lists_ref.shape[1]
-    base = pl.program_id(0) * block
-    total = jnp.zeros(out_ref.shape, jnp.float32)
-    step = 1024
-    for a in range(0, entries, step):
-        shape = (block, step)
-        hit = jnp.broadcast_to(lists_ref[:, a : a + step], shape) == lax.broadcasted_iota(jnp.int32, shape, 0) + base
-        total = total + jnp.dot(
-            jnp.where(hit, 1.0, 0.0).astype(jnp.bfloat16), grads_ref[a : a + step], preferred_element_type=jnp.float32
-        )
-    out_ref[...] = total.astype(out_ref.dtype)
-
-
-def place_gradients(lists, grads, rows):
-    entries, width = grads.shape
-    return pl.pallas_call(
-        place_kernel,
-        name="place_gradients",
-        grid=(rows // 256,),
-        out_shape=jax.ShapeDtypeStruct((rows, width), jnp.bfloat16),
-        in_specs=[pl.BlockSpec((1, entries), lambda i: (0, 0)), pl.BlockSpec((entries, width), lambda i: (0, 0))],
-        out_specs=pl.BlockSpec((256, width), lambda i: (i, 0)),
-        compiler_params=pltpu.CompilerParams(vmem_limit_bytes=40 * 1024 * 1024),
-    )(lists.reshape(1, entries), grads)
-
-
-def coordinates():
+def finish_kernel(
+    slot_grads, h1, dq, dk, dv, lists, small,
+    o_qkv, o_small, o_table,
+    by_column, by_owner, turned, grads, small_core, small_all, *rest,
+):
+    reducer = Reducer(
+        rest[:-8],
+        lambda j: grads.at[j, :, 1 - lax.rem(lax.axis_index("dp"), 2)],
+        lambda j, yy, rows: grads[j, yy, lax.rem(lax.axis_index("dp"), 2), rows, :],
+    )
+    sc_send, sc_recv, s_send, s_recv, a_send, a_recv, b_send, b_recv = rest[-8:]
     dp, store = lax.axis_index("dp"), lax.axis_index("store")
-    return lax.div(dp, 2), lax.rem(dp, 2), lax.div(store, 4), lax.rem(store, 4)
-
-
-def peer(y, core, x, z):
-    return (y * 2 + core, x * 4 + z)
-
-
-def along(axis, offset):
-    y, core, x, z = coordinates()
-    place = [y, x, z]
-    place[axis] = lax.rem(place[axis] + offset, 4)
-    return peer(place[0], core, place[1], place[2]), place[axis]
-
-
-def reduce_kernel(
-    g_down, g_up, g_out, g_q, g_k, g_v, small,
-    o_qkv, o_out, o_up, o_down, o_small,
-    own, got, part0, recv0, part1, recv1, part2, recv2, small_core, small_all,
-    own_sem, core_send, core_recv, send, recv, sc_send, sc_recv, s_send, s_recv,
-):
-    y, core, x, z = coordinates()
-    here = (y, x, z)
-    other = peer(y, 1 - core, x, z)
-    everyone = [other] + [along(a, k)[0] for a in range(3) for k in (1, 2, 3)]
-
-    barrier = pltpu.get_barrier_semaphore()
-    for device in everyone:
-        pl.semaphore_signal(barrier, inc=1, device_id=device, device_id_type=MESH)
-    pl.semaphore_wait(barrier, len(everyone))
-
-    sources = [g_down, g_up, g_out, g_q, g_k, g_v]
-    outs = [o_down, o_up, o_out] + [o_qkv] * 3
-    columns = [0, 0, 0, 0, 1024, 2048]
-    sends = []
-
-    local, cross = [], []
+    groups, owners = by_column.shape[0], by_owner.shape[0]
+    columns = [(lax.rem(dp + k, groups), store) for k in range(groups)]
+    shards = [(dp, lax.rem(store + k, owners)) for k in range(owners)]
+    here = reducer.here
+    meet(columns[1:] + shards[1:])
+
+    to_columns = []
+    for k in range(1, groups):
+        copy = pltpu.make_async_remote_copy(
+            src_ref=slot_grads.at[columns[k][0]], dst_ref=by_column.at[dp],
+            send_sem=a_send.at[k], recv_sem=a_recv.at[k], device_id=columns[k], device_id_type=MESH)
+        copy.start()
+        to_columns.append(copy)
     tiny = pltpu.make_async_remote_copy(
         src_ref=small, dst_ref=small_core, send_sem=sc_send, recv_sem=sc_recv,
-        device_id=other, device_id_type=MESH)
+        device_id=other_core(), device_id_type=MESH)
     tiny.start()
-    for j in range(PIECES):
-        remote = pltpu.make_async_remote_copy(
-            src_ref=sources[j].at[:, 1 - core], dst_ref=got.at[j],
-            send_sem=core_send.at[j], recv_sem=core_recv.at[j],
-            device_id=other, device_id_type=MESH)
-        remote.start()
-        cross.append(remote)
-        keep = pltpu.make_async_copy(sources[j].at[:, core], own.at[j], own_sem.at[j])
-        keep.start()
-        local.append(keep)
-
-    tiny.wait()
+    by_column[dp] = slot_grads[dp]
 
     def spread_small(axis):
         copies = []
         for k in (1, 2, 3):
-            device, _ = along(axis, k)
             copy = pltpu.make_async_remote_copy(
                 src_ref=small_all.at[axis, here[axis]], dst_ref=small_all.at[axis, here[axis]],
                 send_sem=s_send.at[axis, k - 1], recv_sem=s_recv.at[axis, k - 1],
-                device_id=device, device_id_type=MESH)
+                device_id=along(axis, k)[0], device_id_type=MESH)
             copy.start()
             copies.append(copy)
         return copies
@@ -509,154 +640,112 @@
     def total_small(axis):
         return (small_all[axis, 0] + small_all[axis, 1]) + (small_all[axis, 2] + small_all[axis, 3])
 
+    turned[...] = h1[...].T
+    for j, part in enumerate((dq, dk, dv)):
+
+        def multiply(i, carry, j=j, part=part):
+            yy, core = lax.div(i, 2), lax.rem(i, 2)
+            rows = pl.ds(pl.multiple_of(i * 128, 128), 128)
+            grads[j, yy, core] = jnp.dot(
+                turned[rows, :], part[...], preferred_element_type=jnp.float32
+            ).astype(jnp.bfloat16)
+            return carry
+
+        lax.fori_loop(0, 8, multiply, 0)
+        reducer.cross(j).start()
+
+    for copy in to_columns:
+        copy.wait_recv()
+    to_owners = []
+    for k in range(1, owners):
+        copy = pltpu.make_async_remote_copy(
+            src_ref=by_column.at[:, shards[k][1]], dst_ref=by_owner.at[store],
+            send_sem=b_send.at[k], recv_sem=b_recv.at[k], device_id=shards[k], device_id_type=MESH)
+        copy.start()
+        to_owners.append(copy)
+    by_owner[store] = by_column[:, store]
+
+    tiny.wait()
     small_all[0, here[0]] = small[...] + small_core[...]
     tiny_copies = spread_small(0)
-
-    def scatter(j, stage, part):
-        order = ORDERS[j % 3]
-        axis = order[stage]
-        left = [a for a in (0, 1, 2) if a not in order[:stage]]
-        where = left.index(axis)
-        landing = (recv0, recv1, recv2)[stage]
-        copies = []
-        for k in (1, 2, 3):
-            device, place = along(axis, k)
-            block = (j,) + (slice(None),) * where + (place,)
-            copy = pltpu.make_async_remote_copy(
-                src_ref=part.at[block], dst_ref=landing.at[j, k - 1],
-                send_sem=send.at[stage, j, k - 1], recv_sem=recv.at[stage, j, k - 1],
-                device_id=device, device_id_type=MESH)
-            copy.start()
-            copies.append(copy)
-        return copies
-
-    flight = [None] * PIECES
     for j in range(PIECES):
-        local[j].wait()
-        cross[j].wait_recv()
-
-        def add_cores(i, carry, j=j):
-            yy, xx = lax.div(i, 4), lax.rem(i, 4)
-            rows = pl.ds(pl.multiple_of(xx * 32, 32), 32)
-            total = own[j, yy, rows, :].astype(jnp.float32) + got[j, yy, rows, :].astype(jnp.float32)
-            for zz in range(4):
-                mine = total[8 * zz : 8 * zz + 8]
-                part0[j, yy, xx, zz] = jnp.concatenate([mine[:, :512], mine[:, 512:]], 0).astype(jnp.bfloat16)
-            return carry
-
-        lax.fori_loop(0, 16, add_cores, 0)
-        flight[j] = scatter(j, 0, part0)
-
+        reducer.add_cores(j)
     for copy in tiny_copies:
         copy.wait()
     small_all[1, here[1]] = total_small(0)
     tiny_copies = spread_small(1)
-
+    for copy in to_owners:
+        copy.wait_recv()
+
+    entries = lists.shape[1]
+    pairs = owners // lists.shape[0]
+
+    def place(i, carry):
+        base = i * 256
+        total = jnp.zeros((256, 128), jnp.float32)
+        for a in range(lists.shape[0]):
+            shape = (256, entries)
+            hit = jnp.broadcast_to(lists[a : a + 1, :], shape) == lax.broadcasted_iota(jnp.int32, shape, 0) + base
+            total = total + jnp.dot(
+                jnp.where(hit, 1.0, 0.0).astype(jnp.bfloat16),
+                by_owner[pairs * a : pairs * (a + 1)].reshape(entries, 128),
+                preferred_element_type=jnp.float32,
+            )
+        o_table[pl.ds(pl.multiple_of(base, 256), 256), :] = total.astype(jnp.bfloat16)
+        return carry
+
+    blocks = o_table.shape[0] // 256
+    first = blocks // 4
+    lax.fori_loop(0, first, place, 0)
     for j in range(PIECES):
-        for copy in flight[j]:
-            copy.wait_recv()
-        sends += flight[j]
-        axis = ORDERS[j % 3][0]
-
-        def add_first(i, carry, j=j, axis=axis):
-            a, b = lax.div(i, 4), lax.rem(i, 4)
-            block = [a, b]
-            block.insert(axis, here[axis])
-            total = part0[(j,) + tuple(block)].astype(jnp.float32)
-            for k in range(3):
-                total = total + recv0[j, k, a, b].astype(jnp.float32)
-            part1[j, a, b] = total.astype(jnp.bfloat16)
-            return carry
-
-        lax.fori_loop(0, 16, add_first, 0)
-        flight[j] = scatter(j, 1, part1)
-
+        reducer.add(0, j)
     for copy in tiny_copies:
         copy.wait()
     small_all[2, here[2]] = total_small(1)
     tiny_copies = spread_small(2)
-
+    lax.fori_loop(first, first + blocks // 2, place, 0)
     for j in range(PIECES):
-        for copy in flight[j]:
-            copy.wait_recv()
-        sends += flight[j]
-        order = ORDERS[j % 3]
-        where = [a for a in (0, 1, 2) if a != order[0]].index(order[1])
-
-        def add_second(i, carry, j=j, axis=order[1], where=where):
-            block = [i]
-            block.insert(where, here[axis])
-            total = part1[(j,) + tuple(block)].astype(jnp.float32)
-            for k in range(3):
-                total = total + recv1[j, k, i].astype(jnp.float32)
-            part2[j, i] = total.astype(jnp.bfloat16)
-            return carry
-
-        lax.fori_loop(0, 4, add_second, 0)
-        flight[j] = scatter(j, 2, part2)
-
+        reducer.add(1, j)
+    lax.fori_loop(first + blocks // 2, blocks, place, 0)
     for copy in tiny_copies:
         copy.wait()
     o_small[...] = total_small(2)
-
     for j in range(PIECES):
-        for copy in flight[j]:
-            copy.wait_recv()
-        sends += flight[j]
-        axis = ORDERS[j % 3][2]
-        total = part2[j, here[axis]].astype(jnp.float32)
-        for k in range(3):
-            total = total + recv2[j, k].astype(jnp.float32)
-        joined = jnp.concatenate([total[:8], total[8:]], 1).astype(jnp.bfloat16)
-        outs[j][:, columns[j] : columns[j] + 1024] = joined
-
-    for copy in cross + sends:
+        o_qkv[:, j * 1024 : j * 1024 + 1024] = reducer.result(j)
+    reducer.close()
+    for copy in to_columns + to_owners:
         copy.wait_send()
 
 
-def reduce_gradients(gradients, small):
+def finish(slot_grads, h1, dq, dk, dv, lists, small, rows):
     bf16, f32 = jnp.bfloat16, jnp.float32
-    hbm = pl.BlockSpec(memory_space=pl.ANY)
+    groups, owners = slot_grads.shape[:2]
     vmem = pl.BlockSpec(memory_space=pltpu.VMEM)
     dma = pltpu.SemaphoreType.DMA
-    split = lambda g: g.reshape(4, 2, 128, g.shape[1])
     return pl.pallas_call(
-        reduce_kernel,
-        name="reduce_gradients",
+        finish_kernel,
+        name="finish",
         out_shape=(
             jax.ShapeDtypeStruct((8, 3072), bf16),
-            jax.ShapeDtypeStruct((8, 1024), bf16),
-            jax.ShapeDtypeStruct((8, 1024), bf16),
-            jax.ShapeDtypeStruct((8, 1024), bf16),
             jax.ShapeDtypeStruct(small.shape, f32),
+            jax.ShapeDtypeStruct((rows, 128), bf16),
         ),
-        in_specs=[hbm] * PIECES + [vmem],
-        out_specs=[vmem] * 5,
+        in_specs=[vmem] * 7,
+        out_specs=[vmem] * 3,
         scratch_shapes=[
-            pltpu.VMEM((PIECES, 4, 128, 1024), bf16),
-            pltpu.VMEM((PIECES, 4, 128, 1024), bf16),
-            pltpu.VMEM((PIECES, 4, 4, 4, 16, 512), bf16),
-            pltpu.VMEM((PIECES, 3, 4, 4, 16, 512), bf16),
-            pltpu.VMEM((PIECES, 4, 4, 16, 512), bf16),
-            pltpu.VMEM((PIECES, 3, 4, 16, 512), bf16),
-            pltpu.VMEM((PIECES, 4, 16, 512), bf16),
-            pltpu.VMEM((PIECES, 3, 16, 512), bf16),
+            pltpu.VMEM(slot_grads.shape, bf16),
+            pltpu.VMEM((owners, groups) + slot_grads.shape[2:], bf16),
+            pltpu.VMEM((h1.shape[1], h1.shape[0]), bf16),
+            pltpu.VMEM((PIECES, 4, 2, 128, 1024), bf16),
             pltpu.VMEM(small.shape, f32),
             pltpu.VMEM((3, 4) + small.shape, f32),
-            dma((PIECES,)),
-            dma((PIECES,)),
-            dma((PIECES,)),
-            dma((3, PIECES, 3)),
-            dma((3, PIECES, 3)),
-            dma,
-            dma,
-            dma((3, 3)),
-            dma((3, 3)),
-        ],
+        ]
+        + Reducer.scratch()
+        + [dma, dma, dma((3, 3)), dma((3, 3)), dma((groups,)), dma((groups,)), dma((owners,)), dma((owners,))],
         compiler_params=pltpu.CompilerParams(
-            collective_id=0, has_side_effects=True, vmem_limit_bytes=40 * 1024 * 1024
+            collective_id=0, has_side_effects=True, vmem_limit_bytes=48 * 1024 * 1024
         ),
-    )(*[split(g) for g in gradients], small)
+    )(slot_grads, h1, dq, dk, dv, lists, small)
 
 
 def body(
@@ -673,11 +762,10 @@
     bias_table,
 ):
     bf16, f32 = jnp.bfloat16, jnp.float32
-    both = ("dp", "store")
     shard_rows, width = node_table.shape
     owners, cap = touched.shape[1:]
     egos, count = member_slot.shape
-    tokens, slots_held = egos * count, owners * cap
+    tokens = egos * count
     dot = lambda a, b: jnp.dot(a, b, preferred_element_type=f32)
     back = lambda a, b: lax.dot_general(a, b, (((1,), (1,)), ((), ())), preferred_element_type=f32)
     weight = lambda a, b: lax.dot_general(
@@ -704,7 +792,9 @@
     dy = dout.astype(f32) + dy
     dyb = dy.astype(bf16)
     dattn = back(dyb, w_out).astype(bf16)
-    dq, dk, dv, grad_bias = attention_backward(qkv, dattn, probs, distances)
+    dq, dk, dv, grad_bias, (sum_down, sum_up, sum_out) = attention_backward(
+        qkv, dattn, probs, distances, (weight(act, dout), weight(h2, du), weight(attended, dyb))
+    )
     dh1 = (
         back(dq, w_qkv[:, :width])
         + back(dk, w_qkv[:, width : 2 * width])
@@ -713,19 +803,14 @@
     dx, gain_one = layer_normalize_backward(dh1, gains[0], x_hat, x_rstd)
     dx = dy + dx
 
-    slot_grads = slot_gradients(member_slot, dx, slots_held)
-    returned = lax.all_to_all(
-        slot_grads.reshape(-1, cap, 128), both, split_axis=0, concat_axis=0, tiled=True
-    )
-    gradients = (
-        weight(act, dout), weight(h2, du), weight(attended, dyb),
-        weight(h1, dq), weight(h1, dk), weight(h1, dv),
-    )
+    padded = -(-cap // 16) * 16
+    member = member_slot + (padded - cap) * lax.div(member_slot, cap)
+    slot_grads = slot_gradients(member, dx, owners * padded).reshape(-1, owners, padded, 128)
+    entries = lists[:, :, :padded].transpose(1, 0, 2).reshape(owners // 2, -1)
     small = jnp.concatenate(
         [gain_one.reshape(8, 128), gain_two.reshape(8, 128), grad_bias.reshape(8, 128)]
     )
-    sum_qkv, sum_out, sum_up, sum_down, small = reduce_gradients(gradients, small)
-    grad_table = place_gradients(lists, returned.reshape(-1, 128), shard_rows)
+    sum_qkv, small, grad_table = finish(slot_grads, h1, dq, dk, dv, entries, small, shard_rows)
     return (
         layer_out.reshape(egos, count, width),
         grad_table,

time: 214 us -> 226 us (1.056)
  Pallas kernels: 148 us -> 172 us
  starting transfers between devices: 10.3 us -> 0 us
  matrix products: 37.8 us -> 34.9 us
    pallas_call x2 -> x1, Pallas kernels: 56 us -> 69.3 us  [finish(): pl.pallas_call(finish_kernel, name='finish', out_shape=(jax.ShapeDtypeStr...]
    pallas_call x1, Pallas kernels: 37.1 us -> 48.2 us  [attention_backward(): pl.pallas_call(attend_back_kernel, name='attend_back', grid=(egos, groups...]
    all_to_all x1 -> x0, starting transfers between devices: 10.3 us -> none  [body(): lax.all_to_all(slot_grads.reshape(-1, cap, 128), both, split_axis=0, conc...]
    dot_general x6 -> x3, matrix products: 15.6 us -> 8.1 us  [body(): lax.dot_general(a, b, (((0,), (0,)), ((), ())), preferred_element_type=f32)]
    dot_general x6, matrix products: 9.64 us -> 14.9 us  [body(): lax.dot_general(a, b, (((1,), (1,)), ((), ())), preferred_element_type=f32)]
    unnamed x68 -> x49, local copies, waits for them, and re-layouts: 8.83 us -> 10 us
  transfers between devices with their start and end apart: 1 -> 0, of which waited for: 0 -> 0; matrix products, arithmetic and copies ran while one was open for 10% -> 0% of each run, Pallas kernels for 22% -> 0%
where the time goes in v4:
time: 226 us; the launch traced here: 225 us
  Pallas kernels  172 us (76%)
  matrix products  34.9 us (15%)
  local copies, waits for them, and re-layouts  13.1 us (6%)
  other arithmetic  3.84 us (2%)
    pallas_call x1, Pallas kernels, finish(): pl.pallas_call(finish_kernel, name='finish', out_shape=(jax.ShapeDtypeStr...  69.3 us
    pallas_call x1, Pallas kernels, attention_backward(): pl.pallas_call(attend_back_kernel, name='attend_back', grid=(egos, groups...  48.2 us
    pallas_call x1, Pallas kernels, fetch(): pl.pallas_call(fetch_kernel, name='fetch', out_shape=(jax.ShapeDtypeStruc...  32.3 us
    pallas_call x1, Pallas kernels, attention_forward(): pl.pallas_call(attend_kernel, name='attend', grid=(egos, groups), out_sha...  19.8 us
    dot_general x6, matrix products, body(): lax.dot_general(a, b, (((1,), (1,)), ((), ())), preferred_element_type=f32)  14.9 us
    dot_general x4, matrix products, body(): dot = lambda a, b: jnp.dot(a, b, preferred_element_type=f32)  11.9 us
    unnamed x49, local copies, waits for them, and re-layouts  10 us
    dot_general x3, matrix products, body(): lax.dot_general(a, b, (((0,), (0,)), ((), ())), preferred_element_type=f32)  8.1 us

profile of v4, /device:TPU:1, one launch (start us, length us, event | category | flops | bytes accessed | tf_op | source)
XLA Modules:
  0.0 225.1 jit_solution(15795486877988836624)
XLA Ops:
  0.6 0.8 add_bitcast_fusion
  4.0 2.2 copy-done.6
  6.2 1.0 copy-done.7
  7.2 32.3 %fetch.1 = (bf16[512,1024]{1,0:T(8,128)(2,1)S(1)}, s32[8,16,1,128]{3,2,1,0:T(1,128)S(1)}, f32[2,32,256,256]{3,2,1,0:T(8,128)}) custom-call(s32[16,1,128]{2,1,0:T(1,128)S(1)} %pad.8.touched, s32[512,1]{1,0:T(8,128)S(1)} %bitcast.47, bf16[2048,1024]{1,0:T(8,128)(2,1)S(1)} %copy-done.6, s32[2,256,256]{2,1,0:T(8,128)S(1)} %copy-done.7, f32[32,128]{1,0:T(8,128)S(1)} %pad.9.lookup), custom_call_target="tpu_custom_call" | custom-call | tf_op jit(solution)/shard_map/fetch/pallas_call | solution.py:314
  40.7 6.8 %convolution_convert_fusion.q_ref.k_ref.v_ref = bf16[512,3072]{1,0:T(8,128)(2,1)S(1)} fusion(bf16[512,1024]{1,0:T(8,128)(2,1)S(1)} %fusion.6.h1, bf16[1024,3072]{1,0:T(8,128)(2,1)} %param.16), kind=kOutput, calls=%fused_computation | convolution fusion | flops 3222798336 | bytes 10485760 | tf_op jit(solution)/shard_map/dot_general | solution.py:769
  47.6 19.8 %attend.1 = (bf16[512,1024]{1,0:T(8,128)(2,1)S(1)}, f32[2,32,256,256]{3,2,1,0:T(8,128)}) custom-call(bf16[512,3072]{1,0:T(8,128)(2,1)S(1)} %convolution_convert_fusion.q_ref.k_ref.v_ref, bf16[512,3072]{1,0:T(8,128)(2,1)S(1)} %convolution_convert_fusion.q_ref.k_ref.v_ref, bf16[512,3072]{1,0:T(8,128)(2,1)S(1)} %convolution_convert_fusion.q_ref.k_ref.v_ref, ...), custom_call_target="tpu_custom_call" | custom-call | tf_op jit(solution)/shard_map/attend/pallas_call | solution.py:525
  67.4 1.3 fusion.31
  69.1 1.5 multiply_convert_fusion
  71.0 2.0 fusion.18
  73.0 2.2 add_convert_fusion
  75.2 2.6 %convolution_convert_fusion.3 = bf16[1024,1024]{1,0:T(8,128)(2,1)} fusion(bf16[512,1024]{1,0:T(8,128)(2,1)S(1)} %get-tuple-element.50, bf16[512,1024]{1,0:T(8,128)(2,1)S(1)} %bitcast.54), kind=kOutput, calls=%fused_computation.42 | convolution fusion | flops 1074790400 | bytes 4194304 | tf_op jit(solution)/shard_map/dot_general | solution.py:771
  77.8 2.8 %convolution_convert_fusion.2 = bf16[1024,1024]{1,0:T(8,128)(2,1)} fusion(bf16[512,1024]{1,0:T(8,128)(2,1)S(1)} %fusion.18, f32[512,1024]{1,0:T(8,128)S(1)} %get-tuple-element.49, f32[1024]{0:T(1024)S(1)} %bitcast.60, f32[512]{0:T(512)S(1)} %add_rsqrt_fusion, f32[512]{0:T(512)S(1)} %broadcast_multiply_fusion.4), kind=kOutput, calls=%fused_computation.41 | convolution fusion | flops 1076887552 | bytes 5251072 | tf_op jit(solution)/shard_map/dot_general | solution.py:771
  80.7 1.7 multiply_reduce_fusion
  83.2 2.7 %convolution_convert_fusion.1 = bf16[1024,1024]{1,0:T(8,128)(2,1)} fusion(bf16[512,1024]{1,0:T(8,128)(2,1)S(1)} %get-tuple-element.25, f32[512,1024]{1,0:T(8,128)S(1)} %multiply_add_fusion), kind=kOutput, calls=%fused_computation.40 | convolution fusion | flops 1075314688 | bytes 5242880 | tf_op jit(solution)/shard_map/dot_general | solution.py:771
  85.9 1.3 convolution_convert_fusion.4.dattn_ref
  87.2 48.2 %attend_back.1 = (bf16[512,1024]{1,0:T(8,128)(2,1)S(1)}, bf16[512,1024]{1,0:T(8,128)(2,1)S(1)}, bf16[512,1024]{1,0:T(8,128)(2,1)S(1)}, f32[2,32,256]{2,1,0:T(8,1...) custom-call(bf16[512,3072]{1,0:T(8,128)(2,1)} %copy-done.2, ...), custom_call_target="tpu_custom_call" | custom-call | tf_op jit(solution)/shard_map/attend_back/pallas_call | solution.py:546
  135.4 1.0 copy-done.13
  136.7 3.3 %fusion.23 = f32[512,1024]{1,0:T(8,128)S(1)} fusion(bf16[512,1024]{1,0:T(8,128)(2,1)S(1)} %get-tuple-element.27.dq, bf16[1024,3072]{1,0:T(8,128)(2,1)} %param.16), kind=kOutput, calls=%fused_computation.30 | convolution fusion | flops 1073741824 | bytes 5242880 | tf_op jit(solution)/shard_map/dot_general | solution.py:770
  140.1 3.0 %fusion.21 = f32[512,1024]{1,0:T(8,128)S(1)} fusion(bf16[512,1024]{1,0:T(8,128)(2,1)S(1)} %get-tuple-element.28.dk, bf16[1024,3072]{1,0:T(8,128)(2,1)} %param.16), kind=kOutput, calls=%fused_computation.28 | convolution fusion | flops 1073741824 | bytes 5242880 | tf_op jit(solution)/shard_map/dot_general | solution.py:770
  143.1 3.6 %fusion.11 = (f32[1024]{0:T(1024)S(1)}, f32[512]{0:T(512)S(1)}, f32[512]{0:T(512)S(1)}, f32[512,1024]{1,0:T(8,128)S(1)}) fusion(bf16[512,1024]{1,0:T(8,128)(2,1)S(1)} %get-tuple-element.23, f32[512]{0:T(512)S(1)} %add_rsqrt_fusion.1, f32[512]{0:T(512)S(1)} %broadcast_multiply_fusion.5, f32[1024]{0:T(1024)S(1)} %bitcast.57, ...), kind=kOutput, calls=%fused_computation.16 | convolution fusion | flops 1079506944 | bytes 10502144 | tf_op jit(solution)/shard_map/dot_general | solution.py:770
  147.5 2.5 %slot_gradients.1 = bf16[8,768,128]{2,1,0:T(8,128)(2,1)S(1)} custom-call(s32[1,512]{1,0:T(1,128)S(1)} %bitcast.49, f32[512,1024]{1,0:T(8,128)S(1)} %fusion.10.dx_ref), custom_call_target="tpu_custom_call" | custom-call | tf_op jit(solution)/shard_map/slot_gradients/pallas_call | solution.py:587
  150.1 1.1 copy-done.3
  151.2 69.3 %finish.1 = (bf16[8,3072]{1,0:T(8,128)(2,1)S(1)}, f32[24,128]{1,0:T(8,128)S(1)}, bf16[2048,128]{1,0:T(8,128)(2,1)S(1)}) custom-call(bf16[8,16,48,128]{3,2,1,0:T(8,128)(2,1)} %bitcast.46, bf16[512,1024]{1,0:T(8,128)(2,1)S(1)} %copy-done.5, bf16[512,1024]{1,0:T(8,128)(2,1)S(1)} %copy-done.10, bf16[512,1024]{1,0:T(8,128)(2,1)S(1)} %copy-done.12, ...), custom_call_target="tpu_custom_call" | custom-call | tf_op jit(solution)/shard_map/finish/pallas_call | solution.py:725
  221.9 0.8 copy.36
  (74 shorter events, 10.0 us)
Async XLA Ops:
  0.6 68.5 %copy-start = (bf16[1024,1024]{1,0:T(8,128)(2,1)S(1)}, bf16[1024,1024]{1,0:T(8,128)(2,1)}, u32[]{:S(2)}) copy-start(bf16[1024,1024]{1,0:T(8,128)(2,1)} %param.18) | copy-start | bytes 6291460
  4.0 2.2 copy-start.6
  6.2 1.0 copy-start.7
  40.7 6.9 %copy-start.4 = (bf16[512,1024]{1,0:T(8,128)(2,1)}, bf16[512,1024]{1,0:T(8,128)(2,1)S(1)}, u32[]{:S(2)}) copy-start(bf16[512,1024]{1,0:T(8,128)(2,1)S(1)} %fusion.6.h1) | copy-start | bytes 3145732
  47.6 19.8 %copy-start.2 = (bf16[512,3072]{1,0:T(8,128)(2,1)}, bf16[512,3072]{1,0:T(8,128)(2,1)S(1)}, u32[]{:S(2)}) copy-start(bf16[512,3072]{1,0:T(8,128)(2,1)S(1)} %convolution_convert_fusion.q_ref.k_ref.v_ref) | copy-start | bytes 9437188
  47.6 19.8 %copy-start.19 = (bf16[1024,1024]{1,0:T(8,128)(2,1)S(1)}, bf16[1024,1024]{1,0:T(8,128)(2,1)}, u32[]{:S(2)}) copy-start(bf16[1024,1024]{1,0:T(8,128)(2,1)} %param.17) | copy-start | bytes 6291460
  69.1 1.5 copy-start.17
  69.1 1.9 copy-start.18
  83.2 2.7 %copy-start.15 = (f32[512,1024]{1,0:T(8,128)}, f32[512,1024]{1,0:T(8,128)S(1)}, u32[]{:S(2)}) copy-start(f32[512,1024]{1,0:T(8,128)S(1)} %multiply_add_fusion) | copy-start | bytes 6291460
  85.9 1.3 copy-start.8
  135.4 1.0 copy-start.13
  136.4 3.6 %copy-start.9 = (bf16[512,1024]{1,0:T(8,128)(2,1)}, bf16[512,1024]{1,0:T(8,128)(2,1)S(1)}, u32[]{:S(2)}) copy-start(bf16[512,1024]{1,0:T(8,128)(2,1)S(1)} %get-tuple-element.27.dq) | copy-start | bytes 3145732
  136.4 3.6 %copy-start.11 = (bf16[512,1024]{1,0:T(8,128)(2,1)}, bf16[512,1024]{1,0:T(8,128)(2,1)S(1)}, u32[]{:S(2)}) copy-start(bf16[512,1024]{1,0:T(8,128)(2,1)S(1)} %get-tuple-element.28.dk) | copy-start | bytes 3145732
  140.1 3.0 %copy-start.14 = (bf16[512,1024]{1,0:T(8,128)(2,1)S(1)}, bf16[512,1024]{1,0:T(8,128)(2,1)}, u32[]{:S(2)}) copy-start(bf16[512,1024]{1,0:T(8,128)(2,1)} %copy-done.13) | copy-start | bytes 3145732
  143.0 3.7 %copy-start.16 = (f32[512,1024]{1,0:T(8,128)S(1)}, f32[512,1024]{1,0:T(8,128)}, u32[]{:S(2)}) copy-start(f32[512,1024]{1,0:T(8,128)} %copy-done.15) | copy-start | bytes 6291460
  147.5 3.7 %copy-start.5 = (bf16[512,1024]{1,0:T(8,128)(2,1)S(1)}, bf16[512,1024]{1,0:T(8,128)(2,1)}, u32[]{:S(2)}) copy-start(bf16[512,1024]{1,0:T(8,128)(2,1)} %copy-done.4) | copy-start | bytes 3145732
  147.5 3.7 %copy-start.10 = (bf16[512,1024]{1,0:T(8,128)(2,1)S(1)}, bf16[512,1024]{1,0:T(8,128)(2,1)}, u32[]{:S(2)}) copy-start(bf16[512,1024]{1,0:T(8,128)(2,1)} %copy-done.9) | copy-start | bytes 3145732
  147.5 3.7 %copy-start.12 = (bf16[512,1024]{1,0:T(8,128)(2,1)S(1)}, bf16[512,1024]{1,0:T(8,128)(2,1)}, u32[]{:S(2)}) copy-start(bf16[512,1024]{1,0:T(8,128)(2,1)} %copy-done.11) | copy-start | bytes 3145732
  150.1 1.2 copy-start.3
  151.2 73.9 %copy-start.1 = (bf16[1024,1024]{1,0:T(8,128)(2,1)S(1)}, bf16[1024,1024]{1,0:T(8,128)(2,1)}, u32[]{:S(2)}) copy-start(bf16[1024,1024]{1,0:T(8,128)(2,1)} %param.18) | copy-start | bytes 6291460

commit v5 on v4

--- a/solution.py
+++ b/solution.py
@@ -59,11 +59,14 @@
     return peer(y, 1 - core, x, z)
 
 
-def meet(devices):
+def signal_meet(devices):
     barrier = pltpu.get_barrier_semaphore()
     for device in devices:
         pl.semaphore_signal(barrier, inc=1, device_id=device, device_id_type=MESH)
-    pl.semaphore_wait(barrier, len(devices))
+
+
+def wait_meet(devices):
+    pl.semaphore_wait(pltpu.get_barrier_semaphore(), len(devices))
 
 
 class Reducer:
@@ -398,29 +401,33 @@
 
     @pl.when(step == 0)
     def _():
+        signal_meet(torus_peers())
         for j in range(PIECES):
             keep(j).start()
-        meet(torus_peers())
+
+    @pl.when(step == 1)
+    def _():
+        wait_meet(torus_peers())
         for j in range(PIECES):
             reducer.cross(j).start()
 
-    @pl.when(step == 1)
+    @pl.when(step == 3)
     def _():
         for j in range(PIECES):
             keep(j).wait()
             reducer.add_cores(j)
 
-    @pl.when(step == 4)
+    @pl.when(step == 5)
     def _():
         for j in range(PIECES):
             reducer.add(0, j)
 
-    @pl.when(step == 5)
+    @pl.when(step == 6)
     def _():
         for j in range(PIECES):
             reducer.add(1, j)
 
-    @pl.when(step == 6)
+    @pl.when(step == 7)
     def _():
         for j in range(PIECES):
             sums[j][...] = reducer.result(j)
@@ -567,64 +574,120 @@
     return dq, dk, dv, bias.reshape(egos, heads, 8, 32).sum((0, 2)).T, sums
 
 
-def slot_kernel(member_ref, dx_ref, out_ref):
-    slots, tokens = out_ref.shape[1], dx_ref.shape[0]
-    shape = (slots, tokens)
-    hit = jnp.broadcast_to(member_ref[...], shape) == lax.broadcasted_iota(jnp.int32, shape, 0)
-    placed = jnp.where(hit, 1.0, 0.0).astype(jnp.bfloat16)
-    dx = dx_ref[...]
-    high = dx.astype(jnp.bfloat16)
-    low = (dx - high.astype(jnp.float32)).astype(jnp.bfloat16)
-    total = jnp.dot(placed, high, preferred_element_type=jnp.float32) + jnp.dot(
-        placed, low, preferred_element_type=jnp.float32
+CHUNKS = 4
+
+
+def finish_kernel(
+    h1, dq, dk, dv, x, dy, gain, members, lists, small, w_hbm,
+    o_qkv, o_small, o_table,
+    weights, turned, grads, dh1, high, low, gain_sum, slot_grads, by_column, by_owner, placed,
+    mine, small_core, small_all, *rest,
+):
+    dp, store = lax.axis_index("dp"), lax.axis_index("store")
+    core = lax.rem(dp, 2)
+    reducer = Reducer(
+        rest[:-9],
+        lambda j: grads.at[j, :, 1 - core],
+        lambda j, yy, rows: grads[j, yy, core, rows, :],
     )
-    for c in range(out_ref.shape[0]):
-        out_ref[c] = total[:, c * 128 : c * 128 + 128].astype(out_ref.dtype)
-
-
-def slot_gradients(member_slot, dx, slots):
-    tokens, width = dx.shape
-    return pl.pallas_call(
-        slot_kernel,
-        name="slot_gradients",
-        grid=(width // 256,),
-        out_shape=jax.ShapeDtypeStruct((width // 128, slots, 128), jnp.bfloat16),
-        in_specs=[pl.BlockSpec((1, tokens), lambda i: (0, 0)), pl.BlockSpec((tokens, 256), lambda i: (0, i))],
-        out_specs=pl.BlockSpec((2, slots, 128), lambda i: (i, 0, 0)),
-        compiler_params=pltpu.CompilerParams(vmem_limit_bytes=40 * 1024 * 1024),
-    )(member_slot.reshape(1, tokens), dx)
-
-
-def finish_kernel(
-    slot_grads, h1, dq, dk, dv, lists, small,
-    o_qkv, o_small, o_table,
-    by_column, by_owner, turned, grads, small_core, small_all, *rest,
-):
-    reducer = Reducer(
-        rest[:-8],
-        lambda j: grads.at[j, :, 1 - lax.rem(lax.axis_index("dp"), 2)],
-        lambda j, yy, rows: grads[j, yy, lax.rem(lax.axis_index("dp"), 2), rows, :],
-    )
-    sc_send, sc_recv, s_send, s_recv, a_send, a_recv, b_send, b_recv = rest[-8:]
-    dp, store = lax.axis_index("dp"), lax.axis_index("store")
-    groups, owners = by_column.shape[0], by_owner.shape[0]
+    w_sem, sc_send, sc_recv, s_send, s_recv, a_send, a_recv, b_send, b_recv = rest[-9:]
+    groups, owners, padded, _ = by_column.shape
+    per = owners // CHUNKS
+    tokens, width = x.shape
     columns = [(lax.rem(dp + k, groups), store) for k in range(groups)]
     shards = [(dp, lax.rem(store + k, owners)) for k in range(owners)]
     here = reducer.here
-    meet(columns[1:] + shards[1:])
+    signal_meet(columns[1:] + shards[1:])
+    load = pltpu.make_async_copy(w_hbm, weights, w_sem)
+    load.start()
+
+    turned[...] = h1[...].T
+    for j, part in enumerate((dq, dk, dv)):
+
+        def multiply(i, carry, j=j, part=part):
+            rows = pl.ds(pl.multiple_of(i * 256, 256), 256)
+            block = jnp.dot(turned[rows, :], part[...], preferred_element_type=jnp.float32).astype(jnp.bfloat16)
+            grads[j, i, 0] = block[:128]
+            grads[j, i, 1] = block[128:]
+            return carry
+
+        lax.fori_loop(0, 4, multiply, 0)
+        if j == 0:
+            wait_meet(columns[1:] + shards[1:])
+            load.wait()
+        reducer.cross(j).start()
+
+    def back(i, carry):
+        rows = pl.ds(pl.multiple_of(i * 256, 256), 256)
+        total = jnp.zeros((tokens, 256), jnp.float32)
+        for j, part in enumerate((dq, dk, dv)):
+            total = total + lax.dot_general(
+                part[...], weights[rows, j * width : j * width + width], (((1,), (1,)), ((), ())),
+                preferred_element_type=jnp.float32)
+        dh1[i] = total
+        return carry
+
+    lax.fori_loop(0, 2, back, 0)
+    reducer.add_cores(0)
+    lax.fori_loop(2, 4, back, 0)
+    reducer.add_cores(1)
+    reducer.add_cores(2)
+    gain_sum[...] = jnp.zeros_like(gain_sum)
+
+    def norm_back(i, carry):
+        rows = pl.ds(pl.multiple_of(i * 32, 32), 32)
+        centred = x[rows, :].astype(jnp.float32)
+        centred = centred - jnp.mean(centred, -1, keepdims=True)
+        rstd = lax.rsqrt(jnp.mean(centred * centred, -1, keepdims=True) + EPS)
+        vhat = centred * rstd
+        grad = jnp.concatenate([dh1[n, rows, :] for n in range(4)], 1)
+        product = grad * vhat
+        gain_sum[...] += product[:8] + product[8:16] + product[16:24] + product[24:]
+        scaled = grad * gain[...]
+        first = jnp.mean(scaled, -1, keepdims=True)
+        second = jnp.mean(scaled * vhat, -1, keepdims=True)
+        dx = dy[rows, :] + rstd * (scaled - first - vhat * second)
+        top = dx.astype(jnp.bfloat16)
+        high[rows, :] = top
+        low[rows, :] = (dx - top.astype(jnp.float32)).astype(jnp.bfloat16)
+        return carry
+
+    lax.fori_loop(0, tokens // 32, norm_back, 0, unroll=2)
 
     to_columns = []
-    for k in range(1, groups):
-        copy = pltpu.make_async_remote_copy(
-            src_ref=slot_grads.at[columns[k][0]], dst_ref=by_column.at[dp],
-            send_sem=a_send.at[k], recv_sem=a_recv.at[k], device_id=columns[k], device_id_type=MESH)
-        copy.start()
-        to_columns.append(copy)
+    for i in range(CHUNKS):
+        block = (per * padded, tokens)
+        hit = jnp.broadcast_to(members[...], block) == lax.broadcasted_iota(jnp.int32, block, 0) + i * per * padded
+        chosen = jnp.where(hit, 1.0, 0.0).astype(jnp.bfloat16)
+        total = jnp.dot(chosen, high[...], preferred_element_type=jnp.float32) + jnp.dot(
+            chosen, low[...], preferred_element_type=jnp.float32
+        )
+        for c in range(groups):
+            slot_grads[c, i * per : i * per + per] = (
+                total[:, c * 128 : c * 128 + 128].reshape(per, padded, 128).astype(jnp.bfloat16)
+            )
+        some = pl.ds(i * per, per)
+        copies = []
+        for k in range(1, groups):
+            copy = pltpu.make_async_remote_copy(
+                src_ref=slot_grads.at[columns[k][0], some], dst_ref=by_column.at[dp, some],
+                send_sem=a_send.at[i, k], recv_sem=a_recv.at[i, k], device_id=columns[k], device_id_type=MESH)
+            copy.start()
+            copies.append(copy)
+        by_column[dp, some] = slot_grads[dp, some]
+        to_columns.append(copies)
+
+    sums = gain_sum[...]
+    sums = sums[:4] + sums[4:]
+    sums = sums[:2] + sums[2:]
+    sums = sums[:1] + sums[1:]
+    mine[...] = small[...]
+    for n in range(8):
+        mine[n : n + 1, :] = sums[:, n * 128 : n * 128 + 128]
     tiny = pltpu.make_async_remote_copy(
-        src_ref=small, dst_ref=small_core, send_sem=sc_send, recv_sem=sc_recv,
+        src_ref=mine, dst_ref=small_core, send_sem=sc_send, recv_sem=sc_recv,
         device_id=other_core(), device_id_type=MESH)
     tiny.start()
-    by_column[dp] = slot_grads[dp]
 
     def spread_small(axis):
         copies = []
@@ -640,112 +703,112 @@
     def total_small(axis):
         return (small_all[axis, 0] + small_all[axis, 1]) + (small_all[axis, 2] + small_all[axis, 3])
 
-    turned[...] = h1[...].T
-    for j, part in enumerate((dq, dk, dv)):
-
-        def multiply(i, carry, j=j, part=part):
-            yy, core = lax.div(i, 2), lax.rem(i, 2)
-            rows = pl.ds(pl.multiple_of(i * 128, 128), 128)
-            grads[j, yy, core] = jnp.dot(
-                turned[rows, :], part[...], preferred_element_type=jnp.float32
-            ).astype(jnp.bfloat16)
-            return carry
-
-        lax.fori_loop(0, 8, multiply, 0)
-        reducer.cross(j).start()
-
-    for copy in to_columns:
-        copy.wait_recv()
-    to_owners = []
-    for k in range(1, owners):
-        copy = pltpu.make_async_remote_copy(
-            src_ref=by_column.at[:, shards[k][1]], dst_ref=by_owner.at[store],
-            send_sem=b_send.at[k], recv_sem=b_recv.at[k], device_id=shards[k], device_id_type=MESH)
-        copy.start()
-        to_owners.append(copy)
-    by_owner[store] = by_column[:, store]
-
-    tiny.wait()
-    small_all[0, here[0]] = small[...] + small_core[...]
-    tiny_copies = spread_small(0)
-    for j in range(PIECES):
-        reducer.add_cores(j)
-    for copy in tiny_copies:
-        copy.wait()
-    small_all[1, here[1]] = total_small(0)
-    tiny_copies = spread_small(1)
-    for copy in to_owners:
-        copy.wait_recv()
-
-    entries = lists.shape[1]
-    pairs = owners // lists.shape[0]
-
-    def place(i, carry):
-        base = i * 256
-        total = jnp.zeros((256, 128), jnp.float32)
-        for a in range(lists.shape[0]):
-            shape = (256, entries)
-            hit = jnp.broadcast_to(lists[a : a + 1, :], shape) == lax.broadcasted_iota(jnp.int32, shape, 0) + base
-            total = total + jnp.dot(
-                jnp.where(hit, 1.0, 0.0).astype(jnp.bfloat16),
-                by_owner[pairs * a : pairs * (a + 1)].reshape(entries, 128),
-                preferred_element_type=jnp.float32,
-            )
-        o_table[pl.ds(pl.multiple_of(base, 256), 256), :] = total.astype(jnp.bfloat16)
-        return carry
-
-    blocks = o_table.shape[0] // 256
-    first = blocks // 4
-    lax.fori_loop(0, first, place, 0)
     for j in range(PIECES):
         reducer.add(0, j)
-    for copy in tiny_copies:
-        copy.wait()
-    small_all[2, here[2]] = total_small(1)
-    tiny_copies = spread_small(2)
-    lax.fori_loop(first, first + blocks // 2, place, 0)
+    to_owners = []
+    for i in range(CHUNKS):
+        for copy in to_columns[i]:
+            copy.wait_recv()
+        for k in range(i * per, i * per + per):
+            if k == 0:
+                by_owner[0] = by_column[:, 0]
+                continue
+            copy = pltpu.make_async_remote_copy(
+                src_ref=by_column.at[:, k], dst_ref=by_owner.at[k],
+                send_sem=b_send.at[k], recv_sem=b_recv.at[k], device_id=shards[k], device_id_type=MESH)
+            copy.start()
+            to_owners.append(copy)
+        if i == 0:
+            tiny.wait()
+            small_all[0, here[0]] = mine[...] + small_core[...]
+            tiny_copies = spread_small(0)
     for j in range(PIECES):
         reducer.add(1, j)
-    lax.fori_loop(first + blocks // 2, blocks, place, 0)
+    for axis in (1, 2):
+        for copy in tiny_copies:
+            copy.wait()
+        small_all[axis, here[axis]] = total_small(axis - 1)
+        tiny_copies = spread_small(axis)
+
+    entries = 2 * groups * padded
+    for k in range(0, owners, 2):
+        for copy in to_owners[max(k - 1, 0) : k + 1]:
+            copy.wait_recv()
+        senders = [lax.rem(store + owners - k - n, owners) for n in range(2)]
+        wanted = jnp.concatenate([lists[pl.ds(s, 1), :] for s in senders], 1)
+        arrived = by_owner[k : k + 2].reshape(entries, 128)
+
+        def place(i, carry, k=k, wanted=wanted, arrived=arrived):
+            block = (512, entries)
+            rows = pl.ds(pl.multiple_of(i * 512, 512), 512)
+            hit = jnp.broadcast_to(wanted, block) == lax.broadcasted_iota(jnp.int32, block, 0) + i * 512
+            total = jnp.dot(
+                jnp.where(hit, 1.0, 0.0).astype(jnp.bfloat16), arrived, preferred_element_type=jnp.float32
+            )
+            if k > 0:
+                total = total + placed[rows, :]
+            if k < owners - 2:
+                placed[rows, :] = total
+            else:
+                o_table[rows, :] = total.astype(jnp.bfloat16)
+            return carry
+
+        lax.fori_loop(0, o_table.shape[0] // 512, place, 0)
+
     for copy in tiny_copies:
         copy.wait()
     o_small[...] = total_small(2)
     for j in range(PIECES):
         o_qkv[:, j * 1024 : j * 1024 + 1024] = reducer.result(j)
     reducer.close()
-    for copy in to_columns + to_owners:
-        copy.wait_send()
-
-
-def finish(slot_grads, h1, dq, dk, dv, lists, small, rows):
+    for copies in to_columns + [to_owners]:
+        for copy in copies:
+            copy.wait_send()
+
+
+def finish(h1, dq, dk, dv, x, dy, gain, member_slot, lists, small, w_qkv, rows, cap):
     bf16, f32 = jnp.bfloat16, jnp.float32
-    groups, owners = slot_grads.shape[:2]
+    groups, owners, _ = lists.shape
+    tokens, width = x.shape
+    padded = -(-cap // 16) * 16
+    owner = lax.div(member_slot, cap)
+    turn = lax.rem(owner + owners - lax.axis_index("store"), owners)
+    members = (turn * padded + member_slot - owner * cap).reshape(1, tokens)
+    entries = lists[:, :, :padded].transpose(1, 0, 2).reshape(owners, groups * padded)
     vmem = pl.BlockSpec(memory_space=pltpu.VMEM)
     dma = pltpu.SemaphoreType.DMA
     return pl.pallas_call(
         finish_kernel,
         name="finish",
         out_shape=(
-            jax.ShapeDtypeStruct((8, 3072), bf16),
+            jax.ShapeDtypeStruct((8, 3 * width), bf16),
             jax.ShapeDtypeStruct(small.shape, f32),
             jax.ShapeDtypeStruct((rows, 128), bf16),
         ),
-        in_specs=[vmem] * 7,
+        in_specs=[vmem] * 10 + [pl.BlockSpec(memory_space=pl.ANY)],
         out_specs=[vmem] * 3,
         scratch_shapes=[
-            pltpu.VMEM(slot_grads.shape, bf16),
-            pltpu.VMEM((owners, groups) + slot_grads.shape[2:], bf16),
-            pltpu.VMEM((h1.shape[1], h1.shape[0]), bf16),
+            pltpu.VMEM(w_qkv.shape, bf16),
+            pltpu.VMEM((width, tokens), bf16),
             pltpu.VMEM((PIECES, 4, 2, 128, 1024), bf16),
+            pltpu.VMEM((4, tokens, 256), f32),
+            pltpu.VMEM((tokens, width), bf16),
+            pltpu.VMEM((tokens, width), bf16),
+            pltpu.VMEM((8, width), f32),
+            pltpu.VMEM((groups, owners, padded, 128), bf16),
+            pltpu.VMEM((groups, owners, padded, 128), bf16),
+            pltpu.VMEM((owners, groups, padded, 128), bf16),
+            pltpu.VMEM((rows, 128), f32),
+            pltpu.VMEM(small.shape, f32),
             pltpu.VMEM(small.shape, f32),
             pltpu.VMEM((3, 4) + small.shape, f32),
         ]
         + Reducer.scratch()
-        + [dma, dma, dma((3, 3)), dma((3, 3)), dma((groups,)), dma((groups,)), dma((owners,)), dma((owners,))],
+        + [dma, dma, dma, dma((3, 3)), dma((3, 3)), dma((CHUNKS, groups)), dma((CHUNKS, groups)), dma((owners,)), dma((owners,))],
         compiler_params=pltpu.CompilerParams(
-            collective_id=0, has_side_effects=True, vmem_limit_bytes=48 * 1024 * 1024
+            collective_id=0, has_side_effects=True, vmem_limit_bytes=54 * 1024 * 1024
         ),
-    )(slot_grads, h1, dq, dk, dv, lists, small)
+    )(h1, dq, dk, dv, x, dy, gain, members, entries, small, w_qkv)
 
 
 def body(
@@ -773,10 +836,10 @@
     ).astype(bf16)
 
     x, lists, bias = fetch(node_table, touched, member_slot, distances, bias_table)
-    x = x.astype(f32)
+    x_rows, x = x, x.astype(f32)
     dout = cotangent.reshape(tokens, width)
 
-    h1, x_hat, x_rstd = layer_normalize(x, gains[0])
+    h1, _, _ = layer_normalize(x, gains[0])
     h1 = h1.astype(bf16)
     qkv = dot(h1, w_qkv).astype(bf16)
     attended, probs = attention_forward(qkv, bias)
@@ -795,22 +858,12 @@
     dq, dk, dv, grad_bias, (sum_down, sum_up, sum_out) = attention_backward(
         qkv, dattn, probs, distances, (weight(act, dout), weight(h2, du), weight(attended, dyb))
     )
-    dh1 = (
-        back(dq, w_qkv[:, :width])
-        + back(dk, w_qkv[:, width : 2 * width])
-        + back(dv, w_qkv[:, 2 * width :])
+    small = jnp.concatenate(
+        [jnp.zeros((8, 128), f32), gain_two.reshape(8, 128), grad_bias.reshape(8, 128)]
     )
-    dx, gain_one = layer_normalize_backward(dh1, gains[0], x_hat, x_rstd)
-    dx = dy + dx
-
-    padded = -(-cap // 16) * 16
-    member = member_slot + (padded - cap) * lax.div(member_slot, cap)
-    slot_grads = slot_gradients(member, dx, owners * padded).reshape(-1, owners, padded, 128)
-    entries = lists[:, :, :padded].transpose(1, 0, 2).reshape(owners // 2, -1)
-    small = jnp.concatenate(
-        [gain_one.reshape(8, 128), gain_two.reshape(8, 128), grad_bias.reshape(8, 128)]
+    sum_qkv, small, grad_table = finish(
+        h1, dq, dk, dv, x_rows, dy, gains[:1], member_slot, lists, small, w_qkv, shard_rows, cap
     )
-    sum_qkv, small, grad_table = finish(slot_grads, h1, dq, dk, dv, entries, small, shard_rows)
     return (
         layer_out.reshape(egos, count, width),
         grad_table,

time: 226 us -> 224 us (level)
  matrix products: 34.9 us -> 24.6 us
  local copies, waits for them, and re-layouts: 13.1 us -> 19.6 us
  Pallas kernels: 172 us -> 175 us
    dot_general x6 -> x3, matrix products: 14.9 us -> 5 us  [body(): lax.dot_general(a, b, (((1,), (1,)), ((), ())), preferred_element_type=f32)]
    pallas_call x1, Pallas kernels: 69.3 us -> 77.2 us  [finish(): pl.pallas_call(finish_kernel, name='finish', out_shape=(jax.ShapeDtypeStr...]
    unnamed x49 -> x39, local copies, waits for them, and re-layouts: 10 us -> 14.3 us
    pallas_call x1, Pallas kernels: 48.2 us -> 45.3 us  [attention_backward(): pl.pallas_call(attend_back_kernel, name='attend_back', grid=(egos, groups...]
    pallas_call x1 -> x0, Pallas kernels: 2.53 us -> none  [slot_gradients(): pl.pallas_call(slot_kernel, name='slot_gradients', grid=(width // 256,),...]
where the time goes in v5:
time: 224 us; the launch traced here: 223 us
  Pallas kernels  175 us (78%)
  matrix products  24.6 us (11%)
  local copies, waits for them, and re-layouts  19.6 us (9%)
  other arithmetic  3.76 us (2%)
    pallas_call x1, Pallas kernels, finish(): pl.pallas_call(finish_kernel, name='finish', out_shape=(jax.ShapeDtypeStr...  77.2 us
    pallas_call x1, Pallas kernels, attention_backward(): pl.pallas_call(attend_back_kernel, name='attend_back', grid=(egos, groups...  45.3 us
    pallas_call x1, Pallas kernels, fetch(): pl.pallas_call(fetch_kernel, name='fetch', out_shape=(jax.ShapeDtypeStruc...  32.3 us
    pallas_call x1, Pallas kernels, attention_forward(): pl.pallas_call(attend_kernel, name='attend', grid=(egos, groups), out_sha...  19.7 us
    unnamed x39, local copies, waits for them, and re-layouts  14.3 us
    dot_general x4, matrix products, body(): dot = lambda a, b: jnp.dot(a, b, preferred_element_type=f32)  11.5 us
    dot_general x3, matrix products, body(): lax.dot_general(a, b, (((0,), (0,)), ((), ())), preferred_element_type=f32)  8.11 us
    dot_general x3, matrix products, body(): lax.dot_general(a, b, (((1,), (1,)), ((), ())), preferred_element_type=f32)  5 us

profile of v5, /device:TPU:1, one launch (start us, length us, event | category | flops | bytes accessed | tf_op | source)
XLA Modules:
  0.0 223.4 jit_solution(6574612418533832421)
XLA Ops:
  0.7 0.8 fusion.17
  4.6 2.2 copy-done.3
  6.8 1.0 copy-done.4
  7.8 32.3 %fetch.1 = (bf16[512,1024]{1,0:T(8,128)(2,1)S(1)}, s32[8,16,1,128]{3,2,1,0:T(1,128)S(1)}, f32[2,32,256,256]{3,2,1,0:T(8,128)}) custom-call(s32[16,1,128]{2,1,0:T(1,128)S(1)} %pad.8.touched, s32[512,1]{1,0:T(8,128)S(1)} %bitcast.41, bf16[2048,1024]{1,0:T(8,128)(2,1)S(1)} %copy-done.3, s32[2,256,256]{2,1,0:T(8,128)S(1)} %copy-done.4, f32[32,128]{1,0:T(8,128)S(1)} %pad.9.lookup), custom_call_target="tpu_custom_call" | custom-call | tf_op jit(solution)/shard_map/fetch/pallas_call | solution.py:317
  40.2 0.9 reshape.97.lists
  42.1 1.0 copy-done.10
  43.1 6.4 %convolution_convert_fusion.q_ref.k_ref.v_ref = bf16[512,3072]{1,0:T(8,128)(2,1)S(1)} fusion(bf16[512,1024]{1,0:T(8,128)(2,1)S(1)} %fusion.4.h1, bf16[1024,3072]{1,0:T(8,128)(2,1)} %w_hbm.1), kind=kOutput, calls=%fused_computation | convolution fusion | flops 3222798336 | bytes 10485760 | tf_op jit(solution)/shard_map/dot_general | solution.py:832
  49.5 19.7 %attend.1 = (bf16[512,1024]{1,0:T(8,128)(2,1)S(1)}, f32[2,32,256,256]{3,2,1,0:T(8,128)}) custom-call(bf16[512,3072]{1,0:T(8,128)(2,1)S(1)} %convolution_convert_fusion.q_ref.k_ref.v_ref, bf16[512,3072]{1,0:T(8,128)(2,1)S(1)} %convolution_convert_fusion.q_ref.k_ref.v_ref, bf16[512,3072]{1,0:T(8,128)(2,1)S(1)} %convolution_convert_fusion.q_ref.k_ref.v_ref, ...), custom_call_target="tpu_custom_call" | custom-call | tf_op jit(solution)/shard_map/attend/pallas_call | solution.py:532
  69.3 1.3 fusion.20
  71.0 1.5 multiply_convert_fusion
  72.9 2.0 fusion.10
  74.9 2.2 %add_convert_fusion = bf16[512,1024]{1,0:T(8,128)(2,1)} fusion(f32[512,1024]{1,0:T(8,128)S(1)} %get-tuple-element.46, bf16[512,1024]{1,0:T(8,128)(2,1)S(1)} %get-tuple-element.47, bf16[1024,1024]{1,0:T(8,128)(2,1)S(1)} %copy-done.13), kind=kOutput, calls=%fused_computation.19 | convolution fusion | flops 1074790400 | bytes 6291456 | tf_op jit(solution)/shard_map/dot_general | solution.py:832
  77.1 2.6 %convolution_convert_fusion.3 = bf16[1024,1024]{1,0:T(8,128)(2,1)} fusion(bf16[512,1024]{1,0:T(8,128)(2,1)S(1)} %get-tuple-element.47, bf16[512,1024]{1,0:T(8,128)(2,1)S(1)} %bitcast.47), kind=kOutput, calls=%fused_computation.27 | convolution fusion | flops 1074790400 | bytes 4194304 | tf_op jit(solution)/shard_map/dot_general | solution.py:834
  79.7 2.9 %convolution_convert_fusion.2 = bf16[1024,1024]{1,0:T(8,128)(2,1)} fusion(bf16[512,1024]{1,0:T(8,128)(2,1)S(1)} %fusion.10, f32[512,1024]{1,0:T(8,128)S(1)} %get-tuple-element.46, f32[1024]{0:T(1024)S(1)} %bitcast.51, f32[512]{0:T(512)S(1)} %add_rsqrt_fusion, f32[512]{0:T(512)S(1)} %broadcast_multiply_fusion.2), kind=kOutput, calls=%fused_computation.26 | convolution fusion | flops 1076887552 | bytes 5251072 | tf_op jit(solution)/shard_map/dot_general | solution.py:834
  82.6 1.7 multiply_reduce_fusion
  85.1 2.7 %convolution_convert_fusion.1 = bf16[1024,1024]{1,0:T(8,128)(2,1)} fusion(bf16[512,1024]{1,0:T(8,128)(2,1)S(1)} %get-tuple-element.25, f32[512,1024]{1,0:T(8,128)S(1)} %multiply_add_fusion.dy), kind=kOutput, calls=%fused_computation.25 | convolution fusion | flops 1075314688 | bytes 5242880 | tf_op jit(solution)/shard_map/dot_general | solution.py:834
  87.8 1.3 convolution_convert_fusion.4.dattn_ref
  89.1 45.3 %attend_back.1 = (bf16[512,1024]{1,0:T(8,128)(2,1)S(1)}, bf16[512,1024]{1,0:T(8,128)(2,1)S(1)}, bf16[512,1024]{1,0:T(8,128)(2,1)S(1)}, f32[2,32,256]{2,1,0:T(8,1...) custom-call(bf16[512,3072]{1,0:T(8,128)(2,1)} %copy-done.1, ...), custom_call_target="tpu_custom_call" | custom-call | tf_op jit(solution)/shard_map/attend_back/pallas_call | solution.py:553
  134.4 1.0 copy-done.6
  135.4 1.0 copy-done.7
  136.5 1.0 copy-done.8
  138.4 77.2 %finish.1 = (bf16[8,3072]{1,0:T(8,128)(2,1)}, f32[24,128]{1,0:T(8,128)}, bf16[2048,128]{1,0:T(8,128)(2,1)}) custom-call(bf16[512,1024]{1,0:T(8,128)(2,1)} %copy-done.10, bf16[512,1024]{1,0:T(8,128)(2,1)} %copy-done.6, bf16[512,1024]{1,0:T(8,128)(2,1)} %copy-done.7, bf16[512,1024]{1,0:T(8,128)(2,1)} %copy-done.8, bf16[512,1024]{1,0:T(8,128)(2,1)} %copy-done.2, ...), custom_call_target="tpu_custom_call" | custom-call | tf_op jit(solution)/shard_map/finish/pallas_call | solution.py:780
  218.3 1.9 copy.36
  220.1 1.4 copy.37
  (59 shorter events, 11.1 us)
Async XLA Ops:
  0.6 70.4 %copy-start = (bf16[1024,1024]{1,0:T(8,128)(2,1)S(1)}, bf16[1024,1024]{1,0:T(8,128)(2,1)}, u32[]{:S(2)}) copy-start(bf16[1024,1024]{1,0:T(8,128)(2,1)} %param.18) | copy-start | bytes 6291460
  3.6 38.1 %copy-start.12 = (f32[1,1024]{1,0:T(1,128)}, f32[1,1024]{1,0:T(1,128)S(1)}, u32[]{:S(2)}) copy-start(f32[1,1024]{1,0:T(1,128)S(1)} %get-tuple-element.42.gain) | copy-start | bytes 12292
  4.6 2.2 copy-start.3
  6.8 1.0 copy-start.4
  40.1 29.2 %copy-start.2 = (bf16[512,1024]{1,0:T(8,128)(2,1)}, bf16[512,1024]{1,0:T(8,128)(2,1)S(1)}, u32[]{:S(2)}) copy-start(bf16[512,1024]{1,0:T(8,128)(2,1)S(1)} %get-tuple-element.23.x) | copy-start | bytes 3145732
  42.1 1.0 copy-start.10
  49.5 19.8 %copy-start.1 = (bf16[512,3072]{1,0:T(8,128)(2,1)}, bf16[512,3072]{1,0:T(8,128)(2,1)S(1)}, u32[]{:S(2)}) copy-start(bf16[512,3072]{1,0:T(8,128)(2,1)S(1)} %convolution_convert_fusion.q_ref.k_ref.v_ref) | copy-start | bytes 9437188
  49.5 19.8 %copy-start.14 = (bf16[1024,1024]{1,0:T(8,128)(2,1)S(1)}, bf16[1024,1024]{1,0:T(8,128)(2,1)}, u32[]{:S(2)}) copy-start(bf16[1024,1024]{1,0:T(8,128)(2,1)} %param.17) | copy-start | bytes 6291460
  71.0 1.5 copy-start.11
  71.0 1.9 copy-start.13
  85.1 2.7 %copy-start.9 = (f32[512,1024]{1,0:T(8,128)}, f32[512,1024]{1,0:T(8,128)S(1)}, u32[]{:S(2)}) copy-start(f32[512,1024]{1,0:T(8,128)S(1)} %multiply_add_fusion.dy) | copy-start | bytes 6291460
  87.8 1.3 copy-start.5
  134.4 1.0 copy-start.6
  135.4 1.0 copy-start.7
  136.5 1.0 copy-start.8

commit v6 on v3

--- a/solution.py
+++ b/solution.py
@@ -203,7 +203,7 @@
             dma((3,)),
         ],
         compiler_params=pltpu.CompilerParams(
-            collective_id=1, has_side_effects=True, vmem_limit_bytes=48 * 1024 * 1024
+            collective_id=1, has_side_effects=True, vmem_limit_bytes=36 * 1024 * 1024
         ),
     )(listed, members, node_table, spd, lookup)
     return x, lists[:, :, 0, :cap].reshape(-1), bias
@@ -358,7 +358,7 @@
         ),
         in_specs=[column(0), column(1), column(2), probs],
         out_specs=(column(0), probs),
-        compiler_params=pltpu.CompilerParams(vmem_limit_bytes=40 * 1024 * 1024),
+        compiler_params=pltpu.CompilerParams(vmem_limit_bytes=16 * 1024 * 1024),
     )(qkv, qkv, qkv, bias)
 
 
@@ -379,7 +379,7 @@
             pltpu.VMEM((count * 32, count), jnp.bfloat16),
             pltpu.VMEM((groups * 8 * GROUP, 256), jnp.float32),
         ],
-        compiler_params=pltpu.CompilerParams(vmem_limit_bytes=48 * 1024 * 1024),
+        compiler_params=pltpu.CompilerParams(vmem_limit_bytes=26 * 1024 * 1024),
     )(qkv, qkv, qkv, dattn, probs, spd)
     return dq, dk, dv, bias.reshape(egos, heads, 8, 32).sum((0, 2)).T
 
@@ -408,7 +408,7 @@
         out_shape=jax.ShapeDtypeStruct((width // 128, slots, 128), jnp.bfloat16),
         in_specs=[pl.BlockSpec((1, tokens), lambda i: (0, 0)), pl.BlockSpec((tokens, 256), lambda i: (0, i))],
         out_specs=pl.BlockSpec((2, slots, 128), lambda i: (i, 0, 0)),
-        compiler_params=pltpu.CompilerParams(vmem_limit_bytes=40 * 1024 * 1024),
+        compiler_params=pltpu.CompilerParams(vmem_limit_bytes=12 * 1024 * 1024),
     )(member_slot.reshape(1, tokens), dx)
 
 
@@ -431,11 +431,11 @@
     return pl.pallas_call(
         place_kernel,
         name="place_gradients",
-        grid=(rows // 256,),
+        grid=(rows // 512,),
         out_shape=jax.ShapeDtypeStruct((rows, width), jnp.bfloat16),
         in_specs=[pl.BlockSpec((1, entries), lambda i: (0, 0)), pl.BlockSpec((entries, width), lambda i: (0, 0))],
-        out_specs=pl.BlockSpec((256, width), lambda i: (i, 0)),
-        compiler_params=pltpu.CompilerParams(vmem_limit_bytes=40 * 1024 * 1024),
+        out_specs=pl.BlockSpec((512, width), lambda i: (i, 0)),
+        compiler_params=pltpu.CompilerParams(vmem_limit_bytes=12 * 1024 * 1024),
     )(lists.reshape(1, entries), grads)
 
 
@@ -654,7 +654,7 @@
             dma((3, 3)),
         ],
         compiler_params=pltpu.CompilerParams(
-            collective_id=0, has_side_effects=True, vmem_limit_bytes=40 * 1024 * 1024
+            collective_id=0, has_side_effects=True, vmem_limit_bytes=30 * 1024 * 1024
         ),
     )(*[split(g) for g in gradients], small)
 

time: 214 us -> 218 us (1.019)
  local copies, waits for them, and re-layouts: 12.1 us -> 25.1 us
  Pallas kernels: 148 us -> 139 us
    unnamed x68 -> x78, local copies, waits for them, and re-layouts: 8.83 us -> 21.8 us
    pallas_call x1, Pallas kernels: 19.7 us -> 13.4 us  [attention_forward(): pl.pallas_call(attend_kernel, name='attend', grid=(egos, groups), out_sha...]
    pallas_call x1, Pallas kernels: 37.1 us -> 34.8 us  [attention_backward(): pl.pallas_call(attend_back_kernel, name='attend_back', grid=(egos, groups...]
where the time goes in v6:
time: 218 us; the launch traced here: 217 us
  Pallas kernels  139 us (64%)
  matrix products  38 us (17%)
  local copies, waits for them, and re-layouts  25.1 us (12%)
  starting transfers between devices  10.4 us (5%)
  other arithmetic  3.39 us (2%)
    pallas_call x1, Pallas kernels, reduce_gradients(): pl.pallas_call(reduce_kernel, name='reduce_gradients', out_shape=(jax.Sha...  47.4 us
    pallas_call x1, Pallas kernels, attention_backward(): pl.pallas_call(attend_back_kernel, name='attend_back', grid=(egos, groups...  34.8 us
    pallas_call x1, Pallas kernels, fetch(): pl.pallas_call(fetch_kernel, name='fetch', out_shape=(jax.ShapeDtypeStruc...  32.3 us
    unnamed x78, local copies, waits for them, and re-layouts  21.8 us
    dot_general x6, matrix products, body(): lax.dot_general(a, b, (((0,), (0,)), ((), ())), preferred_element_type=f32)  15.8 us
    pallas_call x1, Pallas kernels, attention_forward(): pl.pallas_call(attend_kernel, name='attend', grid=(egos, groups), out_sha...  13.4 us
    dot_general x4, matrix products, body(): dot = lambda a, b: jnp.dot(a, b, preferred_element_type=f32)  12.6 us
    all_to_all x1, starting transfers between devices, body(): lax.all_to_all(slot_grads.reshape(-1, cap, 128), both, split_axis=0, conc...  10.4 us
  transfers between devices with their start and end apart: 1, of which 0 were waited for; matrix products, arithmetic and copies ran while one was open for 10% of the time, Pallas kernels for 22%

profile of v6, /device:TPU:1, one launch (start us, length us, event | category | flops | bytes accessed | tf_op | source)
XLA Modules:
  0.0 217.3 jit_solution(17433190320120066037)
XLA Ops:
  4.6 2.2 %copy-done.4 = bf16[2048,1024]{1,0:T(8,128)(2,1)S(1)} copy-done((bf16[2048,1024]{1,0:T(8,128)(2,1)S(1)}, bf16[2048,1024]{1,0:T(8,128)(2,1)}, u32[]{:S(2)}) %copy-start.4) | copy-done | bytes 4194328
  7.9 32.3 %fetch.1 = (bf16[512,1024]{1,0:T(8,128)(2,1)S(1)}, s32[8,16,1,128]{3,2,1,0:T(1,128)S(1)}, f32[2,32,256,256]{3,2,1,0:T(8,128)}) custom-call(s32[16,1,128]{2,1,0:T(1,128)S(1)} %pad.8.touched, s32[512,1]{1,0:T(8,128)S(1)} %bitcast.56, bf16[2048,1024]{1,0:T(8,128)(2,1)S(1)} %copy-done.4, s32[2,256,256]{2,1,0:T(8,128)S(1)} %copy-done.8, f32[32,128]{1,0:T(8,128)S(1)} %pad.9.lookup), custom_call_target="tpu_custom_call" | custom-call | tf_op jit(solution)/shard_map/fetch/pallas_call | solution.py:178
  40.9 3.9 %convolution_convert_fusion.q_ref.k_ref.v_ref = bf16[512,3072]{1,0:T(8,128)(2,1)S(1)} fusion(bf16[1024,3072]{1,0:T(8,128)(2,1)S(1)} %copy-done.21, bf16[512,1024]{1,0:T(8,128)(2,1)S(1)} %get-tuple-element.22, f32[1024]{0:T(1024)S(1)} %bitcast.65, f32[512]{0:T(512)S(1)} %add_rsqrt_fusion.1, f32[512]{0:T(512)S(1)} %broadcast_multiply_fusion.5), kind=kOutput, calls=%fused_computation | convolution fusion | flops 3225419776 | bytes 10493952 | tf_op jit(solution)/shard_map/dot_general | solution.py:681
  44.8 5.8 %copy-done.3 = f32[2,32,256,256]{3,2,1,0:T(8,128)S(1)} copy-done((f32[2,32,256,256]{3,2,1,0:T(8,128)S(1)}, f32[2,32,256,256]{3,2,1,0:T(8,128)}, u32[]{:S(2)}) %copy-start.3) | copy-done | bytes 16777240
  50.6 13.4 %attend.1 = (bf16[512,1024]{1,0:T(8,128)(2,1)S(1)}, f32[2,32,256,256]{3,2,1,0:T(8,128)S(1)}) custom-call(bf16[512,3072]{1,0:T(8,128)(2,1)S(1)} %convolution_convert_fusion.q_ref.k_ref.v_ref, bf16[512,3072]{1,0:T(8,128)(2,1)S(1)} %convolution_convert_fusion.q_ref.k_ref.v_ref, bf16[512,3072]{1,0:T(8,128)(2,1)S(1)} %convolution_convert_fusion.q_ref.k_ref.v_ref, ...), custom_call_target="tpu_custom_call" | custom-call | tf_op jit(solution)/shard_map/attend/pallas_call | solution.py:351
  64.0 5.7 %copy-done.2 = f32[2,32,256,256]{3,2,1,0:T(8,128)} copy-done((f32[2,32,256,256]{3,2,1,0:T(8,128)}, f32[2,32,256,256]{3,2,1,0:T(8,128)S(1)}, u32[]{:S(2)}) %copy-start.2) | copy-done | bytes 16777240
  69.8 1.3 fusion.35
  71.5 2.7 %multiply_convert_fusion = (bf16[512,1024]{1,0:T(8,128)(2,1)}, f32[512,1024]{1,0:T(8,128)S(1)}) fusion(bf16[1024,1024]{1,0:T(8,128)(2,1)S(1)} %copy-done, f32[512,1024]{1,0:T(8,128)S(1)} %get-tuple-element.45, f32[1024]{0:T(1024)S(1)} %bitcast.61, f32[512]{0:T(512)S(1)} %add_rsqrt_fusion, f32[512]{0:T(512)S(1)} %broadcast_multiply_fusion.4), kind=kOutput, calls=%fused_computation.35 | convolution fusion | flops 1078460416 | bytes 7348224 | tf_op jit(solution)/shard_map/dot_general | solution.py:681
  74.2 2.1 fusion.18
  76.4 1.8 multiply_reduce_fusion
  81.9 34.8 %attend_back.1 = (bf16[512,1024]{1,0:T(8,128)(2,1)S(1)}, bf16[512,1024]{1,0:T(8,128)(2,1)S(1)}, bf16[512,1024]{1,0:T(8,128)(2,1)S(1)}, f32[2,32,256]{2,1,0:T(8,128)S(1)}) custom-call(bf16[512,3072]{1,0:T(8,128)(2,1)S(1)} %convolution_convert_fusion.q_ref.k_ref.v_ref, bf16[512,3072]{1,0:T(8,128)(2,1)S(1)} %convolution_convert_fusion.q_ref.k_ref.v_ref, ...), custom_call_target="tpu_custom_call" | custom-call | tf_op jit(solution)/shard_map/attend_back/pallas_call | solution.py:370
  116.8 1.3 fusion.23
  119.4 1.9 fusion.11
  122.0 3.2 %slot_gradients.1 = bf16[8,640,128]{2,1,0:T(8,128)(2,1)} custom-call(s32[1,512]{1,0:T(1,128)S(1)} %bitcast.57, f32[512,1024]{1,0:T(8,128)S(1)} %fusion.10.dx_ref), custom_call_target="tpu_custom_call" | custom-call | tf_op jit(solution)/shard_map/slot_gradients/pallas_call | solution.py:404
  125.2 10.4 %all-to-all-start = ((bf16[128,40,128]{2,1,0:T(8,128)(2,1)}), bf16[128,40,128]{2,1,0:T(8,128)(2,1)}, u32[]{:S(2)}, u32[]{:S(2)}) async-start(bf16[128,40,128]{2,1,0:T(8,128)(2,1)} %bitcast.6), calls=%async_computation | async-start | bytes 2621440 | tf_op jit(solution)/shard_map/all_to_all | solution.py:717
  135.6 2.7 %convolution_convert_fusion.3 = bf16[1024,1024]{1,0:T(8,128)(2,1)S(1)} fusion(bf16[512,1024]{1,0:T(8,128)(2,1)} %copy-done.15, bf16[512,1024]{1,0:T(8,128)(2,1)S(1)} %get-tuple-element.22, f32[1024]{0:T(1024)S(1)} %bitcast.68, f32[512]{0:T(512)S(1)} %add_rsqrt_fusion.1, f32[512]{0:T(512)S(1)} %broadcast_multiply_fusion.5), kind=kOutput, calls=%fused_computation.42 | convolution fusion | flops 1077411840 | bytes 4202496 | tf_op jit(solution)/shard_map/dot_general | solution.py:683
  138.4 2.8 %convolution_convert_fusion.2 = bf16[1024,1024]{1,0:T(8,128)(2,1)} fusion(bf16[512,1024]{1,0:T(8,128)(2,1)S(1)} %copy-done.14, bf16[512,1024]{1,0:T(8,128)(2,1)S(1)} %get-tuple-element.22, f32[1024]{0:T(1024)S(1)} %bitcast.69, f32[512]{0:T(512)S(1)} %add_rsqrt_fusion.1, f32[512]{0:T(512)S(1)} %broadcast_multiply_fusion.5), kind=kOutput, calls=%fused_computation.41 | convolution fusion | flops 1077411840 | bytes 4202496 | tf_op jit(solution)/shard_map/dot_general | solution.py:683
  141.2 2.8 %convolution_convert_fusion.1 = bf16[1024,1024]{1,0:T(8,128)(2,1)} fusion(bf16[512,1024]{1,0:T(8,128)(2,1)S(1)} %copy-done.12, bf16[512,1024]{1,0:T(8,128)(2,1)S(1)} %get-tuple-element.22, f32[1024]{0:T(1024)S(1)} %bitcast.70, f32[512]{0:T(512)S(1)} %add_rsqrt_fusion.1, f32[512]{0:T(512)S(1)} %broadcast_multiply_fusion.5), kind=kOutput, calls=%fused_computation.40 | convolution fusion | flops 1077411840 | bytes 4202496 | tf_op jit(solution)/shard_map/dot_general | solution.py:683
  144.0 2.6 %convolution_convert_fusion.6 = bf16[1024,1024]{1,0:T(8,128)(2,1)} fusion(bf16[512,1024]{1,0:T(8,128)(2,1)S(1)} %copy-done.27, bf16[512,1024]{1,0:T(8,128)(2,1)S(1)} %bitcast.59), kind=kOutput, calls=%fused_computation.45 | convolution fusion | flops 1074790400 | bytes 4194304 | tf_op jit(solution)/shard_map/dot_general | solution.py:683
  146.9 3.3 %convolution_convert_fusion.4 = bf16[1024,1024]{1,0:T(8,128)(2,1)S(1)} fusion(bf16[512,1024]{1,0:T(8,128)(2,1)} %copy-done.10, f32[512,1024]{1,0:T(8,128)} %copy-done.18), kind=kOutput, calls=%fused_computation.43 | convolution fusion | flops 1075314688 | bytes 5242880 | tf_op jit(solution)/shard_map/dot_general | solution.py:683
  150.3 1.5 convolution_convert_fusion.5
  153.2 47.4 %reduce_gradients.1 = (bf16[8,3072]{1,0:T(8,128)(2,1)S(1)}, bf16[8,1024]{1,0:T(8,128)(2,1)S(1)}, bf16[8,1024]{1,0:T(8,128)(2,1)S(1)}, bf16[8,1024]{1,0:T(8,128)(2,1)S(1)}, f32[24,128]{1,0:T(8,128)S(1)}) custom-call(bf16[4,2,128,1024]{3,2,1,0:T(8,128)(2,1)S(1)} %bitcast.53, bf16[4,2,128,1024]{3,2,1,0:T(8,128)(2,1)S(1)} %bitcast.55, ...), custom_call_target="tpu_custom_call" | custom-call | tf_op jit(solution)/shard_map/reduce_gradients/pallas_call | solution.py:623
  202.1 4.6 %add_convert_fusion = bf16[512,1024]{1,0:T(8,128)(2,1)} fusion(f32[512,1024]{1,0:T(8,128)} %copy-done.16, bf16[512,1024]{1,0:T(8,128)(2,1)S(1)} %copy-done.28, bf16[1024,1024]{1,0:T(8,128)(2,1)} %param.19), kind=kOutput, calls=%fused_computation.34 | convolution fusion | flops 1074790400 | bytes 6291456 | tf_op jit(solution)/shard_map/dot_general | solution.py:681
  206.7 8.1 %place_gradients.1 = bf16[2048,128]{1,0:T(8,128)(2,1)} custom-call(s32[1,5120]{1,0:T(1,128)S(1)} %reshape_reshape_squeeze.3.lists_ref, bf16[5120,128]{1,0:T(8,128)(2,1)} %bitcast.7.grads_ref), custom_call_target="tpu_custom_call" | custom-call | tf_op jit(solution)/shard_map/place_gradients/pallas_call | solution.py:431
  (109 shorter events, 17.4 us)
Async XLA Ops:
  0.6 70.9 %copy-start = (bf16[1024,1024]{1,0:T(8,128)(2,1)S(1)}, bf16[1024,1024]{1,0:T(8,128)(2,1)}, u32[]{:S(2)}) copy-start(bf16[1024,1024]{1,0:T(8,128)(2,1)} %param.18) | copy-start | bytes 6291460
  7.9 33.0 %copy-start.21 = (bf16[1024,3072]{1,0:T(8,128)(2,1)S(1)}, bf16[1024,3072]{1,0:T(8,128)(2,1)}, u32[]{:S(2)}) copy-start(bf16[1024,3072]{1,0:T(8,128)(2,1)} %param.16) | copy-start | bytes 18874372
  44.8 5.8 %copy-start.3 = (f32[2,32,256,256]{3,2,1,0:T(8,128)S(1)}, f32[2,32,256,256]{3,2,1,0:T(8,128)}, u32[]{:S(2)}) copy-start(f32[2,32,256,256]{3,2,1,0:T(8,128)} %get-tuple-element.23.bias_ref) | copy-start | bytes 50331652
  50.6 19.2 %copy-start.22 = (bf16[1024,1024]{1,0:T(8,128)(2,1)S(1)}, bf16[1024,1024]{1,0:T(8,128)(2,1)}, u32[]{:S(2)}) copy-start(bf16[1024,1024]{1,0:T(8,128)(2,1)} %param.17) | copy-start | bytes 6291460
  64.0 5.7 %copy-start.2 = (f32[2,32,256,256]{3,2,1,0:T(8,128)}, f32[2,32,256,256]{3,2,1,0:T(8,128)S(1)}, u32[]{:S(2)}) copy-start(f32[2,32,256,256]{3,2,1,0:T(8,128)S(1)} %get-tuple-element.26.probs_ref) | copy-start | bytes 50331652
  69.8 4.4 %copy-start.10 = (bf16[512,1024]{1,0:T(8,128)(2,1)}, bf16[512,1024]{1,0:T(8,128)(2,1)S(1)}, u32[]{:S(2)}) copy-start(bf16[512,1024]{1,0:T(8,128)(2,1)S(1)} %get-tuple-element.24) | copy-start | bytes 3145732
  71.1 7.1 %copy-start.16 = (f32[512,1024]{1,0:T(8,128)}, f32[512,1024]{1,0:T(8,128)S(1)}, u32[]{:S(2)}) copy-start(f32[512,1024]{1,0:T(8,128)S(1)} %get-tuple-element.45) | copy-start | bytes 6291460
  74.2 6.9 %slice-start = ((s8[16777216]{0:T(1024)(128)(4,1)}), s8[4194304]{0:T(1024)(128)(4,1)S(1)}, s32[]{:S(2)}) async-start(s8[16777216]{0:T(1024)(128)(4,1)} %bitcast.48), calls=%async_computation.1 | async-start | bytes 8388608
  74.2 6.9 %slice-start.1 = ((s8[16777216]{0:T(1024)(128)(4,1)}), s8[4194304]{0:T(1024)(128)(4,1)S(1)}, s32[]{:S(2)}) async-start(s8[16777216]{0:T(1024)(128)(4,1)} %bitcast.48), calls=%async_computation.2 | async-start | bytes 8388608
  76.4 4.8 %slice-start.2 = ((s8[16777216]{0:T(1024)(128)(4,1)}), s8[4194304]{0:T(1024)(128)(4,1)S(1)}, s32[]{:S(2)}) async-start(s8[16777216]{0:T(1024)(128)(4,1)} %bitcast.48), calls=%async_computation.3 | async-start | bytes 8388608
  78.2 3.6 %slice-start.3 = ((s8[16777216]{0:T(1024)(128)(4,1)}), s8[4194304]{0:T(1024)(128)(4,1)S(1)}, s32[]{:S(2)}) async-start(s8[16777216]{0:T(1024)(128)(4,1)} %bitcast.48), calls=%async_computation.4 | async-start | bytes 8388608
  79.8 41.4 %copy-start.18 = (f32[512,1024]{1,0:T(8,128)}, f32[512,1024]{1,0:T(8,128)S(1)}, u32[]{:S(2)}) copy-start(f32[512,1024]{1,0:T(8,128)S(1)} %multiply_add_fusion) | copy-start | bytes 6291460
  79.9 36.9 %slice-start.4 = ((s8[6291456]{0:T(1024)(128)(4,1)}), s8[4194304]{0:T(1024)(128)(4,1)S(1)}, s32[]{:S(2)}) async-start(s8[6291456]{0:T(1024)(128)(4,1)} %bitcast.76), calls=%async_computation.5 | async-start | bytes 8388608
  81.9 34.9 %slice-start.5 = ((s8[6291456]{0:T(1024)(128)(4,1)}), s8[2097152]{0:T(1024)(128)(4,1)S(1)}, s32[]{:S(2)}) async-start(s8[6291456]{0:T(1024)(128)(4,1)} %bitcast.76), calls=%async_computation.6 | async-start | bytes 4194304
  125.2 81.5 %all-to-all-start = ((bf16[128,40,128]{2,1,0:T(8,128)(2,1)}), bf16[128,40,128]{2,1,0:T(8,128)(2,1)}, u32[]{:S(2)}, u32[]{:S(2)}) async-start(bf16[128,40,128]{2,1,0:T(8,128)(2,1)} %bitcast.6), calls=%async_computation | async-start | bytes 2621440 | tf_op jit(solution)/shard_map/all_to_all | solution.py:717
  135.6 2.8 %copy-start.14 = (bf16[512,1024]{1,0:T(8,128)(2,1)S(1)}, bf16[512,1024]{1,0:T(8,128)(2,1)}, u32[]{:S(2)}) copy-start(bf16[512,1024]{1,0:T(8,128)(2,1)} %copy-done.13) | copy-start | bytes 3145732
  138.4 2.8 %copy-start.12 = (bf16[512,1024]{1,0:T(8,128)(2,1)S(1)}, bf16[512,1024]{1,0:T(8,128)(2,1)}, u32[]{:S(2)}) copy-start(bf16[512,1024]{1,0:T(8,128)(2,1)} %copy-done.11) | copy-start | bytes 3145732
  141.2 2.8 %copy-start.20 = (bf16[2,256,1024]{2,1,0:T(8,128)(2,1)S(1)}, bf16[2,256,1024]{2,1,0:T(8,128)(2,1)}, u32[]{:S(2)}) copy-start(bf16[2,256,1024]{2,1,0:T(8,128)(2,1)} %param.15) | copy-start | bytes 3145732
  141.2 2.8 %copy-start.27 = (bf16[512,1024]{1,0:T(8,128)(2,1)S(1)}, bf16[512,1024]{1,0:T(8,128)(2,1)}, u32[]{:S(2)}) copy-start(bf16[512,1024]{1,0:T(8,128)(2,1)} %get-tuple-element.46) | copy-start | bytes 3145732
  146.9 3.4 %copy-start.17 = (f32[512,1024]{1,0:T(8,128)S(1)}, f32[512,1024]{1,0:T(8,128)}, u32[]{:S(2)}) copy-start(f32[512,1024]{1,0:T(8,128)} %copy-done.16) | copy-start | bytes 6291460
  146.9 3.4 %copy-start.26 = (bf16[512,1024]{1,0:T(8,128)(2,1)S(1)}, bf16[512,1024]{1,0:T(8,128)(2,1)}, u32[]{:S(2)}) copy-start(bf16[512,1024]{1,0:T(8,128)(2,1)} %copy-done.25) | copy-start | bytes 3145732
  150.3 2.8 %copy-start.7 = (bf16[1024,1024]{1,0:T(8,128)(2,1)S(1)}, bf16[1024,1024]{1,0:T(8,128)(2,1)}, u32[]{:S(2)}) copy-start(bf16[1024,1024]{1,0:T(8,128)(2,1)} %convolution_convert_fusion.6) | copy-start | bytes 6291460
  153.2 49.0 %copy-start.28 = (bf16[512,1024]{1,0:T(8,128)(2,1)S(1)}, bf16[512,1024]{1,0:T(8,128)(2,1)}, u32[]{:S(2)}) copy-start(bf16[512,1024]{1,0:T(8,128)(2,1)} %get-tuple-element.46) | copy-start | bytes 3145732
  202.1 15.1 %copy-start.1 = (bf16[1024,1024]{1,0:T(8,128)(2,1)S(1)}, bf16[1024,1024]{1,0:T(8,128)(2,1)}, u32[]{:S(2)}) copy-start(bf16[1024,1024]{1,0:T(8,128)(2,1)} %param.18) | copy-start | bytes 6291460
  (12 other events, 24.6 us)

commit v7 on v6

--- a/solution.py
+++ b/solution.py
@@ -203,7 +203,7 @@
             dma((3,)),
         ],
         compiler_params=pltpu.CompilerParams(
-            collective_id=1, has_side_effects=True, vmem_limit_bytes=36 * 1024 * 1024
+            collective_id=1, has_side_effects=True, vmem_limit_bytes=48 * 1024 * 1024
         ),
     )(listed, members, node_table, spd, lookup)
     return x, lists[:, :, 0, :cap].reshape(-1), bias
@@ -358,7 +358,7 @@
         ),
         in_specs=[column(0), column(1), column(2), probs],
         out_specs=(column(0), probs),
-        compiler_params=pltpu.CompilerParams(vmem_limit_bytes=16 * 1024 * 1024),
+        compiler_params=pltpu.CompilerParams(vmem_limit_bytes=40 * 1024 * 1024),
     )(qkv, qkv, qkv, bias)
 
 
@@ -379,7 +379,7 @@
             pltpu.VMEM((count * 32, count), jnp.bfloat16),
             pltpu.VMEM((groups * 8 * GROUP, 256), jnp.float32),
         ],
-        compiler_params=pltpu.CompilerParams(vmem_limit_bytes=26 * 1024 * 1024),
+        compiler_params=pltpu.CompilerParams(vmem_limit_bytes=48 * 1024 * 1024),
     )(qkv, qkv, qkv, dattn, probs, spd)
     return dq, dk, dv, bias.reshape(egos, heads, 8, 32).sum((0, 2)).T
 
@@ -654,7 +654,7 @@
             dma((3, 3)),
         ],
         compiler_params=pltpu.CompilerParams(
-            collective_id=0, has_side_effects=True, vmem_limit_bytes=30 * 1024 * 1024
+            collective_id=0, has_side_effects=True, vmem_limit_bytes=40 * 1024 * 1024
         ),
     )(*[split(g) for g in gradients], small)
 
@@ -704,6 +704,7 @@
     dy = dout.astype(f32) + dy
     dyb = dy.astype(bf16)
     dattn = back(dyb, w_out).astype(bf16)
+    layer_out, dattn = lax.optimization_barrier((layer_out, dattn))
     dq, dk, dv, grad_bias = attention_backward(qkv, dattn, probs, distances)
     dh1 = (
         back(dq, w_qkv[:, :width])

time: 218 us -> 211 us (0.968)
  local copies, waits for them, and re-layouts: 25.1 us -> 14.4 us
  Pallas kernels: 139 us -> 147 us
  matrix products: 38 us -> 33.7 us
    unnamed x78 -> x64, local copies, waits for them, and re-layouts: 21.8 us -> 11.1 us
    pallas_call x1, Pallas kernels: 13.4 us -> 19.7 us  [attention_forward(): pl.pallas_call(attend_kernel, name='attend', grid=(egos, groups), out_sha...]
    dot_general x4, matrix products: 12.6 us -> 8.95 us  [body(): dot = lambda a, b: jnp.dot(a, b, preferred_element_type=f32)]
  transfers between devices with their start and end apart: 1 -> 1, of which waited for: 0 -> 0; matrix products, arithmetic and copies ran while one was open for 10% -> 7% of each run, Pallas kernels for 22% -> 23%
where the time goes in v7:
time: 211 us; the launch traced here: 210 us
  Pallas kernels  147 us (70%)
  matrix products  33.7 us (16%)
  local copies, waits for them, and re-layouts  14.4 us (7%)
  starting transfers between devices  10.3 us (5%)
  other arithmetic  3.37 us (2%)
    pallas_call x1, Pallas kernels, reduce_gradients(): pl.pallas_call(reduce_kernel, name='reduce_gradients', out_shape=(jax.Sha...  47.3 us
    pallas_call x1, Pallas kernels, attention_backward(): pl.pallas_call(attend_back_kernel, name='attend_back', grid=(egos, groups...  36.6 us
    pallas_call x1, Pallas kernels, fetch(): pl.pallas_call(fetch_kernel, name='fetch', out_shape=(jax.ShapeDtypeStruc...  32.3 us
    pallas_call x1, Pallas kernels, attention_forward(): pl.pallas_call(attend_kernel, name='attend', grid=(egos, groups), out_sha...  19.7 us
    dot_general x6, matrix products, body(): lax.dot_general(a, b, (((0,), (0,)), ((), ())), preferred_element_type=f32)  13.8 us
    unnamed x64, local copies, waits for them, and re-layouts  11.1 us
    dot_general x6, matrix products, body(): lax.dot_general(a, b, (((1,), (1,)), ((), ())), preferred_element_type=f32)  11 us
    all_to_all x1, starting transfers between devices, body(): lax.all_to_all(slot_grads.reshape(-1, cap, 128), both, split_axis=0, conc...  10.3 us
  transfers between devices with their start and end apart: 1, of which 0 were waited for; matrix products, arithmetic and copies ran while one was open for 7% of the time, Pallas kernels for 23%

profile of v7, /device:TPU:1, one launch (start us, length us, event | category | flops | bytes accessed | tf_op | source)
XLA Modules:
  0.0 210.0 jit_solution(15419118100307420603)
XLA Ops:
  4.6 2.2 %copy-done.3 = bf16[2048,1024]{1,0:T(8,128)(2,1)S(1)} copy-done((bf16[2048,1024]{1,0:T(8,128)(2,1)S(1)}, bf16[2048,1024]{1,0:T(8,128)(2,1)}, u32[]{:S(2)}) %copy-start.3) | copy-done | bytes 4194328
  7.9 32.3 %fetch.1 = (bf16[512,1024]{1,0:T(8,128)(2,1)S(1)}, s32[8,16,1,128]{3,2,1,0:T(1,128)S(1)}, f32[2,32,256,256]{3,2,1,0:T(8,128)}) custom-call(s32[16,1,128]{2,1,0:T(1,128)S(1)} %pad.8.touched, s32[512,1]{1,0:T(8,128)S(1)} %bitcast.54, bf16[2048,1024]{1,0:T(8,128)(2,1)S(1)} %copy-done.3, s32[2,256,256]{2,1,0:T(8,128)S(1)} %copy-done.7, f32[32,128]{1,0:T(8,128)S(1)} %pad.9.lookup), custom_call_target="tpu_custom_call" | custom-call | tf_op jit(solution)/shard_map/fetch/pallas_call | solution.py:178
  40.9 3.9 %convolution_convert_fusion.q_ref.k_ref.v_ref = bf16[512,3072]{1,0:T(8,128)(2,1)S(1)} fusion(bf16[1024,3072]{1,0:T(8,128)(2,1)S(1)} %copy-done.20, bf16[512,1024]{1,0:T(8,128)(2,1)S(1)} %get-tuple-element.24, f32[1024]{0:T(1024)S(1)} %bitcast.63, f32[512]{0:T(512)S(1)} %add_rsqrt_fusion.1, f32[512]{0:T(512)S(1)} %broadcast_multiply_fusion.5), kind=kOutput, calls=%fused_computation | convolution fusion | flops 3225419776 | bytes 10493952 | tf_op jit(solution)/shard_map/dot_general | solution.py:681
  44.8 19.7 %attend.1 = (bf16[512,1024]{1,0:T(8,128)(2,1)S(1)}, f32[2,32,256,256]{3,2,1,0:T(8,128)}) custom-call(bf16[512,3072]{1,0:T(8,128)(2,1)S(1)} %convolution_convert_fusion.q_ref.k_ref.v_ref, bf16[512,3072]{1,0:T(8,128)(2,1)S(1)} %convolution_convert_fusion.q_ref.k_ref.v_ref, bf16[512,3072]{1,0:T(8,128)(2,1)S(1)} %convolution_convert_fusion.q_ref.k_ref.v_ref, ...), custom_call_target="tpu_custom_call" | custom-call | tf_op jit(solution)/shard_map/attend/pallas_call | solution.py:351
  64.6 1.3 fusion.35
  66.3 1.4 multiply_convert_fusion
  68.3 2.2 %add_convert_fusion = bf16[512,1024]{1,0:T(8,128)(2,1)} fusion(f32[512,1024]{1,0:T(8,128)S(1)} %get-tuple-element.49, bf16[512,1024]{1,0:T(8,128)(2,1)S(1)} %get-tuple-element.50, bf16[1024,1024]{1,0:T(8,128)(2,1)S(1)} %copy-done.21), kind=kOutput, calls=%fused_computation.34 | convolution fusion | flops 1074790400 | bytes 6291456 | tf_op jit(solution)/shard_map/dot_general | solution.py:681
  70.5 1.9 fusion.18
  72.5 1.7 multiply_reduce_fusion
  75.8 1.3 convolution_convert_fusion.7.dattn_ref
  77.2 36.6 %attend_back.1 = (bf16[512,1024]{1,0:T(8,128)(2,1)S(1)}, bf16[512,1024]{1,0:T(8,128)(2,1)S(1)}, bf16[512,1024]{1,0:T(8,128)(2,1)S(1)}, f32[2,32,256]{2,1,0:T(8,128)S(1)}) custom-call(bf16[512,3072]{1,0:T(8,128)(2,1)} %copy-done.2, bf16[512,3072]{1,0:T(8,128)(2,1)} %copy-done.2, bf16[512,3072]{1,0:T(8,128)(2,1)} %copy-done.2, ...), custom_call_target="tpu_custom_call" | custom-call | tf_op jit(solution)/shard_map/attend_back/pallas_call | solution.py:370
  113.8 1.3 fusion.23
  115.1 1.3 fusion.21
  116.4 3.5 %fusion.11 = (f32[1024]{0:T(1024)S(1)}, f32[512]{0:T(512)S(1)}, f32[512]{0:T(512)S(1)}, f32[512,1024]{1,0:T(8,128)S(1)}) fusion(bf16[512,1024]{1,0:T(8,128)(2,1)S(1)} %get-tuple-element.24, f32[512]{0:T(512)S(1)} %add_rsqrt_fusion.1, f32[512]{0:T(512)S(1)} %broadcast_multiply_fusion.5, f32[1024]{0:T(1024)S(1)} %bitcast.64, ...), kind=kOutput, calls=%fused_computation.16 | convolution fusion | flops 1079506944 | bytes 10502144 | tf_op jit(solution)/shard_map/dot_general | solution.py:682
  120.6 3.2 %slot_gradients.1 = bf16[8,640,128]{2,1,0:T(8,128)(2,1)} custom-call(s32[1,512]{1,0:T(1,128)S(1)} %bitcast.55, f32[512,1024]{1,0:T(8,128)S(1)} %fusion.10.dx_ref), custom_call_target="tpu_custom_call" | custom-call | tf_op jit(solution)/shard_map/slot_gradients/pallas_call | solution.py:404
  123.8 10.3 %all-to-all-start = ((bf16[128,40,128]{2,1,0:T(8,128)(2,1)}), bf16[128,40,128]{2,1,0:T(8,128)(2,1)}, u32[]{:S(2)}, u32[]{:S(2)}) async-start(bf16[128,40,128]{2,1,0:T(8,128)(2,1)} %bitcast.6), calls=%async_computation | async-start | bytes 2621440 | tf_op jit(solution)/shard_map/all_to_all | solution.py:718
  134.1 4.1 %convolution_convert_fusion.3 = bf16[1024,1024]{1,0:T(8,128)(2,1)} fusion(bf16[512,1024]{1,0:T(8,128)(2,1)} %copy-done.13, bf16[512,1024]{1,0:T(8,128)(2,1)S(1)} %get-tuple-element.24, f32[1024]{0:T(1024)S(1)} %bitcast.66, f32[512]{0:T(512)S(1)} %add_rsqrt_fusion.1, f32[512]{0:T(512)S(1)} %broadcast_multiply_fusion.5), kind=kOutput, calls=%fused_computation.42 | convolution fusion | flops 1077411840 | bytes 4202496 | tf_op jit(solution)/shard_map/dot_general | solution.py:683
  138.2 2.8 %convolution_convert_fusion.2 = bf16[1024,1024]{1,0:T(8,128)(2,1)} fusion(bf16[512,1024]{1,0:T(8,128)(2,1)S(1)} %copy-done.12, bf16[512,1024]{1,0:T(8,128)(2,1)S(1)} %get-tuple-element.24, f32[1024]{0:T(1024)S(1)} %bitcast.67, f32[512]{0:T(512)S(1)} %add_rsqrt_fusion.1, f32[512]{0:T(512)S(1)} %broadcast_multiply_fusion.5), kind=kOutput, calls=%fused_computation.41 | convolution fusion | flops 1077411840 | bytes 4202496 | tf_op jit(solution)/shard_map/dot_general | solution.py:683
  141.0 2.6 %convolution_convert_fusion.6 = bf16[1024,1024]{1,0:T(8,128)(2,1)} fusion(bf16[512,1024]{1,0:T(8,128)(2,1)S(1)} %copy-done.27, bf16[512,1024]{1,0:T(8,128)(2,1)S(1)} %bitcast.57), kind=kOutput, calls=%fused_computation.45 | convolution fusion | flops 1074790400 | bytes 4194304 | tf_op jit(solution)/shard_map/dot_general | solution.py:683
  143.9 1.5 convolution_convert_fusion.1
  145.9 1.3 convolution_convert_fusion.4
  147.7 1.5 convolution_convert_fusion.5
  150.6 47.3 %reduce_gradients.1 = (bf16[8,3072]{1,0:T(8,128)(2,1)S(1)}, bf16[8,1024]{1,0:T(8,128)(2,1)S(1)}, bf16[8,1024]{1,0:T(8,128)(2,1)S(1)}, bf16[8,1024]{1,0:T(8,128)(2,1)S(1)}, f32[24,128]{1,0:T(8,128)S(1)}) custom-call(bf16[4,2,128,1024]{3,2,1,0:T(8,128)(2,1)S(1)} %bitcast.50, bf16[4,2,128,1024]{3,2,1,0:T(8,128)(2,1)S(1)} %bitcast.53, ...), custom_call_target="tpu_custom_call" | custom-call | tf_op jit(solution)/shard_map/reduce_gradients/pallas_call | solution.py:623
  199.5 8.1 %place_gradients.1 = bf16[2048,128]{1,0:T(8,128)(2,1)} custom-call(s32[1,5120]{1,0:T(1,128)S(1)} %reshape_reshape_squeeze.3.lists_ref, bf16[5120,128]{1,0:T(8,128)(2,1)} %bitcast.7.grads_ref), custom_call_target="tpu_custom_call" | custom-call | tf_op jit(solution)/shard_map/place_gradients/pallas_call | solution.py:431
  (93 shorter events, 15.6 us)
Async XLA Ops:
  0.6 65.7 %copy-start = (bf16[1024,1024]{1,0:T(8,128)(2,1)S(1)}, bf16[1024,1024]{1,0:T(8,128)(2,1)}, u32[]{:S(2)}) copy-start(bf16[1024,1024]{1,0:T(8,128)(2,1)} %param.18) | copy-start | bytes 6291460
  4.6 2.2 %copy-start.3 = (bf16[2048,1024]{1,0:T(8,128)(2,1)S(1)}, bf16[2048,1024]{1,0:T(8,128)(2,1)}, u32[]{:S(2)}) copy-start(bf16[2048,1024]{1,0:T(8,128)(2,1)} %table_hbm.1) | copy-start | bytes 12582916
  7.9 33.0 %copy-start.20 = (bf16[1024,3072]{1,0:T(8,128)(2,1)S(1)}, bf16[1024,3072]{1,0:T(8,128)(2,1)}, u32[]{:S(2)}) copy-start(bf16[1024,3072]{1,0:T(8,128)(2,1)} %param.16) | copy-start | bytes 18874372
  44.8 19.8 %copy-start.2 = (bf16[512,3072]{1,0:T(8,128)(2,1)}, bf16[512,3072]{1,0:T(8,128)(2,1)S(1)}, u32[]{:S(2)}) copy-start(bf16[512,3072]{1,0:T(8,128)(2,1)S(1)} %convolution_convert_fusion.q_ref.k_ref.v_ref) | copy-start | bytes 9437188
  44.8 19.8 %copy-start.22 = (bf16[1024,1024]{1,0:T(8,128)(2,1)S(1)}, bf16[1024,1024]{1,0:T(8,128)(2,1)}, u32[]{:S(2)}) copy-start(bf16[1024,1024]{1,0:T(8,128)(2,1)} %param.17) | copy-start | bytes 6291460
  65.9 8.3 %copy-start.14 = (f32[512,1024]{1,0:T(8,128)}, f32[512,1024]{1,0:T(8,128)S(1)}, u32[]{:S(2)}) copy-start(f32[512,1024]{1,0:T(8,128)S(1)} %get-tuple-element.49) | copy-start | bytes 6291460
  66.3 2.0 copy-start.21
  67.8 2.7 %copy-start.26 = (bf16[512,1024]{1,0:T(8,128)(2,1)}, bf16[512,1024]{1,0:T(8,128)(2,1)S(1)}, u32[]{:S(2)}) copy-start(bf16[512,1024]{1,0:T(8,128)(2,1)S(1)} %get-tuple-element.50) | copy-start | bytes 3145732
  68.3 2.2 %copy-start.18 = (bf16[2,256,1024]{2,1,0:T(8,128)(2,1)S(1)}, bf16[2,256,1024]{2,1,0:T(8,128)(2,1)}, u32[]{:S(2)}) copy-start(bf16[2,256,1024]{2,1,0:T(8,128)(2,1)} %param.15) | copy-start | bytes 3145732
  72.5 1.7 copy-start.24
  74.2 1.6 copy-start.23
  75.8 44.1 %copy-start.16 = (f32[512,1024]{1,0:T(8,128)}, f32[512,1024]{1,0:T(8,128)S(1)}, u32[]{:S(2)}) copy-start(f32[512,1024]{1,0:T(8,128)S(1)} %multiply_add_fusion) | copy-start | bytes 6291460
  123.8 75.7 %all-to-all-start = ((bf16[128,40,128]{2,1,0:T(8,128)(2,1)}), bf16[128,40,128]{2,1,0:T(8,128)(2,1)}, u32[]{:S(2)}, u32[]{:S(2)}) async-start(bf16[128,40,128]{2,1,0:T(8,128)(2,1)} %bitcast.6), calls=%async_computation | async-start | bytes 2621440 | tf_op jit(solution)/shard_map/all_to_all | solution.py:718
  134.1 4.1 %copy-start.12 = (bf16[512,1024]{1,0:T(8,128)(2,1)S(1)}, bf16[512,1024]{1,0:T(8,128)(2,1)}, u32[]{:S(2)}) copy-start(bf16[512,1024]{1,0:T(8,128)(2,1)} %copy-done.11) | copy-start | bytes 3145732
  138.2 2.8 %copy-start.19 = (bf16[2,256,1024]{2,1,0:T(8,128)(2,1)S(1)}, bf16[2,256,1024]{2,1,0:T(8,128)(2,1)}, u32[]{:S(2)}) copy-start(bf16[2,256,1024]{2,1,0:T(8,128)(2,1)} %param.15) | copy-start | bytes 3145732
  138.2 2.8 %copy-start.27 = (bf16[512,1024]{1,0:T(8,128)(2,1)S(1)}, bf16[512,1024]{1,0:T(8,128)(2,1)}, u32[]{:S(2)}) copy-start(bf16[512,1024]{1,0:T(8,128)(2,1)} %copy-done.26) | copy-start | bytes 3145732
  143.9 1.5 copy-start.10
  143.9 1.9 copy-start.17
  145.9 1.6 copy-start.15
  145.9 1.9 copy-start.25
  147.7 1.6 copy-start.4
  147.7 2.2 %copy-start.5 = (bf16[1024,1024]{1,0:T(8,128)(2,1)S(1)}, bf16[1024,1024]{1,0:T(8,128)(2,1)}, u32[]{:S(2)}) copy-start(bf16[1024,1024]{1,0:T(8,128)(2,1)} %convolution_convert_fusion.2) | copy-start | bytes 6291460
  147.7 2.9 %copy-start.6 = (bf16[1024,1024]{1,0:T(8,128)(2,1)S(1)}, bf16[1024,1024]{1,0:T(8,128)(2,1)}, u32[]{:S(2)}) copy-start(bf16[1024,1024]{1,0:T(8,128)(2,1)} %convolution_convert_fusion.6) | copy-start | bytes 6291460
  150.6 59.4 %copy-start.1 = (bf16[1024,1024]{1,0:T(8,128)(2,1)S(1)}, bf16[1024,1024]{1,0:T(8,128)(2,1)}, u32[]{:S(2)}) copy-start(bf16[1024,1024]{1,0:T(8,128)(2,1)} %param.18) | copy-start | bytes 6291460
  (5 other events, 6.4 us)
